TPU v7x, 32 devices: a whole 2x2x4 slice. The times are simulated.
32 devices in a mesh: grp: 2 (over x), col: 8 (over z, y), row: 2 (over core).
Axes of the slice: x: 2, y: 2, z: 4, core: 2. Of those that a mesh axis runs over, the one named last changes fastest.
Arguments:
- cost: float32 [32, 8, 4096], P('grp', 'col', 'row'), parts along dimension 0, may hold values from -6 to 6
- rhs: float32 [32, 2, 16384], P('grp', 'row', 'col'), parts along dimension 0, may hold values from -6 to 6
- primal: float32 [32, 8, 4096], P('grp', 'col', 'row'), parts along dimension 0, may hold values from 0 to 1
- dual: float32 [32, 2, 16384], P('grp', 'row', 'col'), parts along dimension 0, may hold values from 0 to 1
- bound_kind: int32 [16, 4096], P(('grp', 'col'), 'row'), parts along dimension 0, may hold values from 0 to 2
- upper: float32 [16, 4096], P(('grp', 'col'), 'row'), parts along dimension 0, may hold values from 0.3 to 3
- kblocks: bfloat16 [16, 2, 256, 128, 128], P(('grp', 'col'), 'row'), parts along dimension 0, may hold values from -0.125 to 0.125
- block_row: int32 [16, 2, 256], P(('grp', 'col'), 'row'), parts along dimension 0, may hold values from 0 to 127
- block_col: int32 [16, 2, 256], P(('grp', 'col'), 'row'), parts along dimension 0, may hold values from 0 to 31
- block_count: int32 [16, 2], P(('grp', 'col'), 'row'), parts along dimension 0, may hold values from 32 to 256, as said below
Outputs:
- primal_out: float32 [32, 8, 4096], P('grp', 'col', 'row'), parts along dimension 0
- dual_out: float32 [32, 2, 16384], P('grp', 'row', 'col'), parts along dimension 0
There are 2 independent parts, one for each index of `grp`. A program takes and returns all parts, laid end to end along the dimension named above; each array names one. Nothing has to cross between parts.
Inputs may be any that keep to these rules, and one draw needn't show every extreme that they name: `block_count`: equals 256 for at least one tile of every part. `block_row`: live slots of one tile may name the same block position.
All inputs are finite; a program needn't handle non-finite values.
Results may differ from a plain program's by a relative error of at most 0.003.
Values may be sent and summed in bfloat16 or wider, within the bound.
No kernel may reach another device: no remote copies, remote signals or barrier semaphores. Data moves between devices by JAX's collectives and lax.ppermute only.
A program may use at most 64 MiB of HBM per device.

v0:
```python
import jax
import jax.numpy as jnp
from jax import lax
from jax.sharding import PartitionSpec as P

BS = 128
ITERS = 6


def forward_tile(kb, brow, bcol, live, xs, segments):
    picked = jnp.take(xs.reshape(xs.shape[0], -1, BS), bcol, axis=1)
    prod = jnp.einsum("nij,snj->nsi", kb, picked, preferred_element_type=jnp.float32)
    prod = prod * live[:, None, None]
    summed = jax.ops.segment_sum(prod, brow, num_segments=segments)
    return jnp.transpose(summed, (1, 0, 2)).reshape(xs.shape[0], segments * BS)


def backward_tile(kb, brow, bcol, live, ys, segments):
    picked = jnp.take(ys.reshape(ys.shape[0], -1, BS), brow, axis=1)
    prod = jnp.einsum("nij,sni->nsj", kb, picked, preferred_element_type=jnp.float32)
    prod = prod * live[:, None, None]
    summed = jax.ops.segment_sum(prod, bcol, num_segments=segments)
    return jnp.transpose(summed, (1, 0, 2)).reshape(ys.shape[0], segments * BS)


def project(value, kind, upper):
    lifted = jnp.where(kind == 2, value, jnp.maximum(value, 0.0))
    return jnp.where(kind == 1, jnp.minimum(lifted, upper), lifted)


def per_device(
    cost, rhs, primal, dual, bound_kind, upper, kblocks, block_row, block_col, block_count
):
    tile = kblocks[0, 0]
    brow = block_row[0, 0]
    bcol = block_col[0, 0]
    slots = jnp.arange(tile.shape[0], dtype=jnp.int32)
    live = (slots < block_count[0, 0]).astype(jnp.float32)
    own_cols = primal.shape[2]
    own_rows = dual.shape[2]
    col_slab = own_cols * lax.axis_size("row")
    row_slab = own_rows * lax.axis_size("col")
    col_segments = col_slab // BS
    row_segments = row_slab // BS
    x_state = primal[:, 0]
    cost_here = cost[:, 0]
    y_state = dual[:, 0]
    rhs_here = rhs[:, 0]
    for step in range(ITERS):
        y_slab = lax.all_gather(y_state.astype(jnp.bfloat16), "col", axis=1, tiled=True)
        partial_grad = backward_tile(tile, brow, bcol, live, y_slab, col_segments)
        grad = lax.psum_scatter(partial_grad, "row", scatter_dimension=1, tiled=True)
        x_next = project(x_state - 0.4 * (cost_here - grad), bound_kind, upper)
        x_bar = (2.0 * x_next - x_state).astype(jnp.bfloat16)
        x_slab = lax.all_gather(x_bar, "row", axis=1, tiled=True)
        partial_image = forward_tile(tile, brow, bcol, live, x_slab, row_segments)
        image = lax.psum_scatter(partial_image, "col", scatter_dimension=1, tiled=True)
        y_state = jnp.maximum(0.0, y_state + 0.9 * (rhs_here - image))
        x_state = x_next
    return (x_state[:, None, :], y_state[:, None, :])


def solution(mesh):
    return jax.shard_map(
        per_device,
        mesh=mesh,
        in_specs=(
            P("grp", "col", "row"),
            P("grp", "row", "col"),
            P("grp", "col", "row"),
            P("grp", "row", "col"),
            P(("grp", "col"), "row"),
            P(("grp", "col"), "row"),
            P(("grp", "col"), "row", None, None, None),
            P(("grp", "col"), "row", None),
            P(("grp", "col"), "row", None),
            P(("grp", "col"), "row"),
        ),
        out_specs=(P("grp", "col", "row"), P("grp", "row", "col")),
        check_vma=False,
    )
```

profile of v0, /device:TPU:10, one launch (start us, length us, event | category | flops | bytes accessed | tf_op | source)
XLA Modules:
  0.0 871.7 jit_solution(3900271771996375199)
XLA Ops:
  10.2 28.7 %all_gather.36 = bf16[16,16384]{1,0:T(8,128)(2,1)S(1)} all-gather(bf16[16,2048]{1,0:T(8,128)(2,1)S(1)} %bitcast.358), channel_id=1, replica_groups=mesh['grp'=2,'col'=8,'row'=2] {'col'}, dimensions={1}, use_global_device_ids=true | all-gather | bytes 589824 | tf_op jit(solution)/shard_map/all_gather | solution.py:50
  39.9 5.2 fusion.24
  45.2 9.0 %scatter_fusion = f32[32,16,128]{2,1,0:T(8,128)S(1)} fusion(f32[32,16,128]{2,1,0:T(8,128)S(1)} %broadcast.36.clone, s32[256]{0:T(256)S(1)} %bitcast.371, f32[256,16,128]{2,1,0:T(8,128)S(1)} %fusion.24), kind=kCustom, calls=%fused_computation.12 | custom fusion | flops 524288 | bytes 6292480 | tf_op jit(solution)/shard_map/scatter-add | solution.py:22
  55.2 11.7 %reduce-scatter.13.cloned.1.call-done = f32[16,2048]{1,0:T(8,128)} async-done(((f32[16,4096]{1,0:T(8,128)}), f32[16,2048]{1,0:T(8,128)}) %reduce-scatter.13.cloned.1.call-update) | async-done | bytes 131088 | tf_op jit(solution)/shard_map/reduce_scatter | solution.py:52
  66.9 1.7 fusion.139
  68.5 1.9 all_gather.37
  71.3 7.3 fusion.27
  78.7 8.9 %scatter_fusion.1 = f32[128,16,128]{2,1,0:T(8,128)S(1)} fusion(f32[128,16,128]{2,1,0:T(8,128)S(1)} %broadcast.39.clone, s32[256]{0:T(256)S(1)} %bitcast.364, f32[256,16,128]{2,1,0:T(8,128)S(1)} %fusion.27), kind=kCustom, calls=%fused_computation.13 | custom fusion | flops 524288 | bytes 6292480 | tf_op jit(solution)/shard_map/scatter-add | solution.py:14
  87.7 1.1 copy_bitcast_fusion.5
  88.8 64.2 %reduce-scatter.15.cloned.1.call-done = f32[16,2048]{1,0:T(8,128)} async-done(((f32[16,16384]{1,0:T(8,128)}), f32[16,2048]{1,0:T(8,128)}) %reduce-scatter.15.cloned.1.call-update) | async-done | bytes 131088 | tf_op jit(solution)/shard_map/reduce_scatter | solution.py:57
  153.1 1.0 fusion.142
  154.1 28.9 %all_gather.38 = bf16[16,16384]{1,0:T(8,128)(2,1)S(1)} all-gather(bf16[16,2048]{1,0:T(8,128)(2,1)S(1)} %fusion.142), channel_id=1, replica_groups=mesh['grp'=2,'col'=8,'row'=2] {'col'}, dimensions={1}, use_global_device_ids=true | all-gather | bytes 589824 | tf_op jit(solution)/shard_map/all_gather | solution.py:50
  184.1 5.0 fusion.30
  189.1 9.3 %scatter_fusion.2 = f32[32,16,128]{2,1,0:T(8,128)S(1)} fusion(f32[32,16,128]{2,1,0:T(8,128)S(1)} %broadcast.36.clone.1, s32[256]{0:T(256)} %bitcast.367, f32[256,16,128]{2,1,0:T(8,128)S(1)} %fusion.30), kind=kCustom, calls=%fused_computation.14 | custom fusion | flops 524288 | bytes 6292480 | tf_op jit(solution)/shard_map/scatter-add | solution.py:22
  199.2 9.6 %reduce-scatter.17.cloned.1.call-done = f32[16,2048]{1,0:T(8,128)} async-done(((f32[16,4096]{1,0:T(8,128)}), f32[16,2048]{1,0:T(8,128)}) %reduce-scatter.17.cloned.1.call-update) | async-done | bytes 131088 | tf_op jit(solution)/shard_map/reduce_scatter | solution.py:52
  208.8 1.6 subtract_convert_fusion.4
  210.4 2.1 all_gather.39
  212.5 1.0 gather_fusion.3
  213.5 7.1 fusion.33
  220.7 9.0 %scatter_fusion.3 = f32[128,16,128]{2,1,0:T(8,128)S(1)} fusion(f32[128,16,128]{2,1,0:T(8,128)S(1)} %broadcast.39.clone.1, s32[256]{0:T(256)} %bitcast.361, f32[256,16,128]{2,1,0:T(8,128)S(1)} %fusion.33), kind=kCustom, calls=%fused_computation.15 | custom fusion | flops 524288 | bytes 6292480 | tf_op jit(solution)/shard_map/scatter-add | solution.py:14
  229.8 1.1 copy_bitcast_fusion.4
  230.9 64.2 %reduce-scatter.19.cloned.1.call-done = f32[16,2048]{1,0:T(8,128)} async-done(((f32[16,16384]{1,0:T(8,128)}), f32[16,2048]{1,0:T(8,128)}) %reduce-scatter.19.cloned.1.call-update) | async-done | bytes 131088 | tf_op jit(solution)/shard_map/reduce_scatter | solution.py:57
  295.2 1.7 fusion.158
  296.8 28.9 %all_gather.40 = bf16[16,16384]{1,0:T(8,128)(2,1)S(1)} all-gather(bf16[16,2048]{1,0:T(8,128)(2,1)S(1)} %get-tuple-element.16), channel_id=1, replica_groups=mesh['grp'=2,'col'=8,'row'=2] {'col'}, dimensions={1}, use_global_device_ids=true | all-gather | bytes 589824 | tf_op jit(solution)/shard_map/all_gather | solution.py:50
  326.9 5.2 fusion.36
  332.1 9.0 %scatter_fusion.4 = f32[32,16,128]{2,1,0:T(8,128)S(1)} fusion(f32[32,16,128]{2,1,0:T(8,128)S(1)} %broadcast.36.clone.2, s32[256]{0:T(256)S(1)} %bitcast.374, f32[256,16,128]{2,1,0:T(8,128)S(1)} %fusion.36), kind=kCustom, calls=%fused_computation.16 | custom fusion | flops 524288 | bytes 6292480 | tf_op jit(solution)/shard_map/scatter-add | solution.py:22
  342.0 9.5 %reduce-scatter.21.cloned.1.call-done = f32[16,2048]{1,0:T(8,128)} async-done(((f32[16,4096]{1,0:T(8,128)}), f32[16,2048]{1,0:T(8,128)}) %reduce-scatter.21.cloned.1.call-update) | async-done | bytes 131088 | tf_op jit(solution)/shard_map/reduce_scatter | solution.py:52
  352.5 1.9 all_gather.41
  354.4 1.0 gather_fusion.5
  355.4 7.1 fusion.39
  362.6 9.0 %scatter_fusion.5 = f32[128,16,128]{2,1,0:T(8,128)S(1)} fusion(f32[128,16,128]{2,1,0:T(8,128)S(1)} %broadcast.39.clone.2, s32[256]{0:T(256)} %bitcast.362, f32[256,16,128]{2,1,0:T(8,128)S(1)} %fusion.39), kind=kCustom, calls=%fused_computation.17 | custom fusion | flops 524288 | bytes 6292480 | tf_op jit(solution)/shard_map/scatter-add | solution.py:14
  371.6 1.1 copy_bitcast_fusion.3
  372.8 64.2 %reduce-scatter.23.cloned.1.call-done = f32[16,2048]{1,0:T(8,128)} async-done(((f32[16,16384]{1,0:T(8,128)}), f32[16,2048]{1,0:T(8,128)}) %reduce-scatter.23.cloned.1.call-update) | async-done | bytes 131088 | tf_op jit(solution)/shard_map/reduce_scatter | solution.py:57
  438.0 28.9 %all_gather.42 = bf16[16,16384]{1,0:T(8,128)(2,1)S(1)} all-gather(bf16[16,2048]{1,0:T(8,128)(2,1)S(1)} %fusion.141), channel_id=1, replica_groups=mesh['grp'=2,'col'=8,'row'=2] {'col'}, dimensions={1}, use_global_device_ids=true | all-gather | bytes 589824 | tf_op jit(solution)/shard_map/all_gather | solution.py:50
  468.0 5.0 fusion.42
  473.0 9.2 %scatter_fusion.6 = f32[32,16,128]{2,1,0:T(8,128)S(1)} fusion(f32[32,16,128]{2,1,0:T(8,128)S(1)} %broadcast.36.clone.3, s32[256]{0:T(256)} %bitcast.368, f32[256,16,128]{2,1,0:T(8,128)S(1)} %fusion.42), kind=kCustom, calls=%fused_computation.18 | custom fusion | flops 524288 | bytes 6292480 | tf_op jit(solution)/shard_map/scatter-add | solution.py:22
  483.0 9.6 %reduce-scatter.25.cloned.1.call-done = f32[16,2048]{1,0:T(8,128)} async-done(((f32[16,4096]{1,0:T(8,128)}), f32[16,2048]{1,0:T(8,128)}) %reduce-scatter.25.cloned.1.call-update) | async-done | bytes 131088 | tf_op jit(solution)/shard_map/reduce_scatter | solution.py:52
  492.5 1.6 subtract_convert_fusion.2
  494.1 2.1 all_gather.43
  496.3 1.0 gather_fusion.7
  497.3 7.1 fusion.45
  504.5 8.9 %scatter_fusion.7 = f32[128,16,128]{2,1,0:T(8,128)S(1)} fusion(f32[128,16,128]{2,1,0:T(8,128)S(1)} %broadcast.39.clone.3, s32[256]{0:T(256)S(1)} %bitcast.365, f32[256,16,128]{2,1,0:T(8,128)S(1)} %fusion.45), kind=kCustom, calls=%fused_computation.19 | custom fusion | flops 524288 | bytes 6292480 | tf_op jit(solution)/shard_map/scatter-add | solution.py:14
  513.4 1.1 copy_bitcast_fusion.2
  514.5 64.3 %reduce-scatter.27.cloned.1.call-done = f32[16,2048]{1,0:T(8,128)} async-done(((f32[16,16384]{1,0:T(8,128)}), f32[16,2048]{1,0:T(8,128)}) %reduce-scatter.27.cloned.1.call-update) | async-done | bytes 131088 | tf_op jit(solution)/shard_map/reduce_scatter | solution.py:57
  579.8 28.9 %all_gather.44 = bf16[16,16384]{1,0:T(8,128)(2,1)S(1)} all-gather(bf16[16,2048]{1,0:T(8,128)(2,1)S(1)} %get-tuple-element.10), channel_id=1, replica_groups=mesh['grp'=2,'col'=8,'row'=2] {'col'}, dimensions={1}, use_global_device_ids=true | all-gather | bytes 589824 | tf_op jit(solution)/shard_map/all_gather | solution.py:50
  609.8 5.0 fusion.48
  614.9 9.3 %scatter_fusion.8 = f32[32,16,128]{2,1,0:T(8,128)S(1)} fusion(f32[32,16,128]{2,1,0:T(8,128)S(1)} %broadcast.36.clone.4, s32[256]{0:T(256)} %bitcast.369, f32[256,16,128]{2,1,0:T(8,128)S(1)} %fusion.48), kind=kCustom, calls=%fused_computation.20 | custom fusion | flops 524288 | bytes 6292480 | tf_op jit(solution)/shard_map/scatter-add | solution.py:22
  625.0 9.6 %reduce-scatter.29.cloned.1.call-done = f32[16,2048]{1,0:T(8,128)} async-done(((f32[16,4096]{1,0:T(8,128)}), f32[16,2048]{1,0:T(8,128)}) %reduce-scatter.29.cloned.1.call-update) | async-done | bytes 131088 | tf_op jit(solution)/shard_map/reduce_scatter | solution.py:52
  634.6 1.6 subtract_convert_fusion.1
  636.2 1.9 all_gather.45
  639.1 7.1 fusion.51
  646.3 9.0 %scatter_fusion.9 = f32[128,16,128]{2,1,0:T(8,128)S(1)} fusion(f32[128,16,128]{2,1,0:T(8,128)S(1)} %broadcast.39.clone.4, s32[256]{0:T(256)} %bitcast.363, f32[256,16,128]{2,1,0:T(8,128)S(1)} %fusion.51), kind=kCustom, calls=%fused_computation.21 | custom fusion | flops 524288 | bytes 6292480 | tf_op jit(solution)/shard_map/scatter-add | solution.py:14
  655.3 1.1 copy_bitcast_fusion.1
  656.5 64.4 %reduce-scatter.31.cloned.1.call-done = f32[16,2048]{1,0:T(8,128)} async-done(((f32[16,16384]{1,0:T(8,128)}), f32[16,2048]{1,0:T(8,128)}) %reduce-scatter.31.cloned.1.call-update) | async-done | bytes 131088 | tf_op jit(solution)/shard_map/reduce_scatter | solution.py:57
  721.8 28.9 %all_gather.46 = bf16[16,16384]{1,0:T(8,128)(2,1)S(1)} all-gather(bf16[16,2048]{1,0:T(8,128)(2,1)S(1)} %fusion.140), channel_id=1, replica_groups=mesh['grp'=2,'col'=8,'row'=2] {'col'}, dimensions={1}, use_global_device_ids=true | all-gather | bytes 589824 | tf_op jit(solution)/shard_map/all_gather | solution.py:50
  751.8 5.0 fusion.54
  756.9 9.3 %scatter_fusion.10 = f32[32,16,128]{2,1,0:T(8,128)S(1)} fusion(f32[32,16,128]{2,1,0:T(8,128)S(1)} %broadcast.36, s32[256]{0:T(256)} %bitcast.370, f32[256,16,128]{2,1,0:T(8,128)S(1)} %fusion.54), kind=kCustom, calls=%fused_computation.22 | custom fusion | flops 524288 | bytes 6292480 | tf_op jit(solution)/shard_map/scatter-add | solution.py:22
  767.0 9.6 %reduce-scatter.33.cloned.1.call-done = f32[16,2048]{1,0:T(8,128)} async-done(((f32[16,4096]{1,0:T(8,128)}), f32[16,2048]{1,0:T(8,128)}) %reduce-scatter.33.cloned.1.call-update) | async-done | bytes 131088 | tf_op jit(solution)/shard_map/reduce_scatter | solution.py:52
  776.6 1.6 subtract_convert_fusion
  778.2 2.1 all_gather.47
  781.4 7.1 fusion.57
  788.6 8.9 %scatter_fusion.11 = f32[128,16,128]{2,1,0:T(8,128)S(1)} fusion(f32[128,16,128]{2,1,0:T(8,128)S(1)} %broadcast.39, s32[256]{0:T(256)S(1)} %bitcast.366, f32[256,16,128]{2,1,0:T(8,128)S(1)} %fusion.57), kind=kCustom, calls=%fused_computation.23 | custom fusion | flops 524288 | bytes 6292480 | tf_op jit(solution)/shard_map/scatter-add | solution.py:14
  797.5 1.1 copy_bitcast_fusion
  799.4 63.6 %reduce-scatter.35.cloned.1.call-done = f32[16,2048]{1,0:T(8,128)} async-done(((f32[16,16384]{1,0:T(8,128)}), f32[16,2048]{1,0:T(8,128)}) %reduce-scatter.35.cloned.1.call-update) | async-done | bytes 131088 | tf_op jit(solution)/shard_map/reduce_scatter | solution.py:57
  (142 shorter events, 23.8 us)
Async XLA Ops:
  7.2 59.7 %reduce-scatter.13.cloned.1.call-start = ((), (), s32[]{:S(2)}) async-start(), calls=%async_computation.12 | async-start | bytes 393216 | tf_op jit(solution)/shard_map/reduce_scatter | solution.py:52
  9.2 35.9 %copy-start.28 = (pred[256]{0:T(512)(128)(4,1)}, pred[256]{0:T(512)(128)(4,1)S(1)}, u32[]{:S(2)}) copy-start(pred[256]{0:T(512)(128)(4,1)S(1)} %get-tuple-element.24) | copy-start | bytes 772
  9.2 35.9 %copy-start.27 = (s32[1024]{0:T(1024)}, s32[1024]{0:T(1024)S(1)}, u32[]{:S(2)}) copy-start(s32[1024]{0:T(1024)S(1)} %pad_clamp_fusion.1) | copy-start | bytes 12292
  39.9 5.3 copy-start.24
  45.2 9.9 %copy-start.31 = (s32[1,2048]{1,0:T(1,128)S(1)}, s32[1,2048]{1,0:T(1,128)}, u32[]{:S(2)}) copy-start(s32[1,2048]{1,0:T(1,128)} %param.18) | copy-start | bytes 24580
  45.2 21.7 %copy-start.1 = (f32[16,1,2048]{2,1,0:T(1,128)S(1)}, f32[16,1,2048]{2,1,0:T(1,128)}, u32[]{:S(2)}) copy-start(f32[16,1,2048]{2,1,0:T(1,128)} %param.14) | copy-start | bytes 393220
  45.2 21.7 %copy-start.13 = (f32[1,2048]{1,0:T(1,128)S(1)}, f32[1,2048]{1,0:T(1,128)}, u32[]{:S(2)}) copy-start(f32[1,2048]{1,0:T(1,128)} %param.19) | copy-start | bytes 24580
  45.2 21.7 %copy-start.14 = (f32[16,1,2048]{2,1,0:T(1,128)S(1)}, f32[16,1,2048]{2,1,0:T(1,128)}, u32[]{:S(2)}) copy-start(f32[16,1,2048]{2,1,0:T(1,128)} %param.16) | copy-start | bytes 393220
  55.0 98.0 %reduce-scatter.15.cloned.1.call-start = ((), (), s32[]{:S(2)}) async-start(), calls=%async_computation.13 | async-start | bytes 1179648 | tf_op jit(solution)/shard_map/reduce_scatter | solution.py:57
  55.1 23.5 %copy-start.26 = (s32[1024]{0:T(1024)}, s32[1024]{0:T(1024)S(1)}, u32[]{:S(2)}) copy-start(s32[1024]{0:T(1024)S(1)} %pad_clamp_fusion) | copy-start | bytes 12292
  55.2 13.4 %copy-start.15 = (pred[2048]{0:T(1024)(128)(4,1)}, pred[2048]{0:T(1024)(128)(4,1)S(1)}, u32[]{:S(2)}) copy-start(pred[2048]{0:T(1024)(128)(4,1)S(1)} %get-tuple-element.7) | copy-start | bytes 6148
  55.2 23.5 %copy-start.30 = (pred[256]{0:T(512)(128)(4,1)}, pred[256]{0:T(512)(128)(4,1)S(1)}, u32[]{:S(2)}) copy-start(pred[256]{0:T(512)(128)(4,1)S(1)} %compare_and_fusion) | copy-start | bytes 772
  71.3 7.4 copy-start.21
  87.6 65.4 %copy-start = (f32[16,1,2048]{2,1,0:T(1,128)S(1)}, f32[16,1,2048]{2,1,0:T(1,128)}, u32[]{:S(2)}) copy-start(f32[16,1,2048]{2,1,0:T(1,128)} %param.15) | copy-start | bytes 393220
  87.7 65.4 %copy-start.2 = (f32[16,1,2048]{2,1,0:T(1,128)S(1)}, f32[16,1,2048]{2,1,0:T(1,128)}, u32[]{:S(2)}) copy-start(f32[16,1,2048]{2,1,0:T(1,128)} %param.17) | copy-start | bytes 393220
  88.7 120.1 %reduce-scatter.17.cloned.1.call-start = ((), (), s32[]{:S(2)}) async-start(), calls=%async_computation.14 | async-start | bytes 393216 | tf_op jit(solution)/shard_map/reduce_scatter | solution.py:52
  189.1 19.7 %copy-start.12 = (f32[16,2048]{1,0:T(8,128)S(1)}, f32[16,2048]{1,0:T(8,128)}, u32[]{:S(2)}) copy-start(f32[16,2048]{1,0:T(8,128)} %get-tuple-element.21) | copy-start | bytes 393220
  189.1 19.7 %copy-start.16 = (pred[2048]{0:T(1024)(128)(4,1)S(1)}, pred[2048]{0:T(1024)(128)(4,1)}, u32[]{:S(2)}) copy-start(pred[2048]{0:T(1024)(128)(4,1)} %copy-done.15) | copy-start | bytes 6148
  199.1 96.0 %reduce-scatter.19.cloned.1.call-start = ((), (), s32[]{:S(2)}) async-start(), calls=%async_computation.15 | async-start | bytes 1179648 | tf_op jit(solution)/shard_map/reduce_scatter | solution.py:57
  229.8 65.4 %copy-start.7 = (f32[16,2048]{1,0:T(8,128)S(1)}, f32[16,2048]{1,0:T(8,128)}, u32[]{:S(2)}) copy-start(f32[16,2048]{1,0:T(8,128)} %reduce-scatter.15.cloned.1.call-done) | copy-start | bytes 393220
  230.9 96.0 %copy-start.29 = (pred[256]{0:T(512)(128)(4,1)S(1)}, pred[256]{0:T(512)(128)(4,1)}, u32[]{:S(2)}) copy-start(pred[256]{0:T(512)(128)(4,1)} %copy-done.28) | copy-start | bytes 772
  230.9 120.6 %reduce-scatter.21.cloned.1.call-start = ((), (), s32[]{:S(2)}) async-start(), calls=%async_computation.16 | async-start | bytes 393216 | tf_op jit(solution)/shard_map/reduce_scatter | solution.py:52
  326.9 5.3 copy-start.25
  332.1 19.3 %copy-start.11 = (f32[16,2048]{1,0:T(8,128)S(1)}, f32[16,2048]{1,0:T(8,128)}, u32[]{:S(2)}) copy-start(f32[16,2048]{1,0:T(8,128)} %get-tuple-element.19) | copy-start | bytes 393220
  332.1 19.3 %copy-start.17 = (pred[2048]{0:T(1024)(128)(4,1)S(1)}, pred[2048]{0:T(1024)(128)(4,1)}, u32[]{:S(2)}) copy-start(pred[2048]{0:T(1024)(128)(4,1)} %copy-done.15) | copy-start | bytes 6148
  341.9 95.1 %reduce-scatter.23.cloned.1.call-start = ((), (), s32[]{:S(2)}) async-start(), calls=%async_computation.17 | async-start | bytes 1179648 | tf_op jit(solution)/shard_map/reduce_scatter | solution.py:57
  371.6 65.4 %copy-start.3 = (f32[16,2048]{1,0:T(8,128)S(1)}, f32[16,2048]{1,0:T(8,128)}, u32[]{:S(2)}) copy-start(f32[16,2048]{1,0:T(8,128)} %get-tuple-element.17) | copy-start | bytes 393220
  372.7 119.8 %reduce-scatter.25.cloned.1.call-start = ((), (), s32[]{:S(2)}) async-start(), calls=%async_computation.18 | async-start | bytes 393216 | tf_op jit(solution)/shard_map/reduce_scatter | solution.py:52
  473.0 19.5 %copy-start.18 = (pred[2048]{0:T(1024)(128)(4,1)S(1)}, pred[2048]{0:T(1024)(128)(4,1)}, u32[]{:S(2)}) copy-start(pred[2048]{0:T(1024)(128)(4,1)} %copy-done.15) | copy-start | bytes 6148
  482.9 95.9 %reduce-scatter.27.cloned.1.call-start = ((), (), s32[]{:S(2)}) async-start(), calls=%async_computation.19 | async-start | bytes 1179648 | tf_op jit(solution)/shard_map/reduce_scatter | solution.py:57
  497.3 7.2 copy-start.22
  513.4 65.4 %copy-start.4 = (f32[16,2048]{1,0:T(8,128)S(1)}, f32[16,2048]{1,0:T(8,128)}, u32[]{:S(2)}) copy-start(f32[16,2048]{1,0:T(8,128)} %get-tuple-element.17) | copy-start | bytes 393220
  513.4 65.4 %copy-start.6 = (f32[16,2048]{1,0:T(8,128)S(1)}, f32[16,2048]{1,0:T(8,128)}, u32[]{:S(2)}) copy-start(f32[16,2048]{1,0:T(8,128)} %reduce-scatter.23.cloned.1.call-done) | copy-start | bytes 393220
  514.5 120.1 %reduce-scatter.29.cloned.1.call-start = ((), (), s32[]{:S(2)}) async-start(), calls=%async_computation.20 | async-start | bytes 393216 | tf_op jit(solution)/shard_map/reduce_scatter | solution.py:52
  614.8 19.7 %copy-start.9 = (f32[16,2048]{1,0:T(8,128)S(1)}, f32[16,2048]{1,0:T(8,128)}, u32[]{:S(2)}) copy-start(f32[16,2048]{1,0:T(8,128)} %get-tuple-element.13) | copy-start | bytes 393220
  614.8 19.7 %copy-start.19 = (pred[2048]{0:T(1024)(128)(4,1)S(1)}, pred[2048]{0:T(1024)(128)(4,1)}, u32[]{:S(2)}) copy-start(pred[2048]{0:T(1024)(128)(4,1)} %copy-done.15) | copy-start | bytes 6148
  624.9 96.0 %reduce-scatter.31.cloned.1.call-start = ((), (), s32[]{:S(2)}) async-start(), calls=%async_computation.21 | async-start | bytes 1179648 | tf_op jit(solution)/shard_map/reduce_scatter | solution.py:57
  656.4 120.2 %reduce-scatter.33.cloned.1.call-start = ((), (), s32[]{:S(2)}) async-start(), calls=%async_computation.22 | async-start | bytes 393216 | tf_op jit(solution)/shard_map/reduce_scatter | solution.py:52
  756.8 19.8 %copy-start.10 = (f32[16,2048]{1,0:T(8,128)S(1)}, f32[16,2048]{1,0:T(8,128)}, u32[]{:S(2)}) copy-start(f32[16,2048]{1,0:T(8,128)} %get-tuple-element.9) | copy-start | bytes 393220
  756.9 19.7 %copy-start.20 = (pred[2048]{0:T(1024)(128)(4,1)S(1)}, pred[2048]{0:T(1024)(128)(4,1)}, u32[]{:S(2)}) copy-start(pred[2048]{0:T(1024)(128)(4,1)} %copy-done.15) | copy-start | bytes 6148
  766.9 96.1 %reduce-scatter.35.cloned.1.call-start = ((), (), s32[]{:S(2)}) async-start(), calls=%async_computation.23 | async-start | bytes 1179648 | tf_op jit(solution)/shard_map/reduce_scatter | solution.py:57
  781.4 7.2 copy-start.23
  797.5 1.1 copy-start.8
  797.5 65.5 %copy-start.5 = (f32[16,2048]{1,0:T(8,128)S(1)}, f32[16,2048]{1,0:T(8,128)}, u32[]{:S(2)}) copy-start(f32[16,2048]{1,0:T(8,128)} %reduce-scatter.31.cloned.1.call-done) | copy-start | bytes 393220
Sparse Core Ops, SparseCore 0:
  55.1 11.7 reduce-scatter.12
  88.9 64.1 reduce-scatter.14
  199.3 9.4 reduce-scatter.16
  231.0 64.1 reduce-scatter.18
  342.0 9.3 reduce-scatter.20
  372.8 64.1 reduce-scatter.22
  483.0 9.4 reduce-scatter.24
  514.6 64.1 reduce-scatter.26
  625.0 9.4 reduce-scatter.28
  656.5 64.2 reduce-scatter.30
  767.0 9.5 reduce-scatter.32
  798.7 64.2 reduce-scatter.34
where the time goes:
time: 874 us; the launch traced here: 872 us
  waiting for transfers between devices  445 us (51%)
  blocking collectives  185 us (21%)
  other arithmetic  126 us (14%)
  matrix products  73 us (8%)
  local copies, waits for them, and re-layouts  26.1 us (3%)
  between operations  15.6 us (2%)
    reduce_scatter x6, waiting for transfers between devices, per_device(): lax.psum_scatter(partial_image, 'col', scatter_dimension=1, tiled=True)  385 us
    all_gather x6, blocking collectives, per_device(): lax.all_gather(y_state.astype(jnp.bfloat16), 'col', axis=1, tiled=True)  173 us
    reduce_scatter x6, waiting for transfers between devices, per_device(): lax.psum_scatter(partial_grad, 'row', scatter_dimension=1, tiled=True)  59.6 us
    scatter-add x6, other arithmetic, backward_tile(): summed = jax.ops.segment_sum(prod, bcol, num_segments=segments)  55.2 us
    scatter-add x6, other arithmetic, forward_tile(): summed = jax.ops.segment_sum(prod, brow, num_segments=segments)  53.9 us
    dot_general x6, matrix products, forward_tile(): jnp.einsum('nij,snj->nsi', kb, picked, preferred_element_type=jnp.float32)  42.7 us
    dot_general x6, matrix products, backward_tile(): jnp.einsum('nij,sni->nsj', kb, picked, preferred_element_type=jnp.float32)  30.3 us
  transfers between devices with their start and end apart: 12, of which 12 were waited for; matrix products, arithmetic and copies ran while one was open for 0% of the time, Pallas kernels for 0%

commit v1 on v0

v1 whole, which is shorter than its diff:
```python
import functools

import jax
import jax.numpy as jnp
from jax import lax
from jax.experimental import pallas as pl
from jax.experimental.pallas import tpu as pltpu
from jax.sharding import PartitionSpec as P

BS = 128
ITERS = 6
UNROLL = 32
NN = (((1,), (0,)), ((), ()))
NT = (((1,), (1,)), ((), ()))

SMEM = pl.BlockSpec(memory_space=pltpu.SMEM)
VMEM = pl.BlockSpec(memory_space=pltpu.VMEM)
PARAMS = pltpu.CompilerParams(vmem_limit_bytes=24 * 2**20)


def products(groups, src, dst, vecs, blocks, acc, dims):
    def group(g, _):
        first = g * UNROLL
        terms = [
            lax.dot_general(vecs[src[first + u]], blocks[first + u], dims, preferred_element_type=jnp.float32)
            for u in range(UNROLL)
        ]
        for u in range(UNROLL):
            acc[dst[first + u]] += terms[u]
        return 0

    lax.fori_loop(0, groups, group, 0)


def backward_kernel(n_pieces, groups, src, dst, blocks, *refs):
    pieces, (grad, vecs, acc) = refs[:n_pieces], refs[n_pieces:]
    span = pieces[0].shape[0]
    for m in range(n_pieces):
        vecs[pl.ds(m * span, span)] = pieces[m][...]
    acc[...] = jnp.zeros(acc.shape, acc.dtype)
    products(groups[0], src, dst, vecs, blocks, acc, NN)
    grad[...] = acc[pl.ds(0, grad.shape[0])]


def forward_kernel(n_pieces, groups, src, dst, blocks, own, other, x_ref, cost, kind, upper, *refs):
    x_out, pieces, (vecs, acc) = refs[0], refs[1 : 1 + n_pieces], refs[1 + n_pieces :]
    x = x_ref[...]
    value = x - 0.4 * (cost[...] - (own[...] + other[...]))
    lifted = jnp.where(kind[...] == 2, value, jnp.maximum(value, 0.0))
    x_next = jnp.where(kind[...] == 1, jnp.minimum(lifted, upper[...]), lifted)
    x_out[...] = x_next
    vecs[...] = (2.0 * x_next - x).astype(vecs.dtype)
    acc[...] = jnp.zeros(acc.shape, acc.dtype)
    products(groups[0], src, dst, vecs, blocks, acc, NT)
    span = pieces[0].shape[0]
    for m in range(n_pieces):
        pieces[m][...] = acc[pl.ds(m * span, span)].astype(pieces[m].dtype)


def dual_kernel(n_pieces, y_ref, rhs, *refs):
    pieces, (y_out, y_half) = refs[:n_pieces], refs[n_pieces:]
    image = pieces[0][...]
    for m in range(1, n_pieces):
        image = image + pieces[m][...].astype(jnp.float32)
    y = jnp.maximum(0.0, y_ref[...] + 0.9 * (rhs[...] - image))
    y_out[...] = y
    y_half[...] = y.astype(y_half.dtype)


def to_blocks(a):
    return jnp.transpose(a.reshape(a.shape[0], -1, BS), (1, 0, 2))


def from_blocks(a):
    return jnp.transpose(a, (1, 0, 2)).reshape(a.shape[1], -1)


def per_device(
    cost, rhs, primal, dual, bound_kind, upper, kblocks, block_row, block_col, block_count
):
    n_col = lax.axis_size("col")
    n_row = lax.axis_size("row")
    scen = primal.shape[0]
    own_cols, own_rows = primal.shape[2], dual.shape[2]
    span = own_rows // BS
    col_blocks = own_cols * n_row // BS
    row_blocks = span * n_col
    direct = n_col <= 8 and n_col & (n_col - 1) == 0 and span & (span - 1) == 0
    n_pieces = n_col if direct else 1

    tile = kblocks[0, 0]
    slots = jnp.arange(tile.shape[0], dtype=jnp.int32)
    count = block_count[0, 0]
    live = slots < count
    groups = ((count + UNROLL - 1) // UNROLL).reshape(1)
    brow, bcol = block_row[0, 0], block_col[0, 0]
    if direct:
        brow = brow ^ (lax.axis_index("col") * span)
    to_col = jnp.where(live, bcol, col_blocks)
    to_row = jnp.where(live, brow, row_blocks)

    def swap(a):
        return lax.ppermute(a, "row", [(i, n_row - 1 - i) for i in range(n_row)])

    def whole(a):
        return lax.all_gather(a, "row", axis=0, tiled=True)

    x = whole(to_blocks(primal[:, 0]))
    cost_all = whole(to_blocks(cost[:, 0]))
    kind_all = whole(to_blocks(bound_kind))
    upper_all = whole(to_blocks(upper))
    y = to_blocks(dual[:, 0])
    rhs_own = to_blocks(rhs[:, 0])

    def partner(a, m):
        return lax.ppermute(a, "col", [(i, i ^ m) for i in range(n_col)])

    x_shape = jax.ShapeDtypeStruct(x.shape, jnp.float32)
    y_shape = jax.ShapeDtypeStruct(y.shape, jnp.float32)
    y_half_shape = jax.ShapeDtypeStruct(y.shape, jnp.bfloat16)
    if direct:
        piece_shapes = (y_shape,) + (y_half_shape,) * (n_pieces - 1)
    else:
        piece_shapes = (jax.ShapeDtypeStruct((row_blocks, scen, BS), jnp.float32),)

    backward = pl.pallas_call(
        functools.partial(backward_kernel, n_pieces),
        out_shape=x_shape,
        in_specs=[SMEM] * 3 + [VMEM] * (1 + n_pieces),
        out_specs=VMEM,
        scratch_shapes=[
            pltpu.VMEM((row_blocks, scen, BS), jnp.bfloat16),
            pltpu.VMEM((col_blocks + 1, scen, BS), jnp.float32),
        ],
        compiler_params=PARAMS,
        name="backward",
    )
    forward = pl.pallas_call(
        functools.partial(forward_kernel, n_pieces),
        out_shape=(x_shape,) + piece_shapes,
        in_specs=[SMEM] * 3 + [VMEM] * 7,
        out_specs=(VMEM,) * (1 + n_pieces),
        scratch_shapes=[
            pltpu.VMEM((col_blocks, scen, BS), jnp.bfloat16),
            pltpu.VMEM((row_blocks + 1, scen, BS), jnp.float32),
        ],
        compiler_params=PARAMS,
        name="forward",
    )
    dual_step = pl.pallas_call(
        functools.partial(dual_kernel, n_pieces),
        out_shape=(y_shape, y_half_shape),
        in_specs=[VMEM] * (2 + n_pieces),
        out_specs=(VMEM, VMEM),
        compiler_params=PARAMS,
        name="dual_step",
    )

    y_half = y.astype(jnp.bfloat16)
    for step in range(ITERS):
        if direct:
            y_slab = [y_half] + [partner(y_half, m) for m in range(1, n_col)]
        else:
            y_slab = [lax.all_gather(y_half, "col", axis=0, tiled=True)]
        grad = backward(groups, brow, to_col, tile, *y_slab)
        x, *pieces = forward(groups, bcol, to_row, tile, grad, swap(grad), x, cost_all, kind_all, upper_all)
        if direct:
            image = pieces[:1] + [partner(pieces[m], m) for m in range(1, n_col)]
        else:
            image = [lax.psum_scatter(pieces[0], "col", scatter_dimension=0, tiled=True)]
        y, y_half = dual_step(y, rhs_own, *image)

    here = lax.axis_index("row") * (own_cols // BS)
    x_own = lax.dynamic_slice_in_dim(x, here, own_cols // BS, axis=0)
    return (from_blocks(x_own)[:, None, :], from_blocks(y)[:, None, :])


def solution(mesh):
    return jax.shard_map(
        per_device,
        mesh=mesh,
        in_specs=(
            P("grp", "col", "row"),
            P("grp", "row", "col"),
            P("grp", "col", "row"),
            P("grp", "row", "col"),
            P(("grp", "col"), "row"),
            P(("grp", "col"), "row"),
            P(("grp", "col"), "row", None, None, None),
            P(("grp", "col"), "row", None),
            P(("grp", "col"), "row", None),
            P(("grp", "col"), "row"),
        ),
        out_specs=(P("grp", "col", "row"), P("grp", "row", "col")),
        check_vma=False,
    )
```

time: 874 us -> 279 us (0.32)
  waiting for transfers between devices: 445 us -> 83.8 us
  blocking collectives: 185 us -> 8.14 us
  other arithmetic: 126 us -> 1.37 us
  starting transfers between devices: 0.5 us -> 114 us
  matrix products: 73 us -> 0 us
  Pallas kernels: 0 us -> 61.1 us
  local copies, waits for them, and re-layouts: 26.1 us -> 7.75 us
  between operations: 15.6 us -> 1.73 us
    reduce_scatter x12 -> x0, waiting for transfers between devices: 445 us -> none  [the longest x6 385 us: per_device(): lax.psum_scatter(partial_image, 'col', scatter_dimension=1, tiled=True)]
    all_gather x12 -> x4, blocking collectives: 185 us -> 8.14 us  [whole(): return lax.all_gather(a, 'row', axis=0, tiled=True)]
    ppermute x0 -> x90, starting transfers between devices: none -> 114 us  [the longest x84 113 us: partner(): return lax.ppermute(a, 'col', [(i, i ^ m) for i in range(n_col)])]
    scatter-add x12 -> x0, other arithmetic: 109 us -> none  [the longest x6 55.2 us: backward_tile(): summed = jax.ops.segment_sum(prod, bcol, num_segments=segments)]
    ppermute x0 -> x90, waiting for transfers between devices: none -> 83.8 us  [the longest x84 76.2 us: partner(): return lax.ppermute(a, 'col', [(i, i ^ m) for i in range(n_col)])]
    dot_general x12 -> x0, matrix products: 73 us -> none  [the longest x6 42.7 us: forward_tile(): jnp.einsum('nij,snj->nsi', kb, picked, preferred_element_type=jnp.float32)]
    pallas_call x0 -> x18, Pallas kernels: none -> 61.1 us  [the longest x6 37.1 us: per_device(): forward(groups, bcol, to_row, tile, grad, swap(grad), x, cost_all, kind_a...]
    convert_element_type x11 -> x0, other arithmetic: 14.8 us -> none  [the longest x6 9.2 us: per_device(): x_bar = (2.0 * x_next - x_state).astype(jnp.bfloat16)]
  transfers between devices with their start and end apart: 12 -> 90, of which waited for: 12 -> 53; matrix products, arithmetic and copies ran while one was open for 0% -> 1% of each run, Pallas kernels for 0% -> 0%
where the time goes in v1:
time: 279 us; the launch traced here: 278 us
  starting transfers between devices  114 us (41%)
  waiting for transfers between devices  83.8 us (30%)
  Pallas kernels  61.1 us (22%)
  blocking collectives  8.14 us (3%)
  local copies, waits for them, and re-layouts  7.75 us (3%)
    ppermute x84, starting transfers between devices, partner(): return lax.ppermute(a, 'col', [(i, i ^ m) for i in range(n_col)])  113 us
    ppermute x84, waiting for transfers between devices, partner(): return lax.ppermute(a, 'col', [(i, i ^ m) for i in range(n_col)])  76.2 us
    pallas_call x6, Pallas kernels, per_device(): forward(groups, bcol, to_row, tile, grad, swap(grad), x, cost_all, kind_a...  37.1 us
    pallas_call x6, Pallas kernels, per_device(): grad = backward(groups, brow, to_col, tile, *y_slab)  22.8 us
    all_gather x4, blocking collectives, whole(): return lax.all_gather(a, 'row', axis=0, tiled=True)  8.14 us
    ppermute x6, waiting for transfers between devices, swap(): return lax.ppermute(a, 'row', [(i, n_row - 1 - i) for i in range(n_row)])  7.61 us
  transfers between devices with their start and end apart: 90, of which 53 were waited for; matrix products, arithmetic and copies ran while one was open for 1% of the time, Pallas kernels for 0%

profile of v1, /device:TPU:10, one launch (start us, length us, event | category | flops | bytes accessed | tf_op | source)
XLA Modules:
  0.0 277.6 jit_solution(16685682797160725067)
XLA Ops:
  1.6 2.6 collective-permute-start.6
  4.6 4.3 %collective-permute-start.4 = (bf16[16,16,128]{2,1,0:T(8,128)(2,1)S(1)}, bf16[16,16,128]{2,1,0:T(8,128)(2,1)S(1)}, u32[]{:S(2)}, u32[]{:S(2)}) collective-permute-start(bf16[16,16,128]{2,1,0:T(8,128)(2,1)S(1)} %bitcast.53), channel_id=1, source_target_pairs={{0,10},{2,8},{4,14},{6,12},{8,2},{10,0},{12,6},{14,4},{1,11},{3,9}... | collective-permute-start | bytes 196616 | tf_op jit(solution)/shard_map/ppermute | solution.py:116
  9.0 1.7 collective-permute-start.2
  14.7 2.0 all_gather.14.kind
  16.7 2.0 all_gather.15.upper
  20.6 2.0 all_gather.13.cost
  24.3 3.4 %copy-done = bf16[1,1,256,128,128]{4,3,2,1,0:T(8,128)(2,1)S(1)} copy-done((bf16[1,1,256,128,128]{4,3,2,1,0:T(8,128)(2,1)S(1)}, bf16[1,1,256,128,128]{4,3,2,1,0:T(8,128)(2,1)}, u32[]{:S(2)}) %copy-start) | copy-done | bytes 8388632
  27.7 3.8 %backward.6.own = f32[32,16,128]{2,1,0:T(8,128)S(1)} custom-call(s32[1]{0:T(128)} %bitcast.1.groups, s32[256]{0:T(256)S(1)} %bitcast.60, s32[256]{0:T(256)S(1)} %fusion.dst, bf16[256,128,128]{2,1,0:T(8,128)(2,1)S(1)} %bitcast.32, bf16[16,16,128]{2,1,0:T(8,128)(2,1)S(1)} %bitcast.58, bf16[16,16,128]{2,1,0:T(8,128)(2,1)S(1)} %collective-permute-done.refs_1_, ...), custom_call_target="tpu_custom_call" | custom-call | tf_op jit(solution)/shard_map/backward/pallas_call | solution.py:165
  31.5 2.1 all_gather.12.x_ref
  33.7 6.2 %forward.6 = (f32[32,16,128]{2,1,0:T(8,128)S(1)}, f32[16,16,128]{2,1,0:T(8,128)S(1)}, bf16[16,16,128]{2,1,0:T(8,128)(2,1)S(1)}, bf16[16,16,128]{2,1,0:T(8,128)(2...) custom-call(s32[1]{0:T(128)} %bitcast.1.groups, ...), custom_call_target="tpu_custom_call" | custom-call | tf_op jit(solution)/shard_map/forward/pallas_call | solution.py:166
  40.0 3.4 %collective-permute-start.10 = (bf16[16,16,128]{2,1,0:T(8,128)(2,1)S(1)}, bf16[16,16,128]{2,1,0:T(8,128)(2,1)S(1)}, u32[]{:S(2)}, u32[]{:S(2)}) collective-permute-start(bf16[16,16,128]{2,1,0:T(8,128)(2,1)S(1)} %get-tuple-element.70), channel_id=1, source_target_pairs={{0,6},{2,4},{4,2},{6,0},{8,14},{10,12},{12,10},{14,8},{1,7},{3,5},... | collective-permute-start | bytes 196616 | tf_op jit(solution)/shard_map/ppermute | solution.py:116
  43.4 2.4 collective-permute-start.12
  45.9 3.4 %collective-permute-start.14 = (bf16[16,16,128]{2,1,0:T(8,128)(2,1)S(1)}, bf16[16,16,128]{2,1,0:T(8,128)(2,1)S(1)}, u32[]{:S(2)}, u32[]{:S(2)}) collective-permute-start(bf16[16,16,128]{2,1,0:T(8,128)(2,1)S(1)} %get-tuple-element.74), channel_id=1, source_target_pairs={{0,14},{2,12},{4,10},{6,8},{8,6},{10,4},{12,2},{14,0},{1,15},{3,13... | collective-permute-start | bytes 196616 | tf_op jit(solution)/shard_map/ppermute | solution.py:116
  49.4 2.1 collective-permute-done.12.refs_5_
  51.5 4.7 %collective-permute-done.13.refs_6_ = bf16[16,16,128]{2,1,0:T(8,128)(2,1)S(1)} collective-permute-done((bf16[16,16,128]{2,1,0:T(8,128)(2,1)S(1)}, bf16[16,16,128]{2,1,0:T(8,128)(2,1)S(1)}, u32[]{:S(2)}, u32[]{:S(2)}) %collective-permute-start.13) | collective-permute-done | bytes 65568 | tf_op jit(solution)/shard_map/ppermute | solution.py:116
  62.7 2.2 collective-permute-start.17
  65.0 1.9 collective-permute-done.21.refs_7_
  69.3 1.8 collective-permute-done.16.refs_2_
  72.7 3.8 %backward.7.own = f32[32,16,128]{2,1,0:T(8,128)S(1)} custom-call(s32[1]{0:T(128)} %bitcast.1.groups, s32[256]{0:T(256)S(1)} %bitcast.62, s32[256]{0:T(256)S(1)} %fusion.dst, bf16[256,128,128]{2,1,0:T(8,128)(2,1)S(1)} %bitcast.34, bf16[16,16,128]{2,1,0:T(8,128)(2,1)S(1)} %get-tuple-element.76.refs_0_, ...), custom_call_target="tpu_custom_call" | custom-call | tf_op jit(solution)/shard_map/backward/pallas_call | solution.py:165
  78.1 6.2 %forward.7 = (f32[32,16,128]{2,1,0:T(8,128)S(1)}, f32[16,16,128]{2,1,0:T(8,128)S(1)}, bf16[16,16,128]{2,1,0:T(8,128)(2,1)S(1)}, bf16[16,16,128]{2,1,0:T(8,128)(2...) custom-call(s32[1]{0:T(128)} %bitcast.1.groups, ...), custom_call_target="tpu_custom_call" | custom-call | tf_op jit(solution)/shard_map/forward/pallas_call | solution.py:166
  84.4 3.4 %collective-permute-start.25 = (bf16[16,16,128]{2,1,0:T(8,128)(2,1)S(1)}, bf16[16,16,128]{2,1,0:T(8,128)(2,1)S(1)}, u32[]{:S(2)}, u32[]{:S(2)}) collective-permute-start(bf16[16,16,128]{2,1,0:T(8,128)(2,1)S(1)} %get-tuple-element.81), channel_id=1, source_target_pairs={{0,6},{2,4},{4,2},{6,0},{8,14},{10,12},{12,10},{14,8},{1,7},{3,5},... | collective-permute-start | bytes 196616 | tf_op jit(solution)/shard_map/ppermute | solution.py:116
  87.8 2.4 collective-permute-start.27
  90.3 3.4 %collective-permute-start.29 = (bf16[16,16,128]{2,1,0:T(8,128)(2,1)S(1)}, bf16[16,16,128]{2,1,0:T(8,128)(2,1)S(1)}, u32[]{:S(2)}, u32[]{:S(2)}) collective-permute-start(bf16[16,16,128]{2,1,0:T(8,128)(2,1)S(1)} %get-tuple-element.85), channel_id=1, source_target_pairs={{0,14},{2,12},{4,10},{6,8},{8,6},{10,4},{12,2},{14,0},{1,15},{3,13... | collective-permute-start | bytes 196616 | tf_op jit(solution)/shard_map/ppermute | solution.py:116
  93.8 2.2 collective-permute-done.27.refs_5_
  96.0 3.9 %collective-permute-done.28.refs_6_ = bf16[16,16,128]{2,1,0:T(8,128)(2,1)S(1)} collective-permute-done((bf16[16,16,128]{2,1,0:T(8,128)(2,1)S(1)}, bf16[16,16,128]{2,1,0:T(8,128)(2,1)S(1)}, u32[]{:S(2)}, u32[]{:S(2)}) %collective-permute-start.28) | collective-permute-done | bytes 65568 | tf_op jit(solution)/shard_map/ppermute | solution.py:116
  101.0 1.8 collective-permute-start.36
  106.9 2.5 collective-permute-start.32
  113.2 1.8 collective-permute-done.31.refs_2_
  116.5 3.8 %backward.8.own = f32[32,16,128]{2,1,0:T(8,128)S(1)} custom-call(s32[1]{0:T(128)} %bitcast.1.groups, s32[256]{0:T(256)S(1)} %bitcast.63, s32[256]{0:T(256)S(1)} %fusion.dst, bf16[256,128,128]{2,1,0:T(8,128)(2,1)S(1)} %bitcast.36, bf16[16,16,128]{2,1,0:T(8,128)(2,1)S(1)} %get-tuple-element.87.refs_0_, ...), custom_call_target="tpu_custom_call" | custom-call | tf_op jit(solution)/shard_map/backward/pallas_call | solution.py:165
  121.9 6.2 %forward.8 = (f32[32,16,128]{2,1,0:T(8,128)S(1)}, f32[16,16,128]{2,1,0:T(8,128)S(1)}, bf16[16,16,128]{2,1,0:T(8,128)(2,1)S(1)}, bf16[16,16,128]{2,1,0:T(8,128)(2...) custom-call(s32[1]{0:T(128)} %bitcast.1.groups, ...), custom_call_target="tpu_custom_call" | custom-call | tf_op jit(solution)/shard_map/forward/pallas_call | solution.py:166
  128.2 3.4 %collective-permute-start.40 = (bf16[16,16,128]{2,1,0:T(8,128)(2,1)S(1)}, bf16[16,16,128]{2,1,0:T(8,128)(2,1)S(1)}, u32[]{:S(2)}, u32[]{:S(2)}) collective-permute-start(bf16[16,16,128]{2,1,0:T(8,128)(2,1)S(1)} %get-tuple-element.92), channel_id=1, source_target_pairs={{0,6},{2,4},{4,2},{6,0},{8,14},{10,12},{12,10},{14,8},{1,7},{3,5},... | collective-permute-start | bytes 196616 | tf_op jit(solution)/shard_map/ppermute | solution.py:116
  131.6 2.4 collective-permute-start.42
  134.1 3.4 %collective-permute-start.44 = (bf16[16,16,128]{2,1,0:T(8,128)(2,1)S(1)}, bf16[16,16,128]{2,1,0:T(8,128)(2,1)S(1)}, u32[]{:S(2)}, u32[]{:S(2)}) collective-permute-start(bf16[16,16,128]{2,1,0:T(8,128)(2,1)S(1)} %get-tuple-element.96), channel_id=1, source_target_pairs={{0,14},{2,12},{4,10},{6,8},{8,6},{10,4},{12,2},{14,0},{1,15},{3,13... | collective-permute-start | bytes 196616 | tf_op jit(solution)/shard_map/ppermute | solution.py:116
  137.6 2.2 collective-permute-done.42.refs_5_
  139.8 3.9 %collective-permute-done.43.refs_6_ = bf16[16,16,128]{2,1,0:T(8,128)(2,1)S(1)} collective-permute-done((bf16[16,16,128]{2,1,0:T(8,128)(2,1)S(1)}, bf16[16,16,128]{2,1,0:T(8,128)(2,1)S(1)}, u32[]{:S(2)}, u32[]{:S(2)}) %collective-permute-start.43) | collective-permute-done | bytes 65568 | tf_op jit(solution)/shard_map/ppermute | solution.py:116
  144.7 1.8 collective-permute-start.51
  150.7 2.5 collective-permute-start.47
  157.0 1.8 collective-permute-done.46.refs_2_
  160.3 3.8 %backward.9.own = f32[32,16,128]{2,1,0:T(8,128)S(1)} custom-call(s32[1]{0:T(128)} %bitcast.1.groups, s32[256]{0:T(256)S(1)} %bitcast.64, s32[256]{0:T(256)S(1)} %fusion.dst, bf16[256,128,128]{2,1,0:T(8,128)(2,1)S(1)} %bitcast.38, bf16[16,16,128]{2,1,0:T(8,128)(2,1)S(1)} %get-tuple-element.98.refs_0_, ...), custom_call_target="tpu_custom_call" | custom-call | tf_op jit(solution)/shard_map/backward/pallas_call | solution.py:165
  165.7 6.2 %forward.9 = (f32[32,16,128]{2,1,0:T(8,128)S(1)}, f32[16,16,128]{2,1,0:T(8,128)S(1)}, bf16[16,16,128]{2,1,0:T(8,128)(2,1)S(1)}, bf16[16,16,128]{2,1,0:T(8,128)(2...) custom-call(s32[1]{0:T(128)} %bitcast.1.groups, ...), custom_call_target="tpu_custom_call" | custom-call | tf_op jit(solution)/shard_map/forward/pallas_call | solution.py:166
  172.0 3.4 %collective-permute-start.55 = (bf16[16,16,128]{2,1,0:T(8,128)(2,1)S(1)}, bf16[16,16,128]{2,1,0:T(8,128)(2,1)S(1)}, u32[]{:S(2)}, u32[]{:S(2)}) collective-permute-start(bf16[16,16,128]{2,1,0:T(8,128)(2,1)S(1)} %get-tuple-element.103), channel_id=1, source_target_pairs={{0,6},{2,4},{4,2},{6,0},{8,14},{10,12},{12,10},{14,8},{1,7},{3,5},... | collective-permute-start | bytes 196616 | tf_op jit(solution)/shard_map/ppermute | solution.py:116
  175.4 2.4 collective-permute-start.57
  177.9 3.4 %collective-permute-start.59 = (bf16[16,16,128]{2,1,0:T(8,128)(2,1)S(1)}, bf16[16,16,128]{2,1,0:T(8,128)(2,1)S(1)}, u32[]{:S(2)}, u32[]{:S(2)}) collective-permute-start(bf16[16,16,128]{2,1,0:T(8,128)(2,1)S(1)} %get-tuple-element.107), channel_id=1, source_target_pairs={{0,14},{2,12},{4,10},{6,8},{8,6},{10,4},{12,2},{14,0},{1,15},{3,13... | collective-permute-start | bytes 196616 | tf_op jit(solution)/shard_map/ppermute | solution.py:116
  181.4 2.2 collective-permute-done.57.refs_5_
  183.6 3.9 %collective-permute-done.58.refs_6_ = bf16[16,16,128]{2,1,0:T(8,128)(2,1)S(1)} collective-permute-done((bf16[16,16,128]{2,1,0:T(8,128)(2,1)S(1)}, bf16[16,16,128]{2,1,0:T(8,128)(2,1)S(1)}, u32[]{:S(2)}, u32[]{:S(2)}) %collective-permute-start.58) | collective-permute-done | bytes 65568 | tf_op jit(solution)/shard_map/ppermute | solution.py:116
  188.6 1.8 collective-permute-start.66
  194.5 2.5 collective-permute-start.62
  200.8 1.8 collective-permute-done.61.refs_2_
  204.1 3.8 %backward.10.own = f32[32,16,128]{2,1,0:T(8,128)S(1)} custom-call(s32[1]{0:T(128)} %bitcast.1.groups, s32[256]{0:T(256)S(1)} %bitcast.65, s32[256]{0:T(256)S(1)} %fusion.dst, bf16[256,128,128]{2,1,0:T(8,128)(2,1)S(1)} %bitcast.40, bf16[16,16,128]{2,1,0:T(8,128)(2,1)S(1)} %get-tuple-element.109.refs_0_, ...), custom_call_target="tpu_custom_call" | custom-call | tf_op jit(solution)/shard_map/backward/pallas_call | solution.py:165
  209.5 6.3 %forward.10 = (f32[32,16,128]{2,1,0:T(8,128)S(1)}, f32[16,16,128]{2,1,0:T(8,128)S(1)}, bf16[16,16,128]{2,1,0:T(8,128)(2,1)S(1)}, bf16[16,16,128]{2,1,0:T(8,128)(...) custom-call(s32[1]{0:T(128)} %bitcast.1.groups, ...), custom_call_target="tpu_custom_call" | custom-call | tf_op jit(solution)/shard_map/forward/pallas_call | solution.py:166
  216.0 3.4 %collective-permute-start.70 = (bf16[16,16,128]{2,1,0:T(8,128)(2,1)S(1)}, bf16[16,16,128]{2,1,0:T(8,128)(2,1)S(1)}, u32[]{:S(2)}, u32[]{:S(2)}) collective-permute-start(bf16[16,16,128]{2,1,0:T(8,128)(2,1)S(1)} %get-tuple-element.114), channel_id=1, source_target_pairs={{0,6},{2,4},{4,2},{6,0},{8,14},{10,12},{12,10},{14,8},{1,7},{3,5},... | collective-permute-start | bytes 196616 | tf_op jit(solution)/shard_map/ppermute | solution.py:116
  219.4 2.4 collective-permute-start.72
  221.8 3.4 %collective-permute-start.74 = (bf16[16,16,128]{2,1,0:T(8,128)(2,1)S(1)}, bf16[16,16,128]{2,1,0:T(8,128)(2,1)S(1)}, u32[]{:S(2)}, u32[]{:S(2)}) collective-permute-start(bf16[16,16,128]{2,1,0:T(8,128)(2,1)S(1)} %get-tuple-element.118), channel_id=1, source_target_pairs={{0,14},{2,12},{4,10},{6,8},{8,6},{10,4},{12,2},{14,0},{1,15},{3,13... | collective-permute-start | bytes 196616 | tf_op jit(solution)/shard_map/ppermute | solution.py:116
  225.3 2.2 collective-permute-done.72.refs_5_
  227.6 3.9 %collective-permute-done.73.refs_6_ = bf16[16,16,128]{2,1,0:T(8,128)(2,1)S(1)} collective-permute-done((bf16[16,16,128]{2,1,0:T(8,128)(2,1)S(1)}, bf16[16,16,128]{2,1,0:T(8,128)(2,1)S(1)}, u32[]{:S(2)}, u32[]{:S(2)}) %collective-permute-start.73) | collective-permute-done | bytes 65568 | tf_op jit(solution)/shard_map/ppermute | solution.py:116
  232.5 1.8 collective-permute-start.81
  238.4 2.5 collective-permute-start.77
  244.8 1.8 collective-permute-done.76.refs_2_
  248.0 3.8 %backward.11.own = f32[32,16,128]{2,1,0:T(8,128)S(1)} custom-call(s32[1]{0:T(128)} %bitcast.1.groups, s32[256]{0:T(256)S(1)} %bitcast.66, s32[256]{0:T(256)S(1)} %fusion.dst, bf16[256,128,128]{2,1,0:T(8,128)(2,1)S(1)} %bitcast.42, bf16[16,16,128]{2,1,0:T(8,128)(2,1)S(1)} %get-tuple-element.119.refs_0_, ...), custom_call_target="tpu_custom_call" | custom-call | tf_op jit(solution)/shard_map/backward/pallas_call | solution.py:165
  253.4 6.2 %forward.11 = (f32[32,16,128]{2,1,0:T(8,128)S(1)}, f32[16,16,128]{2,1,0:T(8,128)S(1)}, bf16[16,16,128]{2,1,0:T(8,128)(2,1)S(1)}, bf16[16,16,128]{2,1,0:T(8,128)(...) custom-call(s32[1]{0:T(128)} %bitcast.1.groups, ...), custom_call_target="tpu_custom_call" | custom-call | tf_op jit(solution)/shard_map/forward/pallas_call | solution.py:166
  259.8 3.4 %collective-permute-start.85 = (bf16[16,16,128]{2,1,0:T(8,128)(2,1)S(1)}, bf16[16,16,128]{2,1,0:T(8,128)(2,1)S(1)}, u32[]{:S(2)}, u32[]{:S(2)}) collective-permute-start(bf16[16,16,128]{2,1,0:T(8,128)(2,1)S(1)} %get-tuple-element.126), channel_id=1, source_target_pairs={{0,6},{2,4},{4,2},{6,0},{8,14},{10,12},{12,10},{14,8},{1,7},{3,5},... | collective-permute-start | bytes 196616 | tf_op jit(solution)/shard_map/ppermute | solution.py:116
  263.2 2.4 collective-permute-start.87
  265.6 3.4 %collective-permute-start.89 = (bf16[16,16,128]{2,1,0:T(8,128)(2,1)S(1)}, bf16[16,16,128]{2,1,0:T(8,128)(2,1)S(1)}, u32[]{:S(2)}, u32[]{:S(2)}) collective-permute-start(bf16[16,16,128]{2,1,0:T(8,128)(2,1)S(1)} %get-tuple-element.130), channel_id=1, source_target_pairs={{0,14},{2,12},{4,10},{6,8},{8,6},{10,4},{12,2},{14,0},{1,15},{3,13... | collective-permute-start | bytes 196616 | tf_op jit(solution)/shard_map/ppermute | solution.py:116
  271.4 3.9 %collective-permute-done.88.refs_6_ = bf16[16,16,128]{2,1,0:T(8,128)(2,1)S(1)} collective-permute-done((bf16[16,16,128]{2,1,0:T(8,128)(2,1)S(1)}, bf16[16,16,128]{2,1,0:T(8,128)(2,1)S(1)}, u32[]{:S(2)}, u32[]{:S(2)}) %collective-permute-start.88) | collective-permute-done | bytes 65568 | tf_op jit(solution)/shard_map/ppermute | solution.py:116
  (159 shorter events, 74.7 us)
Async XLA Ops:
  1.6 17.1 %collective-permute-start.6 = (bf16[16,16,128]{2,1,0:T(8,128)(2,1)S(1)}, bf16[16,16,128]{2,1,0:T(8,128)(2,1)S(1)}, u32[]{:S(2)}, u32[]{:S(2)}) collective-permute-start(bf16[16,16,128]{2,1,0:T(8,128)(2,1)S(1)} %bitcast.51), channel_id=1, source_target_pairs={{0,14},{2,12},{4,10},{6,8},{8,6},{10,4},{12,2},{14,0},{1,15},{3,13... | collective-permute-start | bytes 196616 | tf_op jit(solution)/shard_map/ppermute | solution.py:116
  4.2 15.8 %collective-permute-start.5 = (bf16[16,16,128]{2,1,0:T(8,128)(2,1)S(1)}, bf16[16,16,128]{2,1,0:T(8,128)(2,1)S(1)}, u32[]{:S(2)}, u32[]{:S(2)}) collective-permute-start(bf16[16,16,128]{2,1,0:T(8,128)(2,1)S(1)} %bitcast.52), channel_id=1, source_target_pairs={{0,12},{2,14},{4,8},{6,10},{8,4},{10,6},{12,0},{14,2},{1,13},{3,15... | collective-permute-start | bytes 196616 | tf_op jit(solution)/shard_map/ppermute | solution.py:116
  4.6 17.9 %collective-permute-start.4 = (bf16[16,16,128]{2,1,0:T(8,128)(2,1)S(1)}, bf16[16,16,128]{2,1,0:T(8,128)(2,1)S(1)}, u32[]{:S(2)}, u32[]{:S(2)}) collective-permute-start(bf16[16,16,128]{2,1,0:T(8,128)(2,1)S(1)} %bitcast.53), channel_id=1, source_target_pairs={{0,10},{2,8},{4,14},{6,12},{8,2},{10,0},{12,6},{14,4},{1,11},{3,9}... | collective-permute-start | bytes 196616 | tf_op jit(solution)/shard_map/ppermute | solution.py:116
  9.0 13.6 %collective-permute-start.3 = (bf16[16,16,128]{2,1,0:T(8,128)(2,1)S(1)}, bf16[16,16,128]{2,1,0:T(8,128)(2,1)S(1)}, u32[]{:S(2)}, u32[]{:S(2)}) collective-permute-start(bf16[16,16,128]{2,1,0:T(8,128)(2,1)S(1)} %bitcast.54), channel_id=1, source_target_pairs={{0,8},{2,10},{4,12},{6,14},{8,0},{10,2},{12,4},{14,6},{1,9},{3,11}... | collective-permute-start | bytes 196616 | tf_op jit(solution)/shard_map/ppermute | solution.py:116
  9.0 13.5 %collective-permute-start.2 = (bf16[16,16,128]{2,1,0:T(8,128)(2,1)S(1)}, bf16[16,16,128]{2,1,0:T(8,128)(2,1)S(1)}, u32[]{:S(2)}, u32[]{:S(2)}) collective-permute-start(bf16[16,16,128]{2,1,0:T(8,128)(2,1)S(1)} %bitcast.55), channel_id=1, source_target_pairs={{0,6},{2,4},{4,2},{6,0},{8,14},{10,12},{12,10},{14,8},{1,7},{3,5},... | collective-permute-start | bytes 196616 | tf_op jit(solution)/shard_map/ppermute | solution.py:116
  39.9 6.0 %collective-permute-start.8 = (bf16[16,16,128]{2,1,0:T(8,128)(2,1)S(1)}, bf16[16,16,128]{2,1,0:T(8,128)(2,1)S(1)}, u32[]{:S(2)}, u32[]{:S(2)}) collective-permute-start(bf16[16,16,128]{2,1,0:T(8,128)(2,1)S(1)} %get-tuple-element.68), channel_id=1, source_target_pairs={{0,2},{2,0},{4,6},{6,4},{8,10},{10,8},{12,14},{14,12},{1,3},{3,1},... | collective-permute-start | bytes 196616 | tf_op jit(solution)/shard_map/ppermute | solution.py:116
  40.0 9.4 %collective-permute-start.10 = (bf16[16,16,128]{2,1,0:T(8,128)(2,1)S(1)}, bf16[16,16,128]{2,1,0:T(8,128)(2,1)S(1)}, u32[]{:S(2)}, u32[]{:S(2)}) collective-permute-start(bf16[16,16,128]{2,1,0:T(8,128)(2,1)S(1)} %get-tuple-element.70), channel_id=1, source_target_pairs={{0,6},{2,4},{4,2},{6,0},{8,14},{10,12},{12,10},{14,8},{1,7},{3,5},... | collective-permute-start | bytes 196616 | tf_op jit(solution)/shard_map/ppermute | solution.py:116
  43.4 6.0 %collective-permute-start.11 = (bf16[16,16,128]{2,1,0:T(8,128)(2,1)S(1)}, bf16[16,16,128]{2,1,0:T(8,128)(2,1)S(1)}, u32[]{:S(2)}, u32[]{:S(2)}) collective-permute-start(bf16[16,16,128]{2,1,0:T(8,128)(2,1)S(1)} %get-tuple-element.71), channel_id=1, source_target_pairs={{0,8},{2,10},{4,12},{6,14},{8,0},{10,2},{12,4},{14,6},{1,9},{3,11}... | collective-permute-start | bytes 196616 | tf_op jit(solution)/shard_map/ppermute | solution.py:116
  43.4 8.1 %collective-permute-start.12 = (bf16[16,16,128]{2,1,0:T(8,128)(2,1)S(1)}, bf16[16,16,128]{2,1,0:T(8,128)(2,1)S(1)}, u32[]{:S(2)}, u32[]{:S(2)}) collective-permute-start(bf16[16,16,128]{2,1,0:T(8,128)(2,1)S(1)} %get-tuple-element.72), channel_id=1, source_target_pairs={{0,10},{2,8},{4,14},{6,12},{8,2},{10,0},{12,6},{14,4},{1,11},{3,9}... | collective-permute-start | bytes 196616 | tf_op jit(solution)/shard_map/ppermute | solution.py:116
  45.9 10.4 %collective-permute-start.13 = (bf16[16,16,128]{2,1,0:T(8,128)(2,1)S(1)}, bf16[16,16,128]{2,1,0:T(8,128)(2,1)S(1)}, u32[]{:S(2)}, u32[]{:S(2)}) collective-permute-start(bf16[16,16,128]{2,1,0:T(8,128)(2,1)S(1)} %get-tuple-element.73), channel_id=1, source_target_pairs={{0,12},{2,14},{4,8},{6,10},{8,4},{10,6},{12,0},{14,2},{1,13},{3,15... | collective-permute-start | bytes 196616 | tf_op jit(solution)/shard_map/ppermute | solution.py:116
  45.9 10.9 %collective-permute-start.14 = (bf16[16,16,128]{2,1,0:T(8,128)(2,1)S(1)}, bf16[16,16,128]{2,1,0:T(8,128)(2,1)S(1)}, u32[]{:S(2)}, u32[]{:S(2)}) collective-permute-start(bf16[16,16,128]{2,1,0:T(8,128)(2,1)S(1)} %get-tuple-element.74), channel_id=1, source_target_pairs={{0,14},{2,12},{4,10},{6,8},{8,6},{10,4},{12,2},{14,0},{1,15},{3,13... | collective-permute-start | bytes 196616 | tf_op jit(solution)/shard_map/ppermute | solution.py:116
  56.8 10.1 %collective-permute-start.21 = (bf16[16,16,128]{2,1,0:T(8,128)(2,1)S(1)}, bf16[16,16,128]{2,1,0:T(8,128)(2,1)S(1)}, u32[]{:S(2)}, u32[]{:S(2)}) collective-permute-start(bf16[16,16,128]{2,1,0:T(8,128)(2,1)S(1)} %get-tuple-element.76.refs_0_), channel_id=1, source_target_pairs={{0,14},{2,12},{4,10},{6,8},{8,6},{10,4},{12,2},{14,0},{1,15},{3,13... | collective-permute-start | bytes 196616 | tf_op jit(solution)/shard_map/ppermute | solution.py:116
  58.4 10.0 %collective-permute-start.20 = (bf16[16,16,128]{2,1,0:T(8,128)(2,1)S(1)}, bf16[16,16,128]{2,1,0:T(8,128)(2,1)S(1)}, u32[]{:S(2)}, u32[]{:S(2)}) collective-permute-start(bf16[16,16,128]{2,1,0:T(8,128)(2,1)S(1)} %get-tuple-element.76.refs_0_), channel_id=1, source_target_pairs={{0,12},{2,14},{4,8},{6,10},{8,4},{10,6},{12,0},{14,2},{1,13},{3,15... | collective-permute-start | bytes 196616 | tf_op jit(solution)/shard_map/ppermute | solution.py:116
  60.0 9.3 %collective-permute-start.19 = (bf16[16,16,128]{2,1,0:T(8,128)(2,1)S(1)}, bf16[16,16,128]{2,1,0:T(8,128)(2,1)S(1)}, u32[]{:S(2)}, u32[]{:S(2)}) collective-permute-start(bf16[16,16,128]{2,1,0:T(8,128)(2,1)S(1)} %get-tuple-element.76.refs_0_), channel_id=1, source_target_pairs={{0,10},{2,8},{4,14},{6,12},{8,2},{10,0},{12,6},{14,4},{1,11},{3,9}... | collective-permute-start | bytes 196616 | tf_op jit(solution)/shard_map/ppermute | solution.py:116
  61.2 8.1 %collective-permute-start.18 = (bf16[16,16,128]{2,1,0:T(8,128)(2,1)S(1)}, bf16[16,16,128]{2,1,0:T(8,128)(2,1)S(1)}, u32[]{:S(2)}, u32[]{:S(2)}) collective-permute-start(bf16[16,16,128]{2,1,0:T(8,128)(2,1)S(1)} %get-tuple-element.76.refs_0_), channel_id=1, source_target_pairs={{0,8},{2,10},{4,12},{6,14},{8,0},{10,2},{12,4},{14,6},{1,9},{3,11}... | collective-permute-start | bytes 196616 | tf_op jit(solution)/shard_map/ppermute | solution.py:116
  62.7 6.6 %collective-permute-start.17 = (bf16[16,16,128]{2,1,0:T(8,128)(2,1)S(1)}, bf16[16,16,128]{2,1,0:T(8,128)(2,1)S(1)}, u32[]{:S(2)}, u32[]{:S(2)}) collective-permute-start(bf16[16,16,128]{2,1,0:T(8,128)(2,1)S(1)} %get-tuple-element.76.refs_0_), channel_id=1, source_target_pairs={{0,6},{2,4},{4,2},{6,0},{8,14},{10,12},{12,10},{14,8},{1,7},{3,5},... | collective-permute-start | bytes 196616 | tf_op jit(solution)/shard_map/ppermute | solution.py:116
  84.3 6.0 %collective-permute-start.23 = (bf16[16,16,128]{2,1,0:T(8,128)(2,1)S(1)}, bf16[16,16,128]{2,1,0:T(8,128)(2,1)S(1)}, u32[]{:S(2)}, u32[]{:S(2)}) collective-permute-start(bf16[16,16,128]{2,1,0:T(8,128)(2,1)S(1)} %get-tuple-element.79), channel_id=1, source_target_pairs={{0,2},{2,0},{4,6},{6,4},{8,10},{10,8},{12,14},{14,12},{1,3},{3,1},... | collective-permute-start | bytes 196616 | tf_op jit(solution)/shard_map/ppermute | solution.py:116
  84.4 9.3 %collective-permute-start.25 = (bf16[16,16,128]{2,1,0:T(8,128)(2,1)S(1)}, bf16[16,16,128]{2,1,0:T(8,128)(2,1)S(1)}, u32[]{:S(2)}, u32[]{:S(2)}) collective-permute-start(bf16[16,16,128]{2,1,0:T(8,128)(2,1)S(1)} %get-tuple-element.81), channel_id=1, source_target_pairs={{0,6},{2,4},{4,2},{6,0},{8,14},{10,12},{12,10},{14,8},{1,7},{3,5},... | collective-permute-start | bytes 196616 | tf_op jit(solution)/shard_map/ppermute | solution.py:116
  87.8 5.9 %collective-permute-start.26 = (bf16[16,16,128]{2,1,0:T(8,128)(2,1)S(1)}, bf16[16,16,128]{2,1,0:T(8,128)(2,1)S(1)}, u32[]{:S(2)}, u32[]{:S(2)}) collective-permute-start(bf16[16,16,128]{2,1,0:T(8,128)(2,1)S(1)} %get-tuple-element.82), channel_id=1, source_target_pairs={{0,8},{2,10},{4,12},{6,14},{8,0},{10,2},{12,4},{14,6},{1,9},{3,11}... | collective-permute-start | bytes 196616 | tf_op jit(solution)/shard_map/ppermute | solution.py:116
  87.8 8.2 %collective-permute-start.27 = (bf16[16,16,128]{2,1,0:T(8,128)(2,1)S(1)}, bf16[16,16,128]{2,1,0:T(8,128)(2,1)S(1)}, u32[]{:S(2)}, u32[]{:S(2)}) collective-permute-start(bf16[16,16,128]{2,1,0:T(8,128)(2,1)S(1)} %get-tuple-element.83), channel_id=1, source_target_pairs={{0,10},{2,8},{4,14},{6,12},{8,2},{10,0},{12,6},{14,4},{1,11},{3,9}... | collective-permute-start | bytes 196616 | tf_op jit(solution)/shard_map/ppermute | solution.py:116
  90.3 9.7 %collective-permute-start.28 = (bf16[16,16,128]{2,1,0:T(8,128)(2,1)S(1)}, bf16[16,16,128]{2,1,0:T(8,128)(2,1)S(1)}, u32[]{:S(2)}, u32[]{:S(2)}) collective-permute-start(bf16[16,16,128]{2,1,0:T(8,128)(2,1)S(1)} %get-tuple-element.84), channel_id=1, source_target_pairs={{0,12},{2,14},{4,8},{6,10},{8,4},{10,6},{12,0},{14,2},{1,13},{3,15... | collective-permute-start | bytes 196616 | tf_op jit(solution)/shard_map/ppermute | solution.py:116
  90.3 10.6 %collective-permute-start.29 = (bf16[16,16,128]{2,1,0:T(8,128)(2,1)S(1)}, bf16[16,16,128]{2,1,0:T(8,128)(2,1)S(1)}, u32[]{:S(2)}, u32[]{:S(2)}) collective-permute-start(bf16[16,16,128]{2,1,0:T(8,128)(2,1)S(1)} %get-tuple-element.85), channel_id=1, source_target_pairs={{0,14},{2,12},{4,10},{6,8},{8,6},{10,4},{12,2},{14,0},{1,15},{3,13... | collective-permute-start | bytes 196616 | tf_op jit(solution)/shard_map/ppermute | solution.py:116
  101.0 9.9 %collective-permute-start.36 = (bf16[16,16,128]{2,1,0:T(8,128)(2,1)S(1)}, bf16[16,16,128]{2,1,0:T(8,128)(2,1)S(1)}, u32[]{:S(2)}, u32[]{:S(2)}) collective-permute-start(bf16[16,16,128]{2,1,0:T(8,128)(2,1)S(1)} %get-tuple-element.87.refs_0_), channel_id=1, source_target_pairs={{0,14},{2,12},{4,10},{6,8},{8,6},{10,4},{12,2},{14,0},{1,15},{3,13... | collective-permute-start | bytes 196616 | tf_op jit(solution)/shard_map/ppermute | solution.py:116
  102.7 9.5 %collective-permute-start.35 = (bf16[16,16,128]{2,1,0:T(8,128)(2,1)S(1)}, bf16[16,16,128]{2,1,0:T(8,128)(2,1)S(1)}, u32[]{:S(2)}, u32[]{:S(2)}) collective-permute-start(bf16[16,16,128]{2,1,0:T(8,128)(2,1)S(1)} %get-tuple-element.87.refs_0_), channel_id=1, source_target_pairs={{0,12},{2,14},{4,8},{6,10},{8,4},{10,6},{12,0},{14,2},{1,13},{3,15... | collective-permute-start | bytes 196616 | tf_op jit(solution)/shard_map/ppermute | solution.py:116
  103.7 9.3 %collective-permute-start.34 = (bf16[16,16,128]{2,1,0:T(8,128)(2,1)S(1)}, bf16[16,16,128]{2,1,0:T(8,128)(2,1)S(1)}, u32[]{:S(2)}, u32[]{:S(2)}) collective-permute-start(bf16[16,16,128]{2,1,0:T(8,128)(2,1)S(1)} %get-tuple-element.87.refs_0_), channel_id=1, source_target_pairs={{0,10},{2,8},{4,14},{6,12},{8,2},{10,0},{12,6},{14,4},{1,11},{3,9}... | collective-permute-start | bytes 196616 | tf_op jit(solution)/shard_map/ppermute | solution.py:116
  105.4 7.7 %collective-permute-start.33 = (bf16[16,16,128]{2,1,0:T(8,128)(2,1)S(1)}, bf16[16,16,128]{2,1,0:T(8,128)(2,1)S(1)}, u32[]{:S(2)}, u32[]{:S(2)}) collective-permute-start(bf16[16,16,128]{2,1,0:T(8,128)(2,1)S(1)} %get-tuple-element.87.refs_0_), channel_id=1, source_target_pairs={{0,8},{2,10},{4,12},{6,14},{8,0},{10,2},{12,4},{14,6},{1,9},{3,11}... | collective-permute-start | bytes 196616 | tf_op jit(solution)/shard_map/ppermute | solution.py:116
  106.9 6.4 %collective-permute-start.32 = (bf16[16,16,128]{2,1,0:T(8,128)(2,1)S(1)}, bf16[16,16,128]{2,1,0:T(8,128)(2,1)S(1)}, u32[]{:S(2)}, u32[]{:S(2)}) collective-permute-start(bf16[16,16,128]{2,1,0:T(8,128)(2,1)S(1)} %get-tuple-element.87.refs_0_), channel_id=1, source_target_pairs={{0,6},{2,4},{4,2},{6,0},{8,14},{10,12},{12,10},{14,8},{1,7},{3,5},... | collective-permute-start | bytes 196616 | tf_op jit(solution)/shard_map/ppermute | solution.py:116
  128.1 6.0 %collective-permute-start.38 = (bf16[16,16,128]{2,1,0:T(8,128)(2,1)S(1)}, bf16[16,16,128]{2,1,0:T(8,128)(2,1)S(1)}, u32[]{:S(2)}, u32[]{:S(2)}) collective-permute-start(bf16[16,16,128]{2,1,0:T(8,128)(2,1)S(1)} %get-tuple-element.90), channel_id=1, source_target_pairs={{0,2},{2,0},{4,6},{6,4},{8,10},{10,8},{12,14},{14,12},{1,3},{3,1},... | collective-permute-start | bytes 196616 | tf_op jit(solution)/shard_map/ppermute | solution.py:116
  128.2 9.3 %collective-permute-start.40 = (bf16[16,16,128]{2,1,0:T(8,128)(2,1)S(1)}, bf16[16,16,128]{2,1,0:T(8,128)(2,1)S(1)}, u32[]{:S(2)}, u32[]{:S(2)}) collective-permute-start(bf16[16,16,128]{2,1,0:T(8,128)(2,1)S(1)} %get-tuple-element.92), channel_id=1, source_target_pairs={{0,6},{2,4},{4,2},{6,0},{8,14},{10,12},{12,10},{14,8},{1,7},{3,5},... | collective-permute-start | bytes 196616 | tf_op jit(solution)/shard_map/ppermute | solution.py:116
  131.6 8.2 %collective-permute-start.42 = (bf16[16,16,128]{2,1,0:T(8,128)(2,1)S(1)}, bf16[16,16,128]{2,1,0:T(8,128)(2,1)S(1)}, u32[]{:S(2)}, u32[]{:S(2)}) collective-permute-start(bf16[16,16,128]{2,1,0:T(8,128)(2,1)S(1)} %get-tuple-element.94), channel_id=1, source_target_pairs={{0,10},{2,8},{4,14},{6,12},{8,2},{10,0},{12,6},{14,4},{1,11},{3,9}... | collective-permute-start | bytes 196616 | tf_op jit(solution)/shard_map/ppermute | solution.py:116
  134.1 9.7 %collective-permute-start.43 = (bf16[16,16,128]{2,1,0:T(8,128)(2,1)S(1)}, bf16[16,16,128]{2,1,0:T(8,128)(2,1)S(1)}, u32[]{:S(2)}, u32[]{:S(2)}) collective-permute-start(bf16[16,16,128]{2,1,0:T(8,128)(2,1)S(1)} %get-tuple-element.95), channel_id=1, source_target_pairs={{0,12},{2,14},{4,8},{6,10},{8,4},{10,6},{12,0},{14,2},{1,13},{3,15... | collective-permute-start | bytes 196616 | tf_op jit(solution)/shard_map/ppermute | solution.py:116
  134.1 10.6 %collective-permute-start.44 = (bf16[16,16,128]{2,1,0:T(8,128)(2,1)S(1)}, bf16[16,16,128]{2,1,0:T(8,128)(2,1)S(1)}, u32[]{:S(2)}, u32[]{:S(2)}) collective-permute-start(bf16[16,16,128]{2,1,0:T(8,128)(2,1)S(1)} %get-tuple-element.96), channel_id=1, source_target_pairs={{0,14},{2,12},{4,10},{6,8},{8,6},{10,4},{12,2},{14,0},{1,15},{3,13... | collective-permute-start | bytes 196616 | tf_op jit(solution)/shard_map/ppermute | solution.py:116
  144.7 9.9 %collective-permute-start.51 = (bf16[16,16,128]{2,1,0:T(8,128)(2,1)S(1)}, bf16[16,16,128]{2,1,0:T(8,128)(2,1)S(1)}, u32[]{:S(2)}, u32[]{:S(2)}) collective-permute-start(bf16[16,16,128]{2,1,0:T(8,128)(2,1)S(1)} %get-tuple-element.98.refs_0_), channel_id=1, source_target_pairs={{0,14},{2,12},{4,10},{6,8},{8,6},{10,4},{12,2},{14,0},{1,15},{3,13... | collective-permute-start | bytes 196616 | tf_op jit(solution)/shard_map/ppermute | solution.py:116
  146.5 9.5 %collective-permute-start.50 = (bf16[16,16,128]{2,1,0:T(8,128)(2,1)S(1)}, bf16[16,16,128]{2,1,0:T(8,128)(2,1)S(1)}, u32[]{:S(2)}, u32[]{:S(2)}) collective-permute-start(bf16[16,16,128]{2,1,0:T(8,128)(2,1)S(1)} %get-tuple-element.98.refs_0_), channel_id=1, source_target_pairs={{0,12},{2,14},{4,8},{6,10},{8,4},{10,6},{12,0},{14,2},{1,13},{3,15... | collective-permute-start | bytes 196616 | tf_op jit(solution)/shard_map/ppermute | solution.py:116
  147.5 9.3 %collective-permute-start.49 = (bf16[16,16,128]{2,1,0:T(8,128)(2,1)S(1)}, bf16[16,16,128]{2,1,0:T(8,128)(2,1)S(1)}, u32[]{:S(2)}, u32[]{:S(2)}) collective-permute-start(bf16[16,16,128]{2,1,0:T(8,128)(2,1)S(1)} %get-tuple-element.98.refs_0_), channel_id=1, source_target_pairs={{0,10},{2,8},{4,14},{6,12},{8,2},{10,0},{12,6},{14,4},{1,11},{3,9}... | collective-permute-start | bytes 196616 | tf_op jit(solution)/shard_map/ppermute | solution.py:116
  149.2 7.7 %collective-permute-start.48 = (bf16[16,16,128]{2,1,0:T(8,128)(2,1)S(1)}, bf16[16,16,128]{2,1,0:T(8,128)(2,1)S(1)}, u32[]{:S(2)}, u32[]{:S(2)}) collective-permute-start(bf16[16,16,128]{2,1,0:T(8,128)(2,1)S(1)} %get-tuple-element.98.refs_0_), channel_id=1, source_target_pairs={{0,8},{2,10},{4,12},{6,14},{8,0},{10,2},{12,4},{14,6},{1,9},{3,11}... | collective-permute-start | bytes 196616 | tf_op jit(solution)/shard_map/ppermute | solution.py:116
  150.7 6.4 %collective-permute-start.47 = (bf16[16,16,128]{2,1,0:T(8,128)(2,1)S(1)}, bf16[16,16,128]{2,1,0:T(8,128)(2,1)S(1)}, u32[]{:S(2)}, u32[]{:S(2)}) collective-permute-start(bf16[16,16,128]{2,1,0:T(8,128)(2,1)S(1)} %get-tuple-element.98.refs_0_), channel_id=1, source_target_pairs={{0,6},{2,4},{4,2},{6,0},{8,14},{10,12},{12,10},{14,8},{1,7},{3,5},... | collective-permute-start | bytes 196616 | tf_op jit(solution)/shard_map/ppermute | solution.py:116
  171.9 6.0 %collective-permute-start.53 = (bf16[16,16,128]{2,1,0:T(8,128)(2,1)S(1)}, bf16[16,16,128]{2,1,0:T(8,128)(2,1)S(1)}, u32[]{:S(2)}, u32[]{:S(2)}) collective-permute-start(bf16[16,16,128]{2,1,0:T(8,128)(2,1)S(1)} %get-tuple-element.101), channel_id=1, source_target_pairs={{0,2},{2,0},{4,6},{6,4},{8,10},{10,8},{12,14},{14,12},{1,3},{3,1},... | collective-permute-start | bytes 196616 | tf_op jit(solution)/shard_map/ppermute | solution.py:116
  172.0 9.3 %collective-permute-start.55 = (bf16[16,16,128]{2,1,0:T(8,128)(2,1)S(1)}, bf16[16,16,128]{2,1,0:T(8,128)(2,1)S(1)}, u32[]{:S(2)}, u32[]{:S(2)}) collective-permute-start(bf16[16,16,128]{2,1,0:T(8,128)(2,1)S(1)} %get-tuple-element.103), channel_id=1, source_target_pairs={{0,6},{2,4},{4,2},{6,0},{8,14},{10,12},{12,10},{14,8},{1,7},{3,5},... | collective-permute-start | bytes 196616 | tf_op jit(solution)/shard_map/ppermute | solution.py:116
  175.4 8.2 %collective-permute-start.57 = (bf16[16,16,128]{2,1,0:T(8,128)(2,1)S(1)}, bf16[16,16,128]{2,1,0:T(8,128)(2,1)S(1)}, u32[]{:S(2)}, u32[]{:S(2)}) collective-permute-start(bf16[16,16,128]{2,1,0:T(8,128)(2,1)S(1)} %get-tuple-element.105), channel_id=1, source_target_pairs={{0,10},{2,8},{4,14},{6,12},{8,2},{10,0},{12,6},{14,4},{1,11},{3,9}... | collective-permute-start | bytes 196616 | tf_op jit(solution)/shard_map/ppermute | solution.py:116
  177.9 9.7 %collective-permute-start.58 = (bf16[16,16,128]{2,1,0:T(8,128)(2,1)S(1)}, bf16[16,16,128]{2,1,0:T(8,128)(2,1)S(1)}, u32[]{:S(2)}, u32[]{:S(2)}) collective-permute-start(bf16[16,16,128]{2,1,0:T(8,128)(2,1)S(1)} %get-tuple-element.106), channel_id=1, source_target_pairs={{0,12},{2,14},{4,8},{6,10},{8,4},{10,6},{12,0},{14,2},{1,13},{3,15... | collective-permute-start | bytes 196616 | tf_op jit(solution)/shard_map/ppermute | solution.py:116
  177.9 10.6 %collective-permute-start.59 = (bf16[16,16,128]{2,1,0:T(8,128)(2,1)S(1)}, bf16[16,16,128]{2,1,0:T(8,128)(2,1)S(1)}, u32[]{:S(2)}, u32[]{:S(2)}) collective-permute-start(bf16[16,16,128]{2,1,0:T(8,128)(2,1)S(1)} %get-tuple-element.107), channel_id=1, source_target_pairs={{0,14},{2,12},{4,10},{6,8},{8,6},{10,4},{12,2},{14,0},{1,15},{3,13... | collective-permute-start | bytes 196616 | tf_op jit(solution)/shard_map/ppermute | solution.py:116
  188.6 9.9 %collective-permute-start.66 = (bf16[16,16,128]{2,1,0:T(8,128)(2,1)S(1)}, bf16[16,16,128]{2,1,0:T(8,128)(2,1)S(1)}, u32[]{:S(2)}, u32[]{:S(2)}) collective-permute-start(bf16[16,16,128]{2,1,0:T(8,128)(2,1)S(1)} %get-tuple-element.109.refs_0_), channel_id=1, source_target_pairs={{0,14},{2,12},{4,10},{6,8},{8,6},{10,4},{12,2},{14,0},{1,15},{3,13... | collective-permute-start | bytes 196616 | tf_op jit(solution)/shard_map/ppermute | solution.py:116
  190.3 9.5 %collective-permute-start.65 = (bf16[16,16,128]{2,1,0:T(8,128)(2,1)S(1)}, bf16[16,16,128]{2,1,0:T(8,128)(2,1)S(1)}, u32[]{:S(2)}, u32[]{:S(2)}) collective-permute-start(bf16[16,16,128]{2,1,0:T(8,128)(2,1)S(1)} %get-tuple-element.109.refs_0_), channel_id=1, source_target_pairs={{0,12},{2,14},{4,8},{6,10},{8,4},{10,6},{12,0},{14,2},{1,13},{3,15... | collective-permute-start | bytes 196616 | tf_op jit(solution)/shard_map/ppermute | solution.py:116
  191.3 9.3 %collective-permute-start.64 = (bf16[16,16,128]{2,1,0:T(8,128)(2,1)S(1)}, bf16[16,16,128]{2,1,0:T(8,128)(2,1)S(1)}, u32[]{:S(2)}, u32[]{:S(2)}) collective-permute-start(bf16[16,16,128]{2,1,0:T(8,128)(2,1)S(1)} %get-tuple-element.109.refs_0_), channel_id=1, source_target_pairs={{0,10},{2,8},{4,14},{6,12},{8,2},{10,0},{12,6},{14,4},{1,11},{3,9}... | collective-permute-start | bytes 196616 | tf_op jit(solution)/shard_map/ppermute | solution.py:116
  193.0 7.7 %collective-permute-start.63 = (bf16[16,16,128]{2,1,0:T(8,128)(2,1)S(1)}, bf16[16,16,128]{2,1,0:T(8,128)(2,1)S(1)}, u32[]{:S(2)}, u32[]{:S(2)}) collective-permute-start(bf16[16,16,128]{2,1,0:T(8,128)(2,1)S(1)} %get-tuple-element.109.refs_0_), channel_id=1, source_target_pairs={{0,8},{2,10},{4,12},{6,14},{8,0},{10,2},{12,4},{14,6},{1,9},{3,11}... | collective-permute-start | bytes 196616 | tf_op jit(solution)/shard_map/ppermute | solution.py:116
  194.5 6.4 %collective-permute-start.62 = (bf16[16,16,128]{2,1,0:T(8,128)(2,1)S(1)}, bf16[16,16,128]{2,1,0:T(8,128)(2,1)S(1)}, u32[]{:S(2)}, u32[]{:S(2)}) collective-permute-start(bf16[16,16,128]{2,1,0:T(8,128)(2,1)S(1)} %get-tuple-element.109.refs_0_), channel_id=1, source_target_pairs={{0,6},{2,4},{4,2},{6,0},{8,14},{10,12},{12,10},{14,8},{1,7},{3,5},... | collective-permute-start | bytes 196616 | tf_op jit(solution)/shard_map/ppermute | solution.py:116
  215.8 6.0 %collective-permute-start.68 = (bf16[16,16,128]{2,1,0:T(8,128)(2,1)S(1)}, bf16[16,16,128]{2,1,0:T(8,128)(2,1)S(1)}, u32[]{:S(2)}, u32[]{:S(2)}) collective-permute-start(bf16[16,16,128]{2,1,0:T(8,128)(2,1)S(1)} %get-tuple-element.112), channel_id=1, source_target_pairs={{0,2},{2,0},{4,6},{6,4},{8,10},{10,8},{12,14},{14,12},{1,3},{3,1},... | collective-permute-start | bytes 196616 | tf_op jit(solution)/shard_map/ppermute | solution.py:116
  216.0 9.3 %collective-permute-start.70 = (bf16[16,16,128]{2,1,0:T(8,128)(2,1)S(1)}, bf16[16,16,128]{2,1,0:T(8,128)(2,1)S(1)}, u32[]{:S(2)}, u32[]{:S(2)}) collective-permute-start(bf16[16,16,128]{2,1,0:T(8,128)(2,1)S(1)} %get-tuple-element.114), channel_id=1, source_target_pairs={{0,6},{2,4},{4,2},{6,0},{8,14},{10,12},{12,10},{14,8},{1,7},{3,5},... | collective-permute-start | bytes 196616 | tf_op jit(solution)/shard_map/ppermute | solution.py:116
  219.4 5.9 %collective-permute-start.71 = (bf16[16,16,128]{2,1,0:T(8,128)(2,1)S(1)}, bf16[16,16,128]{2,1,0:T(8,128)(2,1)S(1)}, u32[]{:S(2)}, u32[]{:S(2)}) collective-permute-start(bf16[16,16,128]{2,1,0:T(8,128)(2,1)S(1)} %get-tuple-element.115), channel_id=1, source_target_pairs={{0,8},{2,10},{4,12},{6,14},{8,0},{10,2},{12,4},{14,6},{1,9},{3,11}... | collective-permute-start | bytes 196616 | tf_op jit(solution)/shard_map/ppermute | solution.py:116
  219.4 8.2 %collective-permute-start.72 = (bf16[16,16,128]{2,1,0:T(8,128)(2,1)S(1)}, bf16[16,16,128]{2,1,0:T(8,128)(2,1)S(1)}, u32[]{:S(2)}, u32[]{:S(2)}) collective-permute-start(bf16[16,16,128]{2,1,0:T(8,128)(2,1)S(1)} %get-tuple-element.116), channel_id=1, source_target_pairs={{0,10},{2,8},{4,14},{6,12},{8,2},{10,0},{12,6},{14,4},{1,11},{3,9}... | collective-permute-start | bytes 196616 | tf_op jit(solution)/shard_map/ppermute | solution.py:116
  221.8 9.7 %collective-permute-start.73 = (bf16[16,16,128]{2,1,0:T(8,128)(2,1)S(1)}, bf16[16,16,128]{2,1,0:T(8,128)(2,1)S(1)}, u32[]{:S(2)}, u32[]{:S(2)}) collective-permute-start(bf16[16,16,128]{2,1,0:T(8,128)(2,1)S(1)} %get-tuple-element.117), channel_id=1, source_target_pairs={{0,12},{2,14},{4,8},{6,10},{8,4},{10,6},{12,0},{14,2},{1,13},{3,15... | collective-permute-start | bytes 196616 | tf_op jit(solution)/shard_map/ppermute | solution.py:116
  221.8 10.6 %collective-permute-start.74 = (bf16[16,16,128]{2,1,0:T(8,128)(2,1)S(1)}, bf16[16,16,128]{2,1,0:T(8,128)(2,1)S(1)}, u32[]{:S(2)}, u32[]{:S(2)}) collective-permute-start(bf16[16,16,128]{2,1,0:T(8,128)(2,1)S(1)} %get-tuple-element.118), channel_id=1, source_target_pairs={{0,14},{2,12},{4,10},{6,8},{8,6},{10,4},{12,2},{14,0},{1,15},{3,13... | collective-permute-start | bytes 196616 | tf_op jit(solution)/shard_map/ppermute | solution.py:116
  232.5 9.9 %collective-permute-start.81 = (bf16[16,16,128]{2,1,0:T(8,128)(2,1)S(1)}, bf16[16,16,128]{2,1,0:T(8,128)(2,1)S(1)}, u32[]{:S(2)}, u32[]{:S(2)}) collective-permute-start(bf16[16,16,128]{2,1,0:T(8,128)(2,1)S(1)} %get-tuple-element.119.refs_0_), channel_id=1, source_target_pairs={{0,14},{2,12},{4,10},{6,8},{8,6},{10,4},{12,2},{14,0},{1,15},{3,13... | collective-permute-start | bytes 196616 | tf_op jit(solution)/shard_map/ppermute | solution.py:116
  234.2 9.5 %collective-permute-start.80 = (bf16[16,16,128]{2,1,0:T(8,128)(2,1)S(1)}, bf16[16,16,128]{2,1,0:T(8,128)(2,1)S(1)}, u32[]{:S(2)}, u32[]{:S(2)}) collective-permute-start(bf16[16,16,128]{2,1,0:T(8,128)(2,1)S(1)} %get-tuple-element.119.refs_0_), channel_id=1, source_target_pairs={{0,12},{2,14},{4,8},{6,10},{8,4},{10,6},{12,0},{14,2},{1,13},{3,15... | collective-permute-start | bytes 196616 | tf_op jit(solution)/shard_map/ppermute | solution.py:116
  235.3 9.3 %collective-permute-start.79 = (bf16[16,16,128]{2,1,0:T(8,128)(2,1)S(1)}, bf16[16,16,128]{2,1,0:T(8,128)(2,1)S(1)}, u32[]{:S(2)}, u32[]{:S(2)}) collective-permute-start(bf16[16,16,128]{2,1,0:T(8,128)(2,1)S(1)} %get-tuple-element.119.refs_0_), channel_id=1, source_target_pairs={{0,10},{2,8},{4,14},{6,12},{8,2},{10,0},{12,6},{14,4},{1,11},{3,9}... | collective-permute-start | bytes 196616 | tf_op jit(solution)/shard_map/ppermute | solution.py:116
  237.0 7.7 %collective-permute-start.78 = (bf16[16,16,128]{2,1,0:T(8,128)(2,1)S(1)}, bf16[16,16,128]{2,1,0:T(8,128)(2,1)S(1)}, u32[]{:S(2)}, u32[]{:S(2)}) collective-permute-start(bf16[16,16,128]{2,1,0:T(8,128)(2,1)S(1)} %get-tuple-element.119.refs_0_), channel_id=1, source_target_pairs={{0,8},{2,10},{4,12},{6,14},{8,0},{10,2},{12,4},{14,6},{1,9},{3,11}... | collective-permute-start | bytes 196616 | tf_op jit(solution)/shard_map/ppermute | solution.py:116
  238.4 6.4 %collective-permute-start.77 = (bf16[16,16,128]{2,1,0:T(8,128)(2,1)S(1)}, bf16[16,16,128]{2,1,0:T(8,128)(2,1)S(1)}, u32[]{:S(2)}, u32[]{:S(2)}) collective-permute-start(bf16[16,16,128]{2,1,0:T(8,128)(2,1)S(1)} %get-tuple-element.119.refs_0_), channel_id=1, source_target_pairs={{0,6},{2,4},{4,2},{6,0},{8,14},{10,12},{12,10},{14,8},{1,7},{3,5},... | collective-permute-start | bytes 196616 | tf_op jit(solution)/shard_map/ppermute | solution.py:116
  259.6 6.0 %collective-permute-start.83 = (bf16[16,16,128]{2,1,0:T(8,128)(2,1)S(1)}, bf16[16,16,128]{2,1,0:T(8,128)(2,1)S(1)}, u32[]{:S(2)}, u32[]{:S(2)}) collective-permute-start(bf16[16,16,128]{2,1,0:T(8,128)(2,1)S(1)} %get-tuple-element.124), channel_id=1, source_target_pairs={{0,2},{2,0},{4,6},{6,4},{8,10},{10,8},{12,14},{14,12},{1,3},{3,1},... | collective-permute-start | bytes 196616 | tf_op jit(solution)/shard_map/ppermute | solution.py:116
  259.8 10.0 %collective-permute-start.85 = (bf16[16,16,128]{2,1,0:T(8,128)(2,1)S(1)}, bf16[16,16,128]{2,1,0:T(8,128)(2,1)S(1)}, u32[]{:S(2)}, u32[]{:S(2)}) collective-permute-start(bf16[16,16,128]{2,1,0:T(8,128)(2,1)S(1)} %get-tuple-element.126), channel_id=1, source_target_pairs={{0,6},{2,4},{4,2},{6,0},{8,14},{10,12},{12,10},{14,8},{1,7},{3,5},... | collective-permute-start | bytes 196616 | tf_op jit(solution)/shard_map/ppermute | solution.py:116
  263.2 6.6 %collective-permute-start.86 = (bf16[16,16,128]{2,1,0:T(8,128)(2,1)S(1)}, bf16[16,16,128]{2,1,0:T(8,128)(2,1)S(1)}, u32[]{:S(2)}, u32[]{:S(2)}) collective-permute-start(bf16[16,16,128]{2,1,0:T(8,128)(2,1)S(1)} %get-tuple-element.127), channel_id=1, source_target_pairs={{0,8},{2,10},{4,12},{6,14},{8,0},{10,2},{12,4},{14,6},{1,9},{3,11}... | collective-permute-start | bytes 196616 | tf_op jit(solution)/shard_map/ppermute | solution.py:116
  263.2 8.2 %collective-permute-start.87 = (bf16[16,16,128]{2,1,0:T(8,128)(2,1)S(1)}, bf16[16,16,128]{2,1,0:T(8,128)(2,1)S(1)}, u32[]{:S(2)}, u32[]{:S(2)}) collective-permute-start(bf16[16,16,128]{2,1,0:T(8,128)(2,1)S(1)} %get-tuple-element.128), channel_id=1, source_target_pairs={{0,10},{2,8},{4,14},{6,12},{8,2},{10,0},{12,6},{14,4},{1,11},{3,9}... | collective-permute-start | bytes 196616 | tf_op jit(solution)/shard_map/ppermute | solution.py:116
  265.6 9.7 %collective-permute-start.88 = (bf16[16,16,128]{2,1,0:T(8,128)(2,1)S(1)}, bf16[16,16,128]{2,1,0:T(8,128)(2,1)S(1)}, u32[]{:S(2)}, u32[]{:S(2)}) collective-permute-start(bf16[16,16,128]{2,1,0:T(8,128)(2,1)S(1)} %get-tuple-element.129), channel_id=1, source_target_pairs={{0,12},{2,14},{4,8},{6,10},{8,4},{10,6},{12,0},{14,2},{1,13},{3,15... | collective-permute-start | bytes 196616 | tf_op jit(solution)/shard_map/ppermute | solution.py:116
  265.6 10.6 %collective-permute-start.89 = (bf16[16,16,128]{2,1,0:T(8,128)(2,1)S(1)}, bf16[16,16,128]{2,1,0:T(8,128)(2,1)S(1)}, u32[]{:S(2)}, u32[]{:S(2)}) collective-permute-start(bf16[16,16,128]{2,1,0:T(8,128)(2,1)S(1)} %get-tuple-element.130), channel_id=1, source_target_pairs={{0,14},{2,12},{4,10},{6,8},{8,6},{10,4},{12,2},{14,0},{1,15},{3,13... | collective-permute-start | bytes 196616 | tf_op jit(solution)/shard_map/ppermute | solution.py:116
  (31 other events, 194.6 us)

commit v2 on v0

v2 whole, which is shorter than its diff:
```python
import functools

import jax
import jax.numpy as jnp
from jax import lax
from jax.experimental import pallas as pl
from jax.experimental.pallas import tpu as pltpu
from jax.sharding import PartitionSpec as P

BS = 128
ITERS = 6
UNROLL = 32
NN = (((1,), (0,)), ((), ()))
NT = (((1,), (1,)), ((), ()))

SMEM = pl.BlockSpec(memory_space=pltpu.SMEM)
VMEM = pl.BlockSpec(memory_space=pltpu.VMEM)
PARAMS = pltpu.CompilerParams(vmem_limit_bytes=24 * 2**20)


def products(groups, src, dst, vecs, blocks, acc, dims):
    def group(g, _):
        first = g * UNROLL
        terms = [
            lax.dot_general(vecs[src[first + u]], blocks[first + u], dims, preferred_element_type=jnp.float32)
            for u in range(UNROLL)
        ]
        for u in range(UNROLL):
            acc[dst[first + u]] += terms[u]
        return 0

    lax.fori_loop(0, groups, group, 0)


def backward_kernel(groups, src, dst, blocks, *refs):
    pieces, (grad, vecs, acc) = refs[:-3], refs[-3:]
    half = len(pieces)
    span = pieces[0].shape[0] // 2
    for m in range(half):
        vecs[pl.ds(m * span, span)] = pieces[m][pl.ds(0, span)]
        vecs[pl.ds((m + half) * span, span)] = pieces[m][pl.ds(span, span)]
    acc[...] = jnp.zeros(acc.shape, acc.dtype)
    products(groups[0], src, dst, vecs, blocks, acc, NN)
    grad[...] = acc[pl.ds(0, grad.shape[0])]


def whole_backward_kernel(groups, src, dst, blocks, vecs, grad, acc):
    acc[...] = jnp.zeros(acc.shape, acc.dtype)
    products(groups[0], src, dst, vecs, blocks, acc, NN)
    grad[...] = acc[pl.ds(0, grad.shape[0])]


def forward_kernel(groups, src, dst, blocks, own, other, x_ref, cost, kind, upper, *refs):
    x_out, pieces, (vecs, acc) = refs[0], refs[1:-2], refs[-2:]
    cols = x_ref.shape[0] // 2
    for h in range(2):
        here, there = pl.ds(h * cols, cols), pl.ds((1 - h) * cols, cols)
        x = x_ref[here]
        value = x - 0.4 * (cost[here] - (own[here] + other[there]))
        lifted = jnp.where(kind[here] == 2, value, jnp.maximum(value, 0.0))
        x_next = jnp.where(kind[here] == 1, jnp.minimum(lifted, upper[here]), lifted)
        x_out[here] = x_next
        vecs[here] = (2.0 * x_next - x).astype(vecs.dtype)
    acc[...] = jnp.zeros(acc.shape, acc.dtype)
    products(groups[0], src, dst, vecs, blocks, acc, NT)
    half = len(pieces)
    span = pieces[0].shape[0] // 2
    for m in range(half):
        pieces[m][pl.ds(0, span)] = acc[pl.ds(m * span, span)].astype(pieces[m].dtype)
        pieces[m][pl.ds(span, span)] = acc[pl.ds((m + half) * span, span)].astype(pieces[m].dtype)


def near_sum_kernel(own, *refs):
    pieces, (total, sent) = refs[:-2], refs[-2:]
    image = own[...]
    for piece in pieces:
        image = image + piece[...].astype(jnp.float32)
    total[...] = image
    n = sent.shape[0]
    sent[...] = image[image.shape[0] - n :].astype(sent.dtype)


def dual_kernel(y_ref, rhs, near, far, y_out, y_half):
    span = near.shape[0] // 2
    for h in range(y_out.shape[0] // span):
        here = pl.ds(h * span, span)
        there = pl.ds(far.shape[0] - (h + 1) * span, span)
        image = near[here] + far[there].astype(jnp.float32)
        y = jnp.maximum(0.0, y_ref[here] + 0.9 * (rhs[here] - image))
        y_out[here] = y
        y_half[here] = y.astype(y_half.dtype)


def whole_dual_kernel(y_ref, rhs, image, y_out, y_half):
    y = jnp.maximum(0.0, y_ref[...] + 0.9 * (rhs[...] - image[...]))
    y_out[...] = y
    y_half[...] = y.astype(y_half.dtype)


def to_blocks(a):
    return jnp.transpose(a.reshape(a.shape[0], -1, BS), (1, 0, 2))


def from_blocks(a):
    return jnp.transpose(a, (1, 0, 2)).reshape(a.shape[1], -1)


def per_device(
    cost, rhs, primal, dual, bound_kind, upper, kblocks, block_row, block_col, block_count
):
    n_col, n_row = lax.axis_size("col"), lax.axis_size("row")
    scen = primal.shape[0]
    span, cols = dual.shape[2] // BS, primal.shape[2] // BS
    row_blocks, col_blocks = span * n_col, cols * n_row
    direct = n_col in (4, 8) and span & (span - 1) == 0
    half = n_col // 2

    tile = kblocks[0, 0]
    slots = jnp.arange(tile.shape[0], dtype=jnp.int32)
    count = block_count[0, 0]
    live = slots < count
    groups = ((count + UNROLL - 1) // UNROLL).reshape(1)
    mine = block_col[0, 0] // cols == lax.axis_index("row")
    bcol = jnp.where(mine, 0, cols) + block_col[0, 0] % cols
    brow = block_row[0, 0]
    if direct:
        brow = brow ^ (lax.axis_index("col") * span)
    to_col = jnp.where(live, bcol, col_blocks)
    to_row = jnp.where(live, brow, row_blocks)

    def swap(a):
        return lax.ppermute(a, "row", [(i, n_row - 1 - i) for i in range(n_row)])

    def partner(a, m):
        return lax.ppermute(a, "col", [(i, i ^ m) for i in range(n_col)])

    def near(a):
        return [partner(a, m) for m in range(1, half)]

    y = to_blocks(dual[:, 0])
    y_half = y.astype(jnp.bfloat16)
    rhs_all = to_blocks(rhs[:, 0])
    if direct:
        y_half = jnp.concatenate([y_half, partner(y_half, half)])
        pair = jnp.stack([y, rhs_all])
        both = jnp.concatenate([pair, partner(pair, half)], axis=1)
        y, rhs_all = both[0], both[1]

    own = jnp.concatenate(
        [to_blocks(primal[:, 0]), to_blocks(cost[:, 0]), to_blocks(upper), to_blocks(bound_kind).astype(jnp.float32)],
        axis=1,
    )
    state = jnp.concatenate([own, swap(own)])
    x, cost_all = state[:, :scen], state[:, scen : 2 * scen]
    upper_all, kind_all = state[:, 2 * scen : 2 * scen + 1], state[:, 2 * scen + 1 :]

    def shape(blocks, dtype):
        return jax.ShapeDtypeStruct((blocks, scen, BS), dtype)

    def call(kernel, outs, ins, scratch=(), scalars=0):
        return pl.pallas_call(
            kernel,
            out_shape=outs,
            in_specs=[SMEM] * scalars + [VMEM] * ins,
            out_specs=tuple(VMEM for _ in outs),
            scratch_shapes=[pltpu.VMEM((blocks, scen, BS), dtype) for blocks, dtype in scratch],
            compiler_params=PARAMS,
            name=kernel.__name__,
        )

    f32, bf16 = jnp.float32, jnp.bfloat16
    backward = call(
        backward_kernel if direct else whole_backward_kernel,
        (shape(col_blocks, f32),),
        1 + (half if direct else 1),
        ((row_blocks, bf16), (col_blocks + 1, f32)) if direct else ((col_blocks + 1, f32),),
        3,
    )
    if direct:
        pieces = (shape(2 * span, f32),) + (shape(2 * span, bf16),) * (half - 1)
    else:
        pieces = (shape(row_blocks, f32),)
    forward = call(
        forward_kernel,
        (shape(col_blocks, f32),) + pieces,
        7,
        ((col_blocks, bf16), (row_blocks + 1, f32)),
        3,
    )

    for step in range(ITERS):
        last = step == ITERS - 1
        y_slab = [y_half] + near(y_half) if direct else [lax.all_gather(y_half, "col", axis=0, tiled=True)]
        (grad,) = backward(groups, brow, to_col, tile, *y_slab)
        x, *image = forward(groups, bcol, to_row, tile, grad, swap(grad), x, cost_all, kind_all, upper_all)
        if direct:
            image = image[:1] + [partner(image[m], m) for m in range(1, half)]
            kept = 1 if last else 2
            total, sent = call(near_sum_kernel, (shape(2 * span, f32), shape(kept * span, bf16)), half)(*image)
            y, y_half = call(dual_kernel, (shape(kept * span, f32), shape(kept * span, bf16)), 4)(
                y, rhs_all, total, partner(sent, half)
            )
        else:
            image = lax.psum_scatter(image[0], "col", scatter_dimension=0, tiled=True)
            y, y_half = call(whole_dual_kernel, (shape(span, f32), shape(span, bf16)), 3)(y, rhs_all, image)

    return (from_blocks(x[:cols])[:, None, :], from_blocks(y)[:, None, :])


def solution(mesh):
    return jax.shard_map(
        per_device,
        mesh=mesh,
        in_specs=(
            P("grp", "col", "row"),
            P("grp", "row", "col"),
            P("grp", "col", "row"),
            P("grp", "row", "col"),
            P(("grp", "col"), "row"),
            P(("grp", "col"), "row"),
            P(("grp", "col"), "row", None, None, None),
            P(("grp", "col"), "row", None),
            P(("grp", "col"), "row", None),
            P(("grp", "col"), "row"),
        ),
        out_specs=(P("grp", "col", "row"), P("grp", "row", "col")),
        check_vma=False,
    )
```

time: 874 us -> 248 us (0.28)
  waiting for transfers between devices: 445 us -> 119 us
  blocking collectives: 185 us -> 0 us
  other arithmetic: 126 us -> 2.97 us
  starting transfers between devices: 0.5 us -> 76 us
  matrix products: 73 us -> 0 us
  Pallas kernels: 0 us -> 35.7 us
  local copies, waits for them, and re-layouts: 26.1 us -> 8.77 us
  between operations: 15.6 us -> 1.64 us
    reduce_scatter x12 -> x0, waiting for transfers between devices: 445 us -> none  [the longest x6 385 us: per_device(): lax.psum_scatter(partial_image, 'col', scatter_dimension=1, tiled=True)]
    all_gather x12 -> x0, blocking collectives: 185 us -> none  [the longest x6 173 us: per_device(): lax.all_gather(y_state.astype(jnp.bfloat16), 'col', axis=1, tiled=True)]
    ppermute x0 -> x51, waiting for transfers between devices: none -> 119 us  [the longest x44 111 us: partner(): return lax.ppermute(a, 'col', [(i, i ^ m) for i in range(n_col)])]
    scatter-add x12 -> x0, other arithmetic: 109 us -> none  [the longest x6 55.2 us: backward_tile(): summed = jax.ops.segment_sum(prod, bcol, num_segments=segments)]
    ppermute x0 -> x51, starting transfers between devices: none -> 76 us  [the longest x44 74.3 us: partner(): return lax.ppermute(a, 'col', [(i, i ^ m) for i in range(n_col)])]
    dot_general x12 -> x0, matrix products: 73 us -> none  [the longest x6 42.7 us: forward_tile(): jnp.einsum('nij,snj->nsi', kb, picked, preferred_element_type=jnp.float32)]
    pallas_call x0 -> x24, Pallas kernels: none -> 35.7 us  [the longest x6 21 us: per_device(): forward(groups, bcol, to_row, tile, grad, swap(grad), x, cost_all, kind_a...]
    convert_element_type x11 -> x1, other arithmetic: 14.8 us -> 0.7 us  [per_device(): to_blocks(bound_kind).astype(jnp.float32)]
  transfers between devices with their start and end apart: 12 -> 51, of which waited for: 12 -> 42; matrix products, arithmetic and copies ran while one was open for 0% -> 3% of each run, Pallas kernels for 0% -> 2%
where the time goes in v2:
time: 248 us; the launch traced here: 244 us
  waiting for transfers between devices  119 us (48%)
  starting transfers between devices  76 us (31%)
  Pallas kernels  35.7 us (14%)
  local copies, waits for them, and re-layouts  8.77 us (4%)
  other arithmetic  2.97 us (1%)
    ppermute x44, waiting for transfers between devices, partner(): return lax.ppermute(a, 'col', [(i, i ^ m) for i in range(n_col)])  111 us
    ppermute x44, starting transfers between devices, partner(): return lax.ppermute(a, 'col', [(i, i ^ m) for i in range(n_col)])  74.3 us
    pallas_call x6, Pallas kernels, per_device(): forward(groups, bcol, to_row, tile, grad, swap(grad), x, cost_all, kind_a...  21 us
    pallas_call x6, Pallas kernels, per_device(): grad, = backward(groups, brow, to_col, tile, *y_slab)  13.3 us
    ppermute x7, waiting for transfers between devices, swap(): return lax.ppermute(a, 'row', [(i, n_row - 1 - i) for i in range(n_row)])  7.82 us
  transfers between devices with their start and end apart: 51, of which 42 were waited for; matrix products, arithmetic and copies ran while one was open for 3% of the time, Pallas kernels for 2%

profile of v2, /device:TPU:10, one launch (start us, length us, event | category | flops | bytes accessed | tf_op | source)
XLA Modules:
  0.0 244.0 jit_solution(8009270321180662816)
XLA Ops:
  1.6 2.7 %collective-permute-start.1 = (bf16[16,16,128]{2,1,0:T(8,128)(2,1)S(1)}, bf16[16,16,128]{2,1,0:T(8,128)(2,1)S(1)}, u32[]{:S(2)}, u32[]{:S(2)}) collective-permute-start(bf16[16,16,128]{2,1,0:T(8,128)(2,1)S(1)} %bitcast.66), channel_id=1, source_target_pairs={{0,8},{2,10},{4,12},{6,14},{8,0},{10,2},{12,4},{14,6},{1,9},{3,11}... | collective-permute-start | bytes 196616 | tf_op jit(solution)/shard_map/ppermute | solution.py:135
  11.2 1.8 collective-permute-done.1
  13.1 3.0 %collective-permute-start.3 = (bf16[32,16,128]{2,1,0:T(8,128)(2,1)S(1)}, bf16[32,16,128]{2,1,0:T(8,128)(2,1)S(1)}, u32[]{:S(2)}, u32[]{:S(2)}) collective-permute-start(bf16[32,16,128]{2,1,0:T(8,128)(2,1)S(1)} %pad_maximum_fusion.4.refs_0_), channel_id=1, source_target_pairs={{0,4},{2,6},{4,0},{6,2},{8,12},{10,14},{12,8},{14,10},{1,5},{3,7},... | collective-permute-start | bytes 393224 | tf_op jit(solution)/shard_map/ppermute | solution.py:135
  16.5 4.9 %collective-permute-done.4.refs_3_ = bf16[32,16,128]{2,1,0:T(8,128)(2,1)S(1)} collective-permute-done((bf16[32,16,128]{2,1,0:T(8,128)(2,1)S(1)}, bf16[32,16,128]{2,1,0:T(8,128)(2,1)S(1)}, u32[]{:S(2)}, u32[]{:S(2)}) %collective-permute-start.4) | collective-permute-done | bytes 131104 | tf_op jit(solution)/shard_map/ppermute | solution.py:135
  21.4 2.0 collective-permute-done.3.refs_2_
  23.4 3.4 %copy-done = bf16[1,1,256,128,128]{4,3,2,1,0:T(8,128)(2,1)S(1)} copy-done((bf16[1,1,256,128,128]{4,3,2,1,0:T(8,128)(2,1)S(1)}, bf16[1,1,256,128,128]{4,3,2,1,0:T(8,128)(2,1)}, u32[]{:S(2)}) %copy-start) | copy-done | bytes 8388632
  26.8 2.2 backward_kernel.6.own
  29.3 1.4 collective-permute-done.5.other
  30.6 3.5 %forward_kernel.6 = (f32[32,16,128]{2,1,0:T(8,128)S(1)}, f32[32,16,128]{2,1,0:T(8,128)S(1)}, bf16[32,16,128]{2,1,0:T(8,128)(2,1)S(1)}, bf16[32,16,128]{2,1,0:T(8,128)(2,1)S(1)}, bf16[32,16,128]{2,1,0:T(8,128)(2,1)S(1)}) custom-call(s32[1]{0:T(128)} %bitcast.1.groups, s32[256]{0:T(256)S(1)} %get-tuple-element.111.src, s32[256]{0:T(256)S(1)} %fusion.2.dst, ...), custom_call_target="tpu_custom_call" | custom-call | tf_op jit(solution)/shard_map/forward_kernel/pallas_call | solution.py:195
  34.7 5.2 %collective-permute-start.8 = (bf16[32,16,128]{2,1,0:T(8,128)(2,1)S(1)}, bf16[32,16,128]{2,1,0:T(8,128)(2,1)S(1)}, u32[]{:S(2)}, u32[]{:S(2)}) collective-permute-start(bf16[32,16,128]{2,1,0:T(8,128)(2,1)S(1)} %get-tuple-element.57), channel_id=1, source_target_pairs={{0,4},{2,6},{4,0},{6,2},{8,12},{10,14},{12,8},{14,10},{1,5},{3,7},... | collective-permute-start | bytes 393224 | tf_op jit(solution)/shard_map/ppermute | solution.py:135
  39.9 1.4 collective-permute-start.9
  41.4 2.9 %collective-permute-done.8.refs_1_ = bf16[32,16,128]{2,1,0:T(8,128)(2,1)S(1)} collective-permute-done((bf16[32,16,128]{2,1,0:T(8,128)(2,1)S(1)}, bf16[32,16,128]{2,1,0:T(8,128)(2,1)S(1)}, u32[]{:S(2)}, u32[]{:S(2)}) %collective-permute-start.8) | collective-permute-done | bytes 131104 | tf_op jit(solution)/shard_map/ppermute | solution.py:135
  44.3 3.4 %collective-permute-done.9.refs_2_ = bf16[32,16,128]{2,1,0:T(8,128)(2,1)S(1)} collective-permute-done((bf16[32,16,128]{2,1,0:T(8,128)(2,1)S(1)}, bf16[32,16,128]{2,1,0:T(8,128)(2,1)S(1)}, u32[]{:S(2)}, u32[]{:S(2)}) %collective-permute-start.9) | collective-permute-done | bytes 131104 | tf_op jit(solution)/shard_map/ppermute | solution.py:135
  47.8 6.5 %collective-permute-done.10.far = bf16[32,16,128]{2,1,0:T(8,128)(2,1)S(1)} collective-permute-done((bf16[32,16,128]{2,1,0:T(8,128)(2,1)S(1)}, bf16[32,16,128]{2,1,0:T(8,128)(2,1)S(1)}, u32[]{:S(2)}, u32[]{:S(2)}) %collective-permute-start.10) | collective-permute-done | bytes 131104 | tf_op jit(solution)/shard_map/ppermute | solution.py:135
  54.4 3.6 %collective-permute-start.13 = (bf16[32,16,128]{2,1,0:T(8,128)(2,1)S(1)}, bf16[32,16,128]{2,1,0:T(8,128)(2,1)S(1)}, u32[]{:S(2)}, u32[]{:S(2)}) collective-permute-start(bf16[32,16,128]{2,1,0:T(8,128)(2,1)S(1)} %get-tuple-element.62.refs_0_), channel_id=1, source_target_pairs={{0,6},{2,4},{4,2},{6,0},{8,14},{10,12},{12,10},{14,8},{1,7},{3,5},... | collective-permute-start | bytes 393224 | tf_op jit(solution)/shard_map/ppermute | solution.py:135
  58.0 1.3 collective-permute-start.11
  59.3 2.8 %collective-permute-done.13.refs_3_ = bf16[32,16,128]{2,1,0:T(8,128)(2,1)S(1)} collective-permute-done((bf16[32,16,128]{2,1,0:T(8,128)(2,1)S(1)}, bf16[32,16,128]{2,1,0:T(8,128)(2,1)S(1)}, u32[]{:S(2)}, u32[]{:S(2)}) %collective-permute-start.13) | collective-permute-done | bytes 131104 | tf_op jit(solution)/shard_map/ppermute | solution.py:135
  62.1 2.0 collective-permute-done.12.refs_2_
  64.3 2.2 backward_kernel.7.own
  66.8 1.4 collective-permute-done.14.other
  68.1 3.5 %forward_kernel.7 = (f32[32,16,128]{2,1,0:T(8,128)S(1)}, f32[32,16,128]{2,1,0:T(8,128)S(1)}, bf16[32,16,128]{2,1,0:T(8,128)(2,1)S(1)}, bf16[32,16,128]{2,1,0:T(8,128)(2,1)S(1)}, bf16[32,16,128]{2,1,0:T(8,128)(2,1)S(1)}) custom-call(s32[1]{0:T(128)} %bitcast.1.groups, s32[256]{0:T(256)S(1)} %get-tuple-element.111.src, s32[256]{0:T(256)S(1)} %fusion.2.dst, ...), custom_call_target="tpu_custom_call" | custom-call | tf_op jit(solution)/shard_map/forward_kernel/pallas_call | solution.py:195
  71.6 1.3 collective-permute-start.15
  73.0 4.4 %collective-permute-start.16 = (bf16[32,16,128]{2,1,0:T(8,128)(2,1)S(1)}, bf16[32,16,128]{2,1,0:T(8,128)(2,1)S(1)}, u32[]{:S(2)}, u32[]{:S(2)}) collective-permute-start(bf16[32,16,128]{2,1,0:T(8,128)(2,1)S(1)} %get-tuple-element.66), channel_id=1, source_target_pairs={{0,4},{2,6},{4,0},{6,2},{8,12},{10,14},{12,8},{14,10},{1,5},{3,7},... | collective-permute-start | bytes 393224 | tf_op jit(solution)/shard_map/ppermute | solution.py:135
  77.4 1.4 collective-permute-start.17
  78.8 2.8 %collective-permute-done.16.refs_1_ = bf16[32,16,128]{2,1,0:T(8,128)(2,1)S(1)} collective-permute-done((bf16[32,16,128]{2,1,0:T(8,128)(2,1)S(1)}, bf16[32,16,128]{2,1,0:T(8,128)(2,1)S(1)}, u32[]{:S(2)}, u32[]{:S(2)}) %collective-permute-start.16) | collective-permute-done | bytes 131104 | tf_op jit(solution)/shard_map/ppermute | solution.py:135
  81.6 3.5 %collective-permute-done.17.refs_2_ = bf16[32,16,128]{2,1,0:T(8,128)(2,1)S(1)} collective-permute-done((bf16[32,16,128]{2,1,0:T(8,128)(2,1)S(1)}, bf16[32,16,128]{2,1,0:T(8,128)(2,1)S(1)}, u32[]{:S(2)}, u32[]{:S(2)}) %collective-permute-start.17) | collective-permute-done | bytes 131104 | tf_op jit(solution)/shard_map/ppermute | solution.py:135
  85.3 5.9 %collective-permute-done.18.far = bf16[32,16,128]{2,1,0:T(8,128)(2,1)S(1)} collective-permute-done((bf16[32,16,128]{2,1,0:T(8,128)(2,1)S(1)}, bf16[32,16,128]{2,1,0:T(8,128)(2,1)S(1)}, u32[]{:S(2)}, u32[]{:S(2)}) %collective-permute-start.18) | collective-permute-done | bytes 131104 | tf_op jit(solution)/shard_map/ppermute | solution.py:135
  91.2 4.5 %collective-permute-start.21 = (bf16[32,16,128]{2,1,0:T(8,128)(2,1)S(1)}, bf16[32,16,128]{2,1,0:T(8,128)(2,1)S(1)}, u32[]{:S(2)}, u32[]{:S(2)}) collective-permute-start(bf16[32,16,128]{2,1,0:T(8,128)(2,1)S(1)} %get-tuple-element.71.refs_0_), channel_id=1, source_target_pairs={{0,6},{2,4},{4,2},{6,0},{8,14},{10,12},{12,10},{14,8},{1,7},{3,5},... | collective-permute-start | bytes 393224 | tf_op jit(solution)/shard_map/ppermute | solution.py:135
  96.8 3.3 %collective-permute-done.21.refs_3_ = bf16[32,16,128]{2,1,0:T(8,128)(2,1)S(1)} collective-permute-done((bf16[32,16,128]{2,1,0:T(8,128)(2,1)S(1)}, bf16[32,16,128]{2,1,0:T(8,128)(2,1)S(1)}, u32[]{:S(2)}, u32[]{:S(2)}) %collective-permute-start.21) | collective-permute-done | bytes 131104 | tf_op jit(solution)/shard_map/ppermute | solution.py:135
  100.1 1.5 collective-permute-done.20.refs_2_
  102.2 2.2 backward_kernel.8.own
  104.7 1.3 collective-permute-done.22.other
  106.1 3.5 %forward_kernel.8 = (f32[32,16,128]{2,1,0:T(8,128)S(1)}, f32[32,16,128]{2,1,0:T(8,128)S(1)}, bf16[32,16,128]{2,1,0:T(8,128)(2,1)S(1)}, bf16[32,16,128]{2,1,0:T(8,128)(2,1)S(1)}, bf16[32,16,128]{2,1,0:T(8,128)(2,1)S(1)}) custom-call(s32[1]{0:T(128)} %bitcast.1.groups, s32[256]{0:T(256)S(1)} %get-tuple-element.111.src, s32[256]{0:T(256)S(1)} %fusion.2.dst, ...), custom_call_target="tpu_custom_call" | custom-call | tf_op jit(solution)/shard_map/forward_kernel/pallas_call | solution.py:195
  110.5 4.7 %collective-permute-start.24 = (bf16[32,16,128]{2,1,0:T(8,128)(2,1)S(1)}, bf16[32,16,128]{2,1,0:T(8,128)(2,1)S(1)}, u32[]{:S(2)}, u32[]{:S(2)}) collective-permute-start(bf16[32,16,128]{2,1,0:T(8,128)(2,1)S(1)} %get-tuple-element.75), channel_id=1, source_target_pairs={{0,4},{2,6},{4,0},{6,2},{8,12},{10,14},{12,8},{14,10},{1,5},{3,7},... | collective-permute-start | bytes 393224 | tf_op jit(solution)/shard_map/ppermute | solution.py:135
  116.3 2.5 %collective-permute-done.24.refs_1_ = bf16[32,16,128]{2,1,0:T(8,128)(2,1)S(1)} collective-permute-done((bf16[32,16,128]{2,1,0:T(8,128)(2,1)S(1)}, bf16[32,16,128]{2,1,0:T(8,128)(2,1)S(1)}, u32[]{:S(2)}, u32[]{:S(2)}) %collective-permute-start.24) | collective-permute-done | bytes 131104 | tf_op jit(solution)/shard_map/ppermute | solution.py:135
  118.8 4.0 %collective-permute-done.25.refs_2_ = bf16[32,16,128]{2,1,0:T(8,128)(2,1)S(1)} collective-permute-done((bf16[32,16,128]{2,1,0:T(8,128)(2,1)S(1)}, bf16[32,16,128]{2,1,0:T(8,128)(2,1)S(1)}, u32[]{:S(2)}, u32[]{:S(2)}) %collective-permute-start.25) | collective-permute-done | bytes 131104 | tf_op jit(solution)/shard_map/ppermute | solution.py:135
  122.9 6.3 %collective-permute-done.26.far = bf16[32,16,128]{2,1,0:T(8,128)(2,1)S(1)} collective-permute-done((bf16[32,16,128]{2,1,0:T(8,128)(2,1)S(1)}, bf16[32,16,128]{2,1,0:T(8,128)(2,1)S(1)}, u32[]{:S(2)}, u32[]{:S(2)}) %collective-permute-start.26) | collective-permute-done | bytes 131104 | tf_op jit(solution)/shard_map/ppermute | solution.py:135
  129.4 4.4 %collective-permute-start.29 = (bf16[32,16,128]{2,1,0:T(8,128)(2,1)S(1)}, bf16[32,16,128]{2,1,0:T(8,128)(2,1)S(1)}, u32[]{:S(2)}, u32[]{:S(2)}) collective-permute-start(bf16[32,16,128]{2,1,0:T(8,128)(2,1)S(1)} %get-tuple-element.80.refs_0_), channel_id=1, source_target_pairs={{0,6},{2,4},{4,2},{6,0},{8,14},{10,12},{12,10},{14,8},{1,7},{3,5},... | collective-permute-start | bytes 393224 | tf_op jit(solution)/shard_map/ppermute | solution.py:135
  134.6 3.4 %collective-permute-done.29.refs_3_ = bf16[32,16,128]{2,1,0:T(8,128)(2,1)S(1)} collective-permute-done((bf16[32,16,128]{2,1,0:T(8,128)(2,1)S(1)}, bf16[32,16,128]{2,1,0:T(8,128)(2,1)S(1)}, u32[]{:S(2)}, u32[]{:S(2)}) %collective-permute-start.29) | collective-permute-done | bytes 131104 | tf_op jit(solution)/shard_map/ppermute | solution.py:135
  138.0 1.5 collective-permute-done.28.refs_2_
  140.2 2.2 backward_kernel.9.own
  144.1 3.5 %forward_kernel.9 = (f32[32,16,128]{2,1,0:T(8,128)S(1)}, f32[32,16,128]{2,1,0:T(8,128)S(1)}, bf16[32,16,128]{2,1,0:T(8,128)(2,1)S(1)}, bf16[32,16,128]{2,1,0:T(8,128)(2,1)S(1)}, bf16[32,16,128]{2,1,0:T(8,128)(2,1)S(1)}) custom-call(s32[1]{0:T(128)} %bitcast.1.groups, s32[256]{0:T(256)S(1)} %get-tuple-element.111.src, s32[256]{0:T(256)S(1)} %fusion.2.dst, ...), custom_call_target="tpu_custom_call" | custom-call | tf_op jit(solution)/shard_map/forward_kernel/pallas_call | solution.py:195
  148.2 5.0 %collective-permute-start.32 = (bf16[32,16,128]{2,1,0:T(8,128)(2,1)S(1)}, bf16[32,16,128]{2,1,0:T(8,128)(2,1)S(1)}, u32[]{:S(2)}, u32[]{:S(2)}) collective-permute-start(bf16[32,16,128]{2,1,0:T(8,128)(2,1)S(1)} %get-tuple-element.84), channel_id=1, source_target_pairs={{0,4},{2,6},{4,0},{6,2},{8,12},{10,14},{12,8},{14,10},{1,5},{3,7},... | collective-permute-start | bytes 393224 | tf_op jit(solution)/shard_map/ppermute | solution.py:135
  154.0 2.9 %collective-permute-done.32.refs_1_ = bf16[32,16,128]{2,1,0:T(8,128)(2,1)S(1)} collective-permute-done((bf16[32,16,128]{2,1,0:T(8,128)(2,1)S(1)}, bf16[32,16,128]{2,1,0:T(8,128)(2,1)S(1)}, u32[]{:S(2)}, u32[]{:S(2)}) %collective-permute-start.32) | collective-permute-done | bytes 131104 | tf_op jit(solution)/shard_map/ppermute | solution.py:135
  156.9 4.0 %collective-permute-done.33.refs_2_ = bf16[32,16,128]{2,1,0:T(8,128)(2,1)S(1)} collective-permute-done((bf16[32,16,128]{2,1,0:T(8,128)(2,1)S(1)}, bf16[32,16,128]{2,1,0:T(8,128)(2,1)S(1)}, u32[]{:S(2)}, u32[]{:S(2)}) %collective-permute-start.33) | collective-permute-done | bytes 131104 | tf_op jit(solution)/shard_map/ppermute | solution.py:135
  161.0 6.3 %collective-permute-done.34.far = bf16[32,16,128]{2,1,0:T(8,128)(2,1)S(1)} collective-permute-done((bf16[32,16,128]{2,1,0:T(8,128)(2,1)S(1)}, bf16[32,16,128]{2,1,0:T(8,128)(2,1)S(1)}, u32[]{:S(2)}, u32[]{:S(2)}) %collective-permute-start.34) | collective-permute-done | bytes 131104 | tf_op jit(solution)/shard_map/ppermute | solution.py:135
  167.4 4.7 %collective-permute-start.37 = (bf16[32,16,128]{2,1,0:T(8,128)(2,1)S(1)}, bf16[32,16,128]{2,1,0:T(8,128)(2,1)S(1)}, u32[]{:S(2)}, u32[]{:S(2)}) collective-permute-start(bf16[32,16,128]{2,1,0:T(8,128)(2,1)S(1)} %get-tuple-element.89.refs_0_), channel_id=1, source_target_pairs={{0,6},{2,4},{4,2},{6,0},{8,14},{10,12},{12,10},{14,8},{1,7},{3,5},... | collective-permute-start | bytes 393224 | tf_op jit(solution)/shard_map/ppermute | solution.py:135
  173.1 3.3 %collective-permute-done.37.refs_3_ = bf16[32,16,128]{2,1,0:T(8,128)(2,1)S(1)} collective-permute-done((bf16[32,16,128]{2,1,0:T(8,128)(2,1)S(1)}, bf16[32,16,128]{2,1,0:T(8,128)(2,1)S(1)}, u32[]{:S(2)}, u32[]{:S(2)}) %collective-permute-start.37) | collective-permute-done | bytes 131104 | tf_op jit(solution)/shard_map/ppermute | solution.py:135
  176.5 1.7 collective-permute-done.36.refs_2_
  178.7 2.2 backward_kernel.10.own
  182.5 3.5 %forward_kernel.10 = (f32[32,16,128]{2,1,0:T(8,128)S(1)}, f32[32,16,128]{2,1,0:T(8,128)S(1)}, bf16[32,16,128]{2,1,0:T(8,128)(2,1)S(1)}, bf16[32,16,128]{2,1,0:T(8,128)(2,1)S(1)}, bf16[32,16,128]{2,1,0:T(8,128)(2,1)S(1)}) custom-call(s32[1]{0:T(128)} %bitcast.1.groups, s32[256]{0:T(256)S(1)} %get-tuple-element.111.src, s32[256]{0:T(256)S(1)} %fusion.2.dst, ...), custom_call_target="tpu_custom_call" | custom-call | tf_op jit(solution)/shard_map/forward_kernel/pallas_call | solution.py:195
  187.0 4.6 %collective-permute-start.40 = (bf16[32,16,128]{2,1,0:T(8,128)(2,1)S(1)}, bf16[32,16,128]{2,1,0:T(8,128)(2,1)S(1)}, u32[]{:S(2)}, u32[]{:S(2)}) collective-permute-start(bf16[32,16,128]{2,1,0:T(8,128)(2,1)S(1)} %get-tuple-element.93), channel_id=1, source_target_pairs={{0,4},{2,6},{4,0},{6,2},{8,12},{10,14},{12,8},{14,10},{1,5},{3,7},... | collective-permute-start | bytes 393224 | tf_op jit(solution)/shard_map/ppermute | solution.py:135
  192.8 2.5 %collective-permute-done.40.refs_1_ = bf16[32,16,128]{2,1,0:T(8,128)(2,1)S(1)} collective-permute-done((bf16[32,16,128]{2,1,0:T(8,128)(2,1)S(1)}, bf16[32,16,128]{2,1,0:T(8,128)(2,1)S(1)}, u32[]{:S(2)}, u32[]{:S(2)}) %collective-permute-start.40) | collective-permute-done | bytes 131104 | tf_op jit(solution)/shard_map/ppermute | solution.py:135
  195.3 4.0 %collective-permute-done.41.refs_2_ = bf16[32,16,128]{2,1,0:T(8,128)(2,1)S(1)} collective-permute-done((bf16[32,16,128]{2,1,0:T(8,128)(2,1)S(1)}, bf16[32,16,128]{2,1,0:T(8,128)(2,1)S(1)}, u32[]{:S(2)}, u32[]{:S(2)}) %collective-permute-start.41) | collective-permute-done | bytes 131104 | tf_op jit(solution)/shard_map/ppermute | solution.py:135
  199.5 6.3 %collective-permute-done.42.far = bf16[32,16,128]{2,1,0:T(8,128)(2,1)S(1)} collective-permute-done((bf16[32,16,128]{2,1,0:T(8,128)(2,1)S(1)}, bf16[32,16,128]{2,1,0:T(8,128)(2,1)S(1)}, u32[]{:S(2)}, u32[]{:S(2)}) %collective-permute-start.42) | collective-permute-done | bytes 131104 | tf_op jit(solution)/shard_map/ppermute | solution.py:135
  205.9 4.3 %collective-permute-start.45 = (bf16[32,16,128]{2,1,0:T(8,128)(2,1)S(1)}, bf16[32,16,128]{2,1,0:T(8,128)(2,1)S(1)}, u32[]{:S(2)}, u32[]{:S(2)}) collective-permute-start(bf16[32,16,128]{2,1,0:T(8,128)(2,1)S(1)} %get-tuple-element.97.refs_0_), channel_id=1, source_target_pairs={{0,6},{2,4},{4,2},{6,0},{8,14},{10,12},{12,10},{14,8},{1,7},{3,5},... | collective-permute-start | bytes 393224 | tf_op jit(solution)/shard_map/ppermute | solution.py:135
  211.1 3.4 %collective-permute-done.45.refs_3_ = bf16[32,16,128]{2,1,0:T(8,128)(2,1)S(1)} collective-permute-done((bf16[32,16,128]{2,1,0:T(8,128)(2,1)S(1)}, bf16[32,16,128]{2,1,0:T(8,128)(2,1)S(1)}, u32[]{:S(2)}, u32[]{:S(2)}) %collective-permute-start.45) | collective-permute-done | bytes 131104 | tf_op jit(solution)/shard_map/ppermute | solution.py:135
  214.5 1.5 collective-permute-done.44.refs_2_
  216.7 2.2 backward_kernel.11.own
  220.5 3.5 %forward_kernel.11 = (f32[32,16,128]{2,1,0:T(8,128)S(1)}, f32[32,16,128]{2,1,0:T(8,128)S(1)}, bf16[32,16,128]{2,1,0:T(8,128)(2,1)S(1)}, bf16[32,16,128]{2,1,0:T(8,128)(2,1)S(1)}, bf16[32,16,128]{2,1,0:T(8,128)(2,1)S(1)}) custom-call(s32[1]{0:T(128)} %bitcast.1.groups, s32[256]{0:T(256)S(1)} %get-tuple-element.111.src, s32[256]{0:T(256)S(1)} %fusion.2.dst, ...), custom_call_target="tpu_custom_call" | custom-call | tf_op jit(solution)/shard_map/forward_kernel/pallas_call | solution.py:195
  224.7 5.0 %collective-permute-start.48 = (bf16[32,16,128]{2,1,0:T(8,128)(2,1)S(1)}, bf16[32,16,128]{2,1,0:T(8,128)(2,1)S(1)}, u32[]{:S(2)}, u32[]{:S(2)}) collective-permute-start(bf16[32,16,128]{2,1,0:T(8,128)(2,1)S(1)} %get-tuple-element.103), channel_id=1, source_target_pairs={{0,4},{2,6},{4,0},{6,2},{8,12},{10,14},{12,8},{14,10},{1,5},{3,7},... | collective-permute-start | bytes 393224 | tf_op jit(solution)/shard_map/ppermute | solution.py:135
  230.5 2.9 %collective-permute-done.48.refs_1_ = bf16[32,16,128]{2,1,0:T(8,128)(2,1)S(1)} collective-permute-done((bf16[32,16,128]{2,1,0:T(8,128)(2,1)S(1)}, bf16[32,16,128]{2,1,0:T(8,128)(2,1)S(1)}, u32[]{:S(2)}, u32[]{:S(2)}) %collective-permute-start.48) | collective-permute-done | bytes 131104 | tf_op jit(solution)/shard_map/ppermute | solution.py:135
  233.4 4.0 %collective-permute-done.49.refs_2_ = bf16[32,16,128]{2,1,0:T(8,128)(2,1)S(1)} collective-permute-done((bf16[32,16,128]{2,1,0:T(8,128)(2,1)S(1)}, bf16[32,16,128]{2,1,0:T(8,128)(2,1)S(1)}, u32[]{:S(2)}, u32[]{:S(2)}) %collective-permute-start.49) | collective-permute-done | bytes 131104 | tf_op jit(solution)/shard_map/ppermute | solution.py:135
  238.2 4.4 %collective-permute-done.50.far = bf16[16,16,128]{2,1,0:T(8,128)(2,1)S(1)} collective-permute-done((bf16[16,16,128]{2,1,0:T(8,128)(2,1)S(1)}, bf16[16,16,128]{2,1,0:T(8,128)(2,1)S(1)}, u32[]{:S(2)}, u32[]{:S(2)}) %collective-permute-start.50) | collective-permute-done | bytes 65568 | tf_op jit(solution)/shard_map/ppermute | solution.py:135
  (87 shorter events, 30.9 us)
Async XLA Ops:
  0.6 28.5 %copy-start.2 = (f32[1,2048]{1,0:T(1,128)S(1)}, f32[1,2048]{1,0:T(1,128)}, u32[]{:S(2)}) copy-start(f32[1,2048]{1,0:T(1,128)} %param.15) | copy-start | bytes 24580
  1.6 11.4 %collective-permute-start.1 = (bf16[16,16,128]{2,1,0:T(8,128)(2,1)S(1)}, bf16[16,16,128]{2,1,0:T(8,128)(2,1)S(1)}, u32[]{:S(2)}, u32[]{:S(2)}) collective-permute-start(bf16[16,16,128]{2,1,0:T(8,128)(2,1)S(1)} %bitcast.66), channel_id=1, source_target_pairs={{0,8},{2,10},{4,12},{6,14},{8,0},{10,2},{12,4},{14,6},{1,9},{3,11}... | collective-permute-start | bytes 196616 | tf_op jit(solution)/shard_map/ppermute | solution.py:135
  6.2 35.1 %collective-permute-start = (f32[2,16,16,128]{3,2,1,0:T(8,128)S(1)}, f32[2,16,16,128]{3,2,1,0:T(8,128)S(1)}, u32[]{:S(2)}, u32[]{:S(2)}) collective-permute-start(f32[2,16,16,128]{3,2,1,0:T(8,128)S(1)} %pad_maximum_fusion.3), channel_id=1, source_target_pairs={{0,8},{2,10},{4,12},{6,14},{8,0},{10,2},{12,4},{14,6},{1,9},{3,11}... | collective-permute-start | bytes 786440 | tf_op jit(solution)/shard_map/ppermute | solution.py:135
  9.1 20.0 %collective-permute-start.6 = (f32[16,34,128]{2,1,0:T(8,128)S(1)}, f32[16,34,128]{2,1,0:T(8,128)S(1)}, u32[]{:S(2)}, u32[]{:S(2)}) collective-permute-start(f32[16,34,128]{2,1,0:T(8,128)S(1)} %pad_maximum_fusion.2), channel_id=1, source_target_pairs={{0,1},{1,0},{2,3},{3,2},{4,5},{5,4},{6,7},{7,6},{8,9},{9,8},{10,11... | collective-permute-start | bytes 835592 | tf_op jit(solution)/shard_map/ppermute | solution.py:132
  13.0 8.4 %collective-permute-start.4 = (bf16[32,16,128]{2,1,0:T(8,128)(2,1)S(1)}, bf16[32,16,128]{2,1,0:T(8,128)(2,1)S(1)}, u32[]{:S(2)}, u32[]{:S(2)}) collective-permute-start(bf16[32,16,128]{2,1,0:T(8,128)(2,1)S(1)} %pad_maximum_fusion.4.refs_0_), channel_id=1, source_target_pairs={{0,6},{2,4},{4,2},{6,0},{8,14},{10,12},{12,10},{14,8},{1,7},{3,5},... | collective-permute-start | bytes 393224 | tf_op jit(solution)/shard_map/ppermute | solution.py:135
  13.1 10.4 %collective-permute-start.3 = (bf16[32,16,128]{2,1,0:T(8,128)(2,1)S(1)}, bf16[32,16,128]{2,1,0:T(8,128)(2,1)S(1)}, u32[]{:S(2)}, u32[]{:S(2)}) collective-permute-start(bf16[32,16,128]{2,1,0:T(8,128)(2,1)S(1)} %pad_maximum_fusion.4.refs_0_), channel_id=1, source_target_pairs={{0,4},{2,6},{4,0},{6,2},{8,12},{10,14},{12,8},{14,10},{1,5},{3,7},... | collective-permute-start | bytes 393224 | tf_op jit(solution)/shard_map/ppermute | solution.py:135
  16.0 7.4 %collective-permute-start.2 = (bf16[32,16,128]{2,1,0:T(8,128)(2,1)S(1)}, bf16[32,16,128]{2,1,0:T(8,128)(2,1)S(1)}, u32[]{:S(2)}, u32[]{:S(2)}) collective-permute-start(bf16[32,16,128]{2,1,0:T(8,128)(2,1)S(1)} %pad_maximum_fusion.4.refs_0_), channel_id=1, source_target_pairs={{0,2},{2,0},{4,6},{6,4},{8,10},{10,8},{12,14},{14,12},{1,3},{3,1},... | collective-permute-start | bytes 393224 | tf_op jit(solution)/shard_map/ppermute | solution.py:135
  23.4 3.4 %copy-start = (bf16[1,1,256,128,128]{4,3,2,1,0:T(8,128)(2,1)S(1)}, bf16[1,1,256,128,128]{4,3,2,1,0:T(8,128)(2,1)}, u32[]{:S(2)}) copy-start(bf16[1,1,256,128,128]{4,3,2,1,0:T(8,128)(2,1)} %param.16) | copy-start | bytes 25165828
  26.8 3.8 %copy-start.1 = (bf16[1,1,256,128,128]{4,3,2,1,0:T(8,128)(2,1)S(1)}, bf16[1,1,256,128,128]{4,3,2,1,0:T(8,128)(2,1)}, u32[]{:S(2)}) copy-start(bf16[1,1,256,128,128]{4,3,2,1,0:T(8,128)(2,1)} %param.16) | copy-start | bytes 25165828
  29.0 1.6 collective-permute-start.5
  34.1 7.2 %collective-permute-start.7 = (bf16[32,16,128]{2,1,0:T(8,128)(2,1)S(1)}, bf16[32,16,128]{2,1,0:T(8,128)(2,1)S(1)}, u32[]{:S(2)}, u32[]{:S(2)}) collective-permute-start(bf16[32,16,128]{2,1,0:T(8,128)(2,1)S(1)} %get-tuple-element.56), channel_id=1, source_target_pairs={{0,2},{2,0},{4,6},{6,4},{8,10},{10,8},{12,14},{14,12},{1,3},{3,1},... | collective-permute-start | bytes 393224 | tf_op jit(solution)/shard_map/ppermute | solution.py:135
  34.7 9.6 %collective-permute-start.8 = (bf16[32,16,128]{2,1,0:T(8,128)(2,1)S(1)}, bf16[32,16,128]{2,1,0:T(8,128)(2,1)S(1)}, u32[]{:S(2)}, u32[]{:S(2)}) collective-permute-start(bf16[32,16,128]{2,1,0:T(8,128)(2,1)S(1)} %get-tuple-element.57), channel_id=1, source_target_pairs={{0,4},{2,6},{4,0},{6,2},{8,12},{10,14},{12,8},{14,10},{1,5},{3,7},... | collective-permute-start | bytes 393224 | tf_op jit(solution)/shard_map/ppermute | solution.py:135
  39.9 7.7 %collective-permute-start.9 = (bf16[32,16,128]{2,1,0:T(8,128)(2,1)S(1)}, bf16[32,16,128]{2,1,0:T(8,128)(2,1)S(1)}, u32[]{:S(2)}, u32[]{:S(2)}) collective-permute-start(bf16[32,16,128]{2,1,0:T(8,128)(2,1)S(1)} %get-tuple-element.58), channel_id=1, source_target_pairs={{0,6},{2,4},{4,2},{6,0},{8,14},{10,12},{12,10},{14,8},{1,7},{3,5},... | collective-permute-start | bytes 393224 | tf_op jit(solution)/shard_map/ppermute | solution.py:135
  47.7 6.6 %collective-permute-start.10 = (bf16[32,16,128]{2,1,0:T(8,128)(2,1)S(1)}, bf16[32,16,128]{2,1,0:T(8,128)(2,1)S(1)}, u32[]{:S(2)}, u32[]{:S(2)}) collective-permute-start(bf16[32,16,128]{2,1,0:T(8,128)(2,1)S(1)} %get-tuple-element.60), channel_id=1, source_target_pairs={{0,8},{2,10},{4,12},{6,14},{8,0},{10,2},{12,4},{14,6},{1,9},{3,11}... | collective-permute-start | bytes 393224 | tf_op jit(solution)/shard_map/ppermute | solution.py:135
  54.4 7.7 %collective-permute-start.13 = (bf16[32,16,128]{2,1,0:T(8,128)(2,1)S(1)}, bf16[32,16,128]{2,1,0:T(8,128)(2,1)S(1)}, u32[]{:S(2)}, u32[]{:S(2)}) collective-permute-start(bf16[32,16,128]{2,1,0:T(8,128)(2,1)S(1)} %get-tuple-element.62.refs_0_), channel_id=1, source_target_pairs={{0,6},{2,4},{4,2},{6,0},{8,14},{10,12},{12,10},{14,8},{1,7},{3,5},... | collective-permute-start | bytes 393224 | tf_op jit(solution)/shard_map/ppermute | solution.py:135
  58.0 6.1 %collective-permute-start.12 = (bf16[32,16,128]{2,1,0:T(8,128)(2,1)S(1)}, bf16[32,16,128]{2,1,0:T(8,128)(2,1)S(1)}, u32[]{:S(2)}, u32[]{:S(2)}) collective-permute-start(bf16[32,16,128]{2,1,0:T(8,128)(2,1)S(1)} %get-tuple-element.62.refs_0_), channel_id=1, source_target_pairs={{0,4},{2,6},{4,0},{6,2},{8,12},{10,14},{12,8},{14,10},{1,5},{3,7},... | collective-permute-start | bytes 393224 | tf_op jit(solution)/shard_map/ppermute | solution.py:135
  58.0 6.3 %collective-permute-start.11 = (bf16[32,16,128]{2,1,0:T(8,128)(2,1)S(1)}, bf16[32,16,128]{2,1,0:T(8,128)(2,1)S(1)}, u32[]{:S(2)}, u32[]{:S(2)}) collective-permute-start(bf16[32,16,128]{2,1,0:T(8,128)(2,1)S(1)} %get-tuple-element.62.refs_0_), channel_id=1, source_target_pairs={{0,2},{2,0},{4,6},{6,4},{8,10},{10,8},{12,14},{14,12},{1,3},{3,1},... | collective-permute-start | bytes 393224 | tf_op jit(solution)/shard_map/ppermute | solution.py:135
  66.5 1.6 collective-permute-start.14
  71.6 7.1 %collective-permute-start.15 = (bf16[32,16,128]{2,1,0:T(8,128)(2,1)S(1)}, bf16[32,16,128]{2,1,0:T(8,128)(2,1)S(1)}, u32[]{:S(2)}, u32[]{:S(2)}) collective-permute-start(bf16[32,16,128]{2,1,0:T(8,128)(2,1)S(1)} %get-tuple-element.65), channel_id=1, source_target_pairs={{0,2},{2,0},{4,6},{6,4},{8,10},{10,8},{12,14},{14,12},{1,3},{3,1},... | collective-permute-start | bytes 393224 | tf_op jit(solution)/shard_map/ppermute | solution.py:135
  73.0 8.6 %collective-permute-start.16 = (bf16[32,16,128]{2,1,0:T(8,128)(2,1)S(1)}, bf16[32,16,128]{2,1,0:T(8,128)(2,1)S(1)}, u32[]{:S(2)}, u32[]{:S(2)}) collective-permute-start(bf16[32,16,128]{2,1,0:T(8,128)(2,1)S(1)} %get-tuple-element.66), channel_id=1, source_target_pairs={{0,4},{2,6},{4,0},{6,2},{8,12},{10,14},{12,8},{14,10},{1,5},{3,7},... | collective-permute-start | bytes 393224 | tf_op jit(solution)/shard_map/ppermute | solution.py:135
  77.4 7.7 %collective-permute-start.17 = (bf16[32,16,128]{2,1,0:T(8,128)(2,1)S(1)}, bf16[32,16,128]{2,1,0:T(8,128)(2,1)S(1)}, u32[]{:S(2)}, u32[]{:S(2)}) collective-permute-start(bf16[32,16,128]{2,1,0:T(8,128)(2,1)S(1)} %get-tuple-element.67), channel_id=1, source_target_pairs={{0,6},{2,4},{4,2},{6,0},{8,14},{10,12},{12,10},{14,8},{1,7},{3,5},... | collective-permute-start | bytes 393224 | tf_op jit(solution)/shard_map/ppermute | solution.py:135
  85.2 5.9 %collective-permute-start.18 = (bf16[32,16,128]{2,1,0:T(8,128)(2,1)S(1)}, bf16[32,16,128]{2,1,0:T(8,128)(2,1)S(1)}, u32[]{:S(2)}, u32[]{:S(2)}) collective-permute-start(bf16[32,16,128]{2,1,0:T(8,128)(2,1)S(1)} %get-tuple-element.69), channel_id=1, source_target_pairs={{0,8},{2,10},{4,12},{6,14},{8,0},{10,2},{12,4},{14,6},{1,9},{3,11}... | collective-permute-start | bytes 393224 | tf_op jit(solution)/shard_map/ppermute | solution.py:135
  91.2 8.8 %collective-permute-start.21 = (bf16[32,16,128]{2,1,0:T(8,128)(2,1)S(1)}, bf16[32,16,128]{2,1,0:T(8,128)(2,1)S(1)}, u32[]{:S(2)}, u32[]{:S(2)}) collective-permute-start(bf16[32,16,128]{2,1,0:T(8,128)(2,1)S(1)} %get-tuple-element.71.refs_0_), channel_id=1, source_target_pairs={{0,6},{2,4},{4,2},{6,0},{8,14},{10,12},{12,10},{14,8},{1,7},{3,5},... | collective-permute-start | bytes 393224 | tf_op jit(solution)/shard_map/ppermute | solution.py:135
  95.8 5.8 %collective-permute-start.20 = (bf16[32,16,128]{2,1,0:T(8,128)(2,1)S(1)}, bf16[32,16,128]{2,1,0:T(8,128)(2,1)S(1)}, u32[]{:S(2)}, u32[]{:S(2)}) collective-permute-start(bf16[32,16,128]{2,1,0:T(8,128)(2,1)S(1)} %get-tuple-element.71.refs_0_), channel_id=1, source_target_pairs={{0,4},{2,6},{4,0},{6,2},{8,12},{10,14},{12,8},{14,10},{1,5},{3,7},... | collective-permute-start | bytes 393224 | tf_op jit(solution)/shard_map/ppermute | solution.py:135
  95.8 6.5 %collective-permute-start.19 = (bf16[32,16,128]{2,1,0:T(8,128)(2,1)S(1)}, bf16[32,16,128]{2,1,0:T(8,128)(2,1)S(1)}, u32[]{:S(2)}, u32[]{:S(2)}) collective-permute-start(bf16[32,16,128]{2,1,0:T(8,128)(2,1)S(1)} %get-tuple-element.71.refs_0_), channel_id=1, source_target_pairs={{0,2},{2,0},{4,6},{6,4},{8,10},{10,8},{12,14},{14,12},{1,3},{3,1},... | collective-permute-start | bytes 393224 | tf_op jit(solution)/shard_map/ppermute | solution.py:135
  104.5 1.6 collective-permute-start.22
  109.6 6.7 %collective-permute-start.23 = (bf16[32,16,128]{2,1,0:T(8,128)(2,1)S(1)}, bf16[32,16,128]{2,1,0:T(8,128)(2,1)S(1)}, u32[]{:S(2)}, u32[]{:S(2)}) collective-permute-start(bf16[32,16,128]{2,1,0:T(8,128)(2,1)S(1)} %get-tuple-element.74), channel_id=1, source_target_pairs={{0,2},{2,0},{4,6},{6,4},{8,10},{10,8},{12,14},{14,12},{1,3},{3,1},... | collective-permute-start | bytes 393224 | tf_op jit(solution)/shard_map/ppermute | solution.py:135
  110.5 8.3 %collective-permute-start.24 = (bf16[32,16,128]{2,1,0:T(8,128)(2,1)S(1)}, bf16[32,16,128]{2,1,0:T(8,128)(2,1)S(1)}, u32[]{:S(2)}, u32[]{:S(2)}) collective-permute-start(bf16[32,16,128]{2,1,0:T(8,128)(2,1)S(1)} %get-tuple-element.75), channel_id=1, source_target_pairs={{0,4},{2,6},{4,0},{6,2},{8,12},{10,14},{12,8},{14,10},{1,5},{3,7},... | collective-permute-start | bytes 393224 | tf_op jit(solution)/shard_map/ppermute | solution.py:135
  115.1 7.7 %collective-permute-start.25 = (bf16[32,16,128]{2,1,0:T(8,128)(2,1)S(1)}, bf16[32,16,128]{2,1,0:T(8,128)(2,1)S(1)}, u32[]{:S(2)}, u32[]{:S(2)}) collective-permute-start(bf16[32,16,128]{2,1,0:T(8,128)(2,1)S(1)} %get-tuple-element.76), channel_id=1, source_target_pairs={{0,6},{2,4},{4,2},{6,0},{8,14},{10,12},{12,10},{14,8},{1,7},{3,5},... | collective-permute-start | bytes 393224 | tf_op jit(solution)/shard_map/ppermute | solution.py:135
  122.9 6.4 %collective-permute-start.26 = (bf16[32,16,128]{2,1,0:T(8,128)(2,1)S(1)}, bf16[32,16,128]{2,1,0:T(8,128)(2,1)S(1)}, u32[]{:S(2)}, u32[]{:S(2)}) collective-permute-start(bf16[32,16,128]{2,1,0:T(8,128)(2,1)S(1)} %get-tuple-element.78), channel_id=1, source_target_pairs={{0,8},{2,10},{4,12},{6,14},{8,0},{10,2},{12,4},{14,6},{1,9},{3,11}... | collective-permute-start | bytes 393224 | tf_op jit(solution)/shard_map/ppermute | solution.py:135
  129.4 8.7 %collective-permute-start.29 = (bf16[32,16,128]{2,1,0:T(8,128)(2,1)S(1)}, bf16[32,16,128]{2,1,0:T(8,128)(2,1)S(1)}, u32[]{:S(2)}, u32[]{:S(2)}) collective-permute-start(bf16[32,16,128]{2,1,0:T(8,128)(2,1)S(1)} %get-tuple-element.80.refs_0_), channel_id=1, source_target_pairs={{0,6},{2,4},{4,2},{6,0},{8,14},{10,12},{12,10},{14,8},{1,7},{3,5},... | collective-permute-start | bytes 393224 | tf_op jit(solution)/shard_map/ppermute | solution.py:135
  133.7 5.8 %collective-permute-start.28 = (bf16[32,16,128]{2,1,0:T(8,128)(2,1)S(1)}, bf16[32,16,128]{2,1,0:T(8,128)(2,1)S(1)}, u32[]{:S(2)}, u32[]{:S(2)}) collective-permute-start(bf16[32,16,128]{2,1,0:T(8,128)(2,1)S(1)} %get-tuple-element.80.refs_0_), channel_id=1, source_target_pairs={{0,4},{2,6},{4,0},{6,2},{8,12},{10,14},{12,8},{14,10},{1,5},{3,7},... | collective-permute-start | bytes 393224 | tf_op jit(solution)/shard_map/ppermute | solution.py:135
  133.7 6.5 %collective-permute-start.27 = (bf16[32,16,128]{2,1,0:T(8,128)(2,1)S(1)}, bf16[32,16,128]{2,1,0:T(8,128)(2,1)S(1)}, u32[]{:S(2)}, u32[]{:S(2)}) collective-permute-start(bf16[32,16,128]{2,1,0:T(8,128)(2,1)S(1)} %get-tuple-element.80.refs_0_), channel_id=1, source_target_pairs={{0,2},{2,0},{4,6},{6,4},{8,10},{10,8},{12,14},{14,12},{1,3},{3,1},... | collective-permute-start | bytes 393224 | tf_op jit(solution)/shard_map/ppermute | solution.py:135
  142.5 1.6 collective-permute-start.30
  147.6 6.4 %collective-permute-start.31 = (bf16[32,16,128]{2,1,0:T(8,128)(2,1)S(1)}, bf16[32,16,128]{2,1,0:T(8,128)(2,1)S(1)}, u32[]{:S(2)}, u32[]{:S(2)}) collective-permute-start(bf16[32,16,128]{2,1,0:T(8,128)(2,1)S(1)} %get-tuple-element.83), channel_id=1, source_target_pairs={{0,2},{2,0},{4,6},{6,4},{8,10},{10,8},{12,14},{14,12},{1,3},{3,1},... | collective-permute-start | bytes 393224 | tf_op jit(solution)/shard_map/ppermute | solution.py:135
  148.2 8.7 %collective-permute-start.32 = (bf16[32,16,128]{2,1,0:T(8,128)(2,1)S(1)}, bf16[32,16,128]{2,1,0:T(8,128)(2,1)S(1)}, u32[]{:S(2)}, u32[]{:S(2)}) collective-permute-start(bf16[32,16,128]{2,1,0:T(8,128)(2,1)S(1)} %get-tuple-element.84), channel_id=1, source_target_pairs={{0,4},{2,6},{4,0},{6,2},{8,12},{10,14},{12,8},{14,10},{1,5},{3,7},... | collective-permute-start | bytes 393224 | tf_op jit(solution)/shard_map/ppermute | solution.py:135
  153.2 7.7 %collective-permute-start.33 = (bf16[32,16,128]{2,1,0:T(8,128)(2,1)S(1)}, bf16[32,16,128]{2,1,0:T(8,128)(2,1)S(1)}, u32[]{:S(2)}, u32[]{:S(2)}) collective-permute-start(bf16[32,16,128]{2,1,0:T(8,128)(2,1)S(1)} %get-tuple-element.85), channel_id=1, source_target_pairs={{0,6},{2,4},{4,2},{6,0},{8,14},{10,12},{12,10},{14,8},{1,7},{3,5},... | collective-permute-start | bytes 393224 | tf_op jit(solution)/shard_map/ppermute | solution.py:135
  161.0 6.4 %collective-permute-start.34 = (bf16[32,16,128]{2,1,0:T(8,128)(2,1)S(1)}, bf16[32,16,128]{2,1,0:T(8,128)(2,1)S(1)}, u32[]{:S(2)}, u32[]{:S(2)}) collective-permute-start(bf16[32,16,128]{2,1,0:T(8,128)(2,1)S(1)} %get-tuple-element.87), channel_id=1, source_target_pairs={{0,8},{2,10},{4,12},{6,14},{8,0},{10,2},{12,4},{14,6},{1,9},{3,11}... | collective-permute-start | bytes 393224 | tf_op jit(solution)/shard_map/ppermute | solution.py:135
  167.4 9.0 %collective-permute-start.37 = (bf16[32,16,128]{2,1,0:T(8,128)(2,1)S(1)}, bf16[32,16,128]{2,1,0:T(8,128)(2,1)S(1)}, u32[]{:S(2)}, u32[]{:S(2)}) collective-permute-start(bf16[32,16,128]{2,1,0:T(8,128)(2,1)S(1)} %get-tuple-element.89.refs_0_), channel_id=1, source_target_pairs={{0,6},{2,4},{4,2},{6,0},{8,14},{10,12},{12,10},{14,8},{1,7},{3,5},... | collective-permute-start | bytes 393224 | tf_op jit(solution)/shard_map/ppermute | solution.py:135
  172.2 6.0 %collective-permute-start.36 = (bf16[32,16,128]{2,1,0:T(8,128)(2,1)S(1)}, bf16[32,16,128]{2,1,0:T(8,128)(2,1)S(1)}, u32[]{:S(2)}, u32[]{:S(2)}) collective-permute-start(bf16[32,16,128]{2,1,0:T(8,128)(2,1)S(1)} %get-tuple-element.89.refs_0_), channel_id=1, source_target_pairs={{0,4},{2,6},{4,0},{6,2},{8,12},{10,14},{12,8},{14,10},{1,5},{3,7},... | collective-permute-start | bytes 393224 | tf_op jit(solution)/shard_map/ppermute | solution.py:135
  172.2 6.5 %collective-permute-start.35 = (bf16[32,16,128]{2,1,0:T(8,128)(2,1)S(1)}, bf16[32,16,128]{2,1,0:T(8,128)(2,1)S(1)}, u32[]{:S(2)}, u32[]{:S(2)}) collective-permute-start(bf16[32,16,128]{2,1,0:T(8,128)(2,1)S(1)} %get-tuple-element.89.refs_0_), channel_id=1, source_target_pairs={{0,2},{2,0},{4,6},{6,4},{8,10},{10,8},{12,14},{14,12},{1,3},{3,1},... | collective-permute-start | bytes 393224 | tf_op jit(solution)/shard_map/ppermute | solution.py:135
  180.9 1.6 collective-permute-start.38
  186.0 6.8 %collective-permute-start.39 = (bf16[32,16,128]{2,1,0:T(8,128)(2,1)S(1)}, bf16[32,16,128]{2,1,0:T(8,128)(2,1)S(1)}, u32[]{:S(2)}, u32[]{:S(2)}) collective-permute-start(bf16[32,16,128]{2,1,0:T(8,128)(2,1)S(1)} %get-tuple-element.92), channel_id=1, source_target_pairs={{0,2},{2,0},{4,6},{6,4},{8,10},{10,8},{12,14},{14,12},{1,3},{3,1},... | collective-permute-start | bytes 393224 | tf_op jit(solution)/shard_map/ppermute | solution.py:135
  187.0 8.3 %collective-permute-start.40 = (bf16[32,16,128]{2,1,0:T(8,128)(2,1)S(1)}, bf16[32,16,128]{2,1,0:T(8,128)(2,1)S(1)}, u32[]{:S(2)}, u32[]{:S(2)}) collective-permute-start(bf16[32,16,128]{2,1,0:T(8,128)(2,1)S(1)} %get-tuple-element.93), channel_id=1, source_target_pairs={{0,4},{2,6},{4,0},{6,2},{8,12},{10,14},{12,8},{14,10},{1,5},{3,7},... | collective-permute-start | bytes 393224 | tf_op jit(solution)/shard_map/ppermute | solution.py:135
  191.6 7.7 %collective-permute-start.41 = (bf16[32,16,128]{2,1,0:T(8,128)(2,1)S(1)}, bf16[32,16,128]{2,1,0:T(8,128)(2,1)S(1)}, u32[]{:S(2)}, u32[]{:S(2)}) collective-permute-start(bf16[32,16,128]{2,1,0:T(8,128)(2,1)S(1)} %get-tuple-element.94), channel_id=1, source_target_pairs={{0,6},{2,4},{4,2},{6,0},{8,14},{10,12},{12,10},{14,8},{1,7},{3,5},... | collective-permute-start | bytes 393224 | tf_op jit(solution)/shard_map/ppermute | solution.py:135
  199.4 6.4 %collective-permute-start.42 = (bf16[32,16,128]{2,1,0:T(8,128)(2,1)S(1)}, bf16[32,16,128]{2,1,0:T(8,128)(2,1)S(1)}, u32[]{:S(2)}, u32[]{:S(2)}) collective-permute-start(bf16[32,16,128]{2,1,0:T(8,128)(2,1)S(1)} %get-tuple-element.96), channel_id=1, source_target_pairs={{0,8},{2,10},{4,12},{6,14},{8,0},{10,2},{12,4},{14,6},{1,9},{3,11}... | collective-permute-start | bytes 393224 | tf_op jit(solution)/shard_map/ppermute | solution.py:135
  205.9 8.6 %collective-permute-start.45 = (bf16[32,16,128]{2,1,0:T(8,128)(2,1)S(1)}, bf16[32,16,128]{2,1,0:T(8,128)(2,1)S(1)}, u32[]{:S(2)}, u32[]{:S(2)}) collective-permute-start(bf16[32,16,128]{2,1,0:T(8,128)(2,1)S(1)} %get-tuple-element.97.refs_0_), channel_id=1, source_target_pairs={{0,6},{2,4},{4,2},{6,0},{8,14},{10,12},{12,10},{14,8},{1,7},{3,5},... | collective-permute-start | bytes 393224 | tf_op jit(solution)/shard_map/ppermute | solution.py:135
  210.2 5.8 %collective-permute-start.44 = (bf16[32,16,128]{2,1,0:T(8,128)(2,1)S(1)}, bf16[32,16,128]{2,1,0:T(8,128)(2,1)S(1)}, u32[]{:S(2)}, u32[]{:S(2)}) collective-permute-start(bf16[32,16,128]{2,1,0:T(8,128)(2,1)S(1)} %get-tuple-element.97.refs_0_), channel_id=1, source_target_pairs={{0,4},{2,6},{4,0},{6,2},{8,12},{10,14},{12,8},{14,10},{1,5},{3,7},... | collective-permute-start | bytes 393224 | tf_op jit(solution)/shard_map/ppermute | solution.py:135
  210.2 6.5 %collective-permute-start.43 = (bf16[32,16,128]{2,1,0:T(8,128)(2,1)S(1)}, bf16[32,16,128]{2,1,0:T(8,128)(2,1)S(1)}, u32[]{:S(2)}, u32[]{:S(2)}) collective-permute-start(bf16[32,16,128]{2,1,0:T(8,128)(2,1)S(1)} %get-tuple-element.97.refs_0_), channel_id=1, source_target_pairs={{0,2},{2,0},{4,6},{6,4},{8,10},{10,8},{12,14},{14,12},{1,3},{3,1},... | collective-permute-start | bytes 393224 | tf_op jit(solution)/shard_map/ppermute | solution.py:135
  218.9 1.6 collective-permute-start.46
  224.0 6.5 %collective-permute-start.47 = (bf16[32,16,128]{2,1,0:T(8,128)(2,1)S(1)}, bf16[32,16,128]{2,1,0:T(8,128)(2,1)S(1)}, u32[]{:S(2)}, u32[]{:S(2)}) collective-permute-start(bf16[32,16,128]{2,1,0:T(8,128)(2,1)S(1)} %get-tuple-element.102), channel_id=1, source_target_pairs={{0,2},{2,0},{4,6},{6,4},{8,10},{10,8},{12,14},{14,12},{1,3},{3,1},... | collective-permute-start | bytes 393224 | tf_op jit(solution)/shard_map/ppermute | solution.py:135
  224.7 8.7 %collective-permute-start.48 = (bf16[32,16,128]{2,1,0:T(8,128)(2,1)S(1)}, bf16[32,16,128]{2,1,0:T(8,128)(2,1)S(1)}, u32[]{:S(2)}, u32[]{:S(2)}) collective-permute-start(bf16[32,16,128]{2,1,0:T(8,128)(2,1)S(1)} %get-tuple-element.103), channel_id=1, source_target_pairs={{0,4},{2,6},{4,0},{6,2},{8,12},{10,14},{12,8},{14,10},{1,5},{3,7},... | collective-permute-start | bytes 393224 | tf_op jit(solution)/shard_map/ppermute | solution.py:135
  229.7 7.7 %collective-permute-start.49 = (bf16[32,16,128]{2,1,0:T(8,128)(2,1)S(1)}, bf16[32,16,128]{2,1,0:T(8,128)(2,1)S(1)}, u32[]{:S(2)}, u32[]{:S(2)}) collective-permute-start(bf16[32,16,128]{2,1,0:T(8,128)(2,1)S(1)} %get-tuple-element.104), channel_id=1, source_target_pairs={{0,6},{2,4},{4,2},{6,0},{8,14},{10,12},{12,10},{14,8},{1,7},{3,5},... | collective-permute-start | bytes 393224 | tf_op jit(solution)/shard_map/ppermute | solution.py:135
  237.4 5.2 %collective-permute-start.50 = (bf16[16,16,128]{2,1,0:T(8,128)(2,1)S(1)}, bf16[16,16,128]{2,1,0:T(8,128)(2,1)S(1)}, u32[]{:S(2)}, u32[]{:S(2)}) collective-permute-start(bf16[16,16,128]{2,1,0:T(8,128)(2,1)S(1)} %get-tuple-element.106), channel_id=1, source_target_pairs={{0,8},{2,10},{4,12},{6,14},{8,0},{10,2},{12,4},{14,6},{1,9},{3,11}... | collective-permute-start | bytes 196616 | tf_op jit(solution)/shard_map/ppermute | solution.py:135

commit v3 on v2

--- a/solution.py
+++ b/solution.py
@@ -9,7 +9,7 @@
 
 BS = 128
 ITERS = 6
-UNROLL = 32
+WIDE, NARROW = 32, 8
 NN = (((1,), (0,)), ((), ()))
 NT = (((1,), (1,)), ((), ()))
 
@@ -18,39 +18,143 @@
 PARAMS = pltpu.CompilerParams(vmem_limit_bytes=24 * 2**20)
 
 
-def products(groups, src, dst, vecs, blocks, acc, dims):
-    def group(g, _):
-        first = g * UNROLL
-        terms = [
-            lax.dot_general(vecs[src[first + u]], blocks[first + u], dims, preferred_element_type=jnp.float32)
-            for u in range(UNROLL)
-        ]
-        for u in range(UNROLL):
-            acc[dst[first + u]] += terms[u]
+class Plan:
+    def __init__(self, ref, slots, columns):
+        self.ref = ref
+        self.pairs = plan_pairs(slots, columns)
+
+    def slot(self, i):
+        return 8 + i
+
+    def row(self, i):
+        return 8 + 2 * self.pairs + i
+
+    def col(self, pair):
+        return 8 + 4 * self.pairs + pair
+
+
+def plan_pairs(slots, columns):
+    return -(-(slots + columns) // (2 * NARROW)) * NARROW
+
+
+def prepare_kernel(columns, rows, place, brow, bcol, blocks, plan_ref, tile, ends, sem):
+    copy = pltpu.make_async_copy(blocks, tile, sem)
+    copy.start()
+    count, row_flip, col_flip = place[0], place[1], place[2]
+    plan = Plan(plan_ref, brow.shape[0], columns)
+
+    for c in range(columns + 1):
+        ends[c] = 0
+
+    def column(n):
+        return jnp.where(n < count, bcol[n] ^ col_flip, columns)
+
+    def tally(n, _):
+        c = column(n)
+        ends[c] = ends[c] + 1
         return 0
 
-    lax.fori_loop(0, groups, group, 0)
-
-
-def backward_kernel(groups, src, dst, blocks, *refs):
-    pieces, (grad, vecs, acc) = refs[:-3], refs[-3:]
+    lax.fori_loop(0, brow.shape[0], tally, 0, unroll=16)
+
+    def fill(at):
+        plan_ref[plan.slot(at)] = 0
+        plan_ref[plan.row(at)] = rows
+        plan_ref[plan.col(at // 2)] = 0
+
+    start = jnp.int32(0)
+    for c in range(columns):
+        size = ends[c]
+        ends[c] = start
+        fill(start + size)
+        start = start + ((size + 1) // 2) * 2
+    size = ends[columns]
+    ends[columns] = start
+    plan_ref[0] = start // 2
+    for i in range(columns):
+        fill(jnp.minimum(start + size + i, 2 * plan.pairs - 1))
+
+    def put(n, _):
+        c = column(n)
+        at = ends[c]
+        ends[c] = at + 1
+        plan_ref[plan.slot(at)] = n
+        plan_ref[plan.row(at)] = jnp.where(n < count, brow[n] ^ row_flip, rows)
+        plan_ref[plan.col(at // 2)] = jnp.where(n < count, c, 0)
+        return 0
+
+    lax.fori_loop(0, brow.shape[0], put, 0, unroll=16)
+    copy.wait()
+
+
+def over_pairs(pairs, step):
+    wide = pairs // WIDE
+
+    def run(i, _, size, start):
+        step(start + i * size, size)
+        return 0
+
+    lax.fori_loop(0, wide, functools.partial(run, size=WIDE, start=0), 0)
+    rest = wide * WIDE
+    lax.fori_loop(0, (pairs - rest + NARROW - 1) // NARROW, functools.partial(run, size=NARROW, start=rest), 0)
+
+
+def transposed_products(plan_ref, tile, vecs, acc):
+    plan = Plan(plan_ref, tile.shape[0], acc.shape[0])
+
+    def step(first, n):
+        terms = []
+        for u in range(n):
+            i = 2 * (first + u)
+            left = [vecs[plan_ref[plan.row(i + k)]] for k in range(2)]
+            right = [tile[plan_ref[plan.slot(i + k)]] for k in range(2)]
+            terms.append(
+                lax.dot_general(
+                    jnp.concatenate(left, axis=1), jnp.concatenate(right, axis=0), NN, preferred_element_type=jnp.float32
+                )
+            )
+        for u in range(n):
+            acc[plan_ref[plan.col(first + u)]] += terms[u]
+
+    acc[...] = jnp.zeros(acc.shape, acc.dtype)
+    over_pairs(plan_ref[0], step)
+
+
+def products(plan_ref, tile, vecs, acc):
+    plan = Plan(plan_ref, tile.shape[0], vecs.shape[0])
+
+    def step(first, n):
+        terms = []
+        for u in range(n):
+            i = 2 * (first + u)
+            right = [tile[plan_ref[plan.slot(i + k)]] for k in range(2)]
+            terms.append(
+                lax.dot_general(
+                    vecs[plan_ref[plan.col(first + u)]],
+                    jnp.concatenate(right, axis=0),
+                    NT,
+                    preferred_element_type=jnp.float32,
+                )
+            )
+        for u in range(n):
+            for k in range(2):
+                acc[plan_ref[plan.row(2 * (first + u) + k)]] += terms[u][:, k * BS : (k + 1) * BS]
+
+    acc[...] = jnp.zeros(acc.shape, acc.dtype)
+    over_pairs(plan_ref[0], step)
+
+
+def backward_kernel(plan, tile, *refs):
+    pieces, (grad, vecs) = refs[:-2], refs[-2:]
     half = len(pieces)
     span = pieces[0].shape[0] // 2
     for m in range(half):
         vecs[pl.ds(m * span, span)] = pieces[m][pl.ds(0, span)]
         vecs[pl.ds((m + half) * span, span)] = pieces[m][pl.ds(span, span)]
-    acc[...] = jnp.zeros(acc.shape, acc.dtype)
-    products(groups[0], src, dst, vecs, blocks, acc, NN)
-    grad[...] = acc[pl.ds(0, grad.shape[0])]
-
-
-def whole_backward_kernel(groups, src, dst, blocks, vecs, grad, acc):
-    acc[...] = jnp.zeros(acc.shape, acc.dtype)
-    products(groups[0], src, dst, vecs, blocks, acc, NN)
-    grad[...] = acc[pl.ds(0, grad.shape[0])]
-
-
-def forward_kernel(groups, src, dst, blocks, own, other, x_ref, cost, kind, upper, *refs):
+    vecs[2 * half * span] = jnp.zeros(vecs.shape[1:], vecs.dtype)
+    transposed_products(plan, tile, vecs, grad)
+
+
+def forward_kernel(plan, tile, own, other, x_ref, cost, kind, upper, *refs):
     x_out, pieces, (vecs, acc) = refs[0], refs[1:-2], refs[-2:]
     cols = x_ref.shape[0] // 2
     for h in range(2):
@@ -61,8 +165,7 @@
         x_next = jnp.where(kind[here] == 1, jnp.minimum(lifted, upper[here]), lifted)
         x_out[here] = x_next
         vecs[here] = (2.0 * x_next - x).astype(vecs.dtype)
-    acc[...] = jnp.zeros(acc.shape, acc.dtype)
-    products(groups[0], src, dst, vecs, blocks, acc, NT)
+    products(plan, tile, vecs, acc)
     half = len(pieces)
     span = pieces[0].shape[0] // 2
     for m in range(half):
@@ -115,18 +218,22 @@
     direct = n_col in (4, 8) and span & (span - 1) == 0
     half = n_col // 2
 
-    tile = kblocks[0, 0]
-    slots = jnp.arange(tile.shape[0], dtype=jnp.int32)
-    count = block_count[0, 0]
-    live = slots < count
-    groups = ((count + UNROLL - 1) // UNROLL).reshape(1)
-    mine = block_col[0, 0] // cols == lax.axis_index("row")
-    bcol = jnp.where(mine, 0, cols) + block_col[0, 0] % cols
-    brow = block_row[0, 0]
-    if direct:
-        brow = brow ^ (lax.axis_index("col") * span)
-    to_col = jnp.where(live, bcol, col_blocks)
-    to_row = jnp.where(live, brow, row_blocks)
+    blocks = kblocks[0, 0]
+    slots = blocks.shape[0]
+    row_flip = lax.axis_index("col") * span if direct else 0
+    place = jnp.stack([block_count[0, 0], row_flip, lax.axis_index("row") * cols]).astype(jnp.int32)
+    plan, tile = pl.pallas_call(
+        functools.partial(prepare_kernel, col_blocks, row_blocks),
+        out_shape=(
+            jax.ShapeDtypeStruct((8 + 5 * plan_pairs(slots, col_blocks),), jnp.int32),
+            pltpu.VMEM(blocks.shape, blocks.dtype),
+        ),
+        in_specs=[SMEM] * 3 + [pl.BlockSpec(memory_space=pltpu.HBM)],
+        out_specs=(SMEM, VMEM),
+        scratch_shapes=[pltpu.SMEM((col_blocks + 1,), jnp.int32), pltpu.SemaphoreType.DMA],
+        compiler_params=PARAMS,
+        name="prepare_kernel",
+    )(place, block_row[0, 0], block_col[0, 0], pltpu.with_memory_space_constraint(blocks, pltpu.HBM))
 
     def swap(a):
         return lax.ppermute(a, "row", [(i, n_row - 1 - i) for i in range(n_row)])
@@ -142,9 +249,6 @@
     rhs_all = to_blocks(rhs[:, 0])
     if direct:
         y_half = jnp.concatenate([y_half, partner(y_half, half)])
-        pair = jnp.stack([y, rhs_all])
-        both = jnp.concatenate([pair, partner(pair, half)], axis=1)
-        y, rhs_all = both[0], both[1]
 
     own = jnp.concatenate(
         [to_blocks(primal[:, 0]), to_blocks(cost[:, 0]), to_blocks(upper), to_blocks(bound_kind).astype(jnp.float32)],
@@ -169,30 +273,25 @@
         )
 
     f32, bf16 = jnp.float32, jnp.bfloat16
-    backward = call(
-        backward_kernel if direct else whole_backward_kernel,
-        (shape(col_blocks, f32),),
-        1 + (half if direct else 1),
-        ((row_blocks, bf16), (col_blocks + 1, f32)) if direct else ((col_blocks + 1, f32),),
-        3,
-    )
     if direct:
+        backward = call(backward_kernel, (shape(col_blocks, f32),), 1 + half, ((row_blocks + 1, bf16),), 1)
         pieces = (shape(2 * span, f32),) + (shape(2 * span, bf16),) * (half - 1)
     else:
+        backward = call(backward_kernel, (shape(col_blocks, f32),), 2, ((row_blocks + 1, bf16),), 1)
         pieces = (shape(row_blocks, f32),)
     forward = call(
-        forward_kernel,
-        (shape(col_blocks, f32),) + pieces,
-        7,
-        ((col_blocks, bf16), (row_blocks + 1, f32)),
-        3,
+        forward_kernel, (shape(col_blocks, f32),) + pieces, 7, ((col_blocks, bf16), (row_blocks + 1, f32)), 1
     )
 
     for step in range(ITERS):
         last = step == ITERS - 1
         y_slab = [y_half] + near(y_half) if direct else [lax.all_gather(y_half, "col", axis=0, tiled=True)]
-        (grad,) = backward(groups, brow, to_col, tile, *y_slab)
-        x, *image = forward(groups, bcol, to_row, tile, grad, swap(grad), x, cost_all, kind_all, upper_all)
+        if direct and step == 0:
+            pair, *y_slab = lax.optimization_barrier([jnp.stack([y, rhs_all])] + y_slab)
+            both = jnp.concatenate([pair, partner(pair, half)], axis=1)
+            y, rhs_all = both[0], both[1]
+        (grad,) = backward(plan, tile, *y_slab)
+        x, *image = forward(plan, tile, grad, swap(grad), x, cost_all, kind_all, upper_all)
         if direct:
             image = image[:1] + [partner(image[m], m) for m in range(1, half)]
             kept = 1 if last else 2

time: 248 us -> 221 us (0.89); the launches traced: 244 us -> 221 us
  waiting for transfers between devices: 119 us -> 105 us
  Pallas kernels: 35.7 us -> 30.7 us
  local copies, waits for them, and re-layouts: 8.77 us -> 5.93 us
    ppermute x44, waiting for transfers between devices: 111 us -> 98.1 us  [partner(): return lax.ppermute(a, 'col', [(i, i ^ m) for i in range(n_col)])]
    pallas_call x12 -> x13, Pallas kernels: 34.3 us -> 29.3 us  [the longest x6 13.9 us: per_device(): forward(plan, tile, grad, swap(grad), x, cost_all, kind_all, upper_all)]
    ppermute x44, starting transfers between devices: 74.3 us -> 71.7 us  [partner(): return lax.ppermute(a, 'col', [(i, i ^ m) for i in range(n_col)])]
  transfers between devices with their start and end apart: 51 -> 51, of which waited for: 42 -> 41; matrix products, arithmetic and copies ran while one was open for 3% -> 2% of each run, Pallas kernels for 2% -> 4%
where the time goes in v3:
time: 221 us
  waiting for transfers between devices  105 us (48%)
  starting transfers between devices  75.7 us (34%)
  Pallas kernels  30.7 us (14%)
  local copies, waits for them, and re-layouts  5.93 us (3%)
    ppermute x44, waiting for transfers between devices, partner(): return lax.ppermute(a, 'col', [(i, i ^ m) for i in range(n_col)])  98.1 us
    ppermute x44, starting transfers between devices, partner(): return lax.ppermute(a, 'col', [(i, i ^ m) for i in range(n_col)])  71.7 us
    pallas_call x6, Pallas kernels, per_device(): forward(plan, tile, grad, swap(grad), x, cost_all, kind_all, upper_all)  13.9 us
    pallas_call x6, Pallas kernels, per_device(): grad, = backward(plan, tile, *y_slab)  9.67 us
    ppermute x7, waiting for transfers between devices, swap(): return lax.ppermute(a, 'row', [(i, n_row - 1 - i) for i in range(n_row)])  7.17 us
    pallas_call x1, Pallas kernels, per_device(): pl.pallas_call(functools.partial(prepare_kernel, col_blocks, row_blocks),...  5.7 us
  transfers between devices with their start and end apart: 51, of which 41 were waited for; matrix products, arithmetic and copies ran while one was open for 2% of the time, Pallas kernels for 4%

profile of v3, /device:TPU:10, one launch (start us, length us, event | category | flops | bytes accessed | tf_op | source)
XLA Modules:
  0.0 220.8 jit_solution(1737554634325153105)
XLA Ops:
  1.6 2.7 %collective-permute-start = (bf16[16,16,128]{2,1,0:T(8,128)(2,1)S(1)}, bf16[16,16,128]{2,1,0:T(8,128)(2,1)S(1)}, u32[]{:S(2)}, u32[]{:S(2)}) collective-permute-start(bf16[16,16,128]{2,1,0:T(8,128)(2,1)S(1)} %bitcast.43), channel_id=1, source_target_pairs={{0,8},{2,10},{4,12},{6,14},{8,0},{10,2},{12,4},{14,6},{1,9},{3,11}... | collective-permute-start | bytes 196616 | tf_op jit(solution)/shard_map/ppermute | solution.py:242
  13.5 5.7 %prepare_kernel.1 = (s32[728]{0:T(1024)S(1)}, bf16[256,128,128]{2,1,0:T(8,128)(2,1)S(1)}) custom-call(s32[3]{0:T(128)S(1)} %pad_add_fusion.place, s32[256]{0:T(256)S(1)} %bitcast.38, s32[256]{0:T(256)S(1)} %bitcast.39, bf16[256,128,128]{2,1,0:T(8,128)(2,1)} %bitcast.40), custom_call_target="tpu_custom_call" | custom-call | tf_op jit(solution)/shard_map/prepare_kernel/pallas_call | solution.py:225
  19.3 1.8 collective-permute-start.4
  21.1 1.6 backward_kernel.6.own
  24.3 2.3 %forward_kernel.6 = (f32[32,16,128]{2,1,0:T(8,128)S(1)}, f32[32,16,128]{2,1,0:T(8,128)S(1)}, bf16[32,16,128]{2,1,0:T(8,128)(2,1)S(1)}, bf16[32,16,128]{2,1,0:T(8,128)(2,1)S(1)}, bf16[32,16,128]{2,1,0:T(8,128)(2,1)S(1)}) custom-call(s32[728]{0:T(1024)S(1)} %get-tuple-element.62.plan, bf16[256,128,128]{2,1,0:T(8,128)(2,1)S(1)} %get-tuple-element.63.tile, ...), custom_call_target="tpu_custom_call" | custom-call | tf_op jit(solution)/shard_map/forward_kernel/pallas_call | solution.py:294
  26.6 3.3 %collective-permute-start.7 = (bf16[32,16,128]{2,1,0:T(8,128)(2,1)S(1)}, bf16[32,16,128]{2,1,0:T(8,128)(2,1)S(1)}, u32[]{:S(2)}, u32[]{:S(2)}) collective-permute-start(bf16[32,16,128]{2,1,0:T(8,128)(2,1)S(1)} %get-tuple-element.70), channel_id=1, source_target_pairs={{0,2},{2,0},{4,6},{6,4},{8,10},{10,8},{12,14},{14,12},{1,3},{3,1},... | collective-permute-start | bytes 393224 | tf_op jit(solution)/shard_map/ppermute | solution.py:242
  31.6 2.6 %collective-permute-done.7.refs_0_ = bf16[32,16,128]{2,1,0:T(8,128)(2,1)S(1)} collective-permute-done((bf16[32,16,128]{2,1,0:T(8,128)(2,1)S(1)}, bf16[32,16,128]{2,1,0:T(8,128)(2,1)S(1)}, u32[]{:S(2)}, u32[]{:S(2)}) %collective-permute-start.7) | collective-permute-done | bytes 131104 | tf_op jit(solution)/shard_map/ppermute | solution.py:242
  34.2 2.1 collective-permute-done.8.refs_1_
  36.3 1.9 collective-permute-done.9.refs_2_
  38.3 2.8 %collective-permute-start.10 = (bf16[32,16,128]{2,1,0:T(8,128)(2,1)S(1)}, bf16[32,16,128]{2,1,0:T(8,128)(2,1)S(1)}, u32[]{:S(2)}, u32[]{:S(2)}) collective-permute-start(bf16[32,16,128]{2,1,0:T(8,128)(2,1)S(1)} %get-tuple-element.74), channel_id=1, source_target_pairs={{0,8},{2,10},{4,12},{6,14},{8,0},{10,2},{12,4},{14,6},{1,9},{3,11}... | collective-permute-start | bytes 393224 | tf_op jit(solution)/shard_map/ppermute | solution.py:242
  41.1 5.3 %collective-permute-done.10.far = bf16[32,16,128]{2,1,0:T(8,128)(2,1)S(1)} collective-permute-done((bf16[32,16,128]{2,1,0:T(8,128)(2,1)S(1)}, bf16[32,16,128]{2,1,0:T(8,128)(2,1)S(1)}, u32[]{:S(2)}, u32[]{:S(2)}) %collective-permute-start.10) | collective-permute-done | bytes 131104 | tf_op jit(solution)/shard_map/ppermute | solution.py:242
  46.4 3.2 %collective-permute-start.13 = (bf16[32,16,128]{2,1,0:T(8,128)(2,1)S(1)}, bf16[32,16,128]{2,1,0:T(8,128)(2,1)S(1)}, u32[]{:S(2)}, u32[]{:S(2)}) collective-permute-start(bf16[32,16,128]{2,1,0:T(8,128)(2,1)S(1)} %get-tuple-element.76.refs_0_), channel_id=1, source_target_pairs={{0,6},{2,4},{4,2},{6,0},{8,14},{10,12},{12,10},{14,8},{1,7},{3,5},... | collective-permute-start | bytes 393224 | tf_op jit(solution)/shard_map/ppermute | solution.py:242
  50.7 3.2 %collective-permute-done.13.refs_3_ = bf16[32,16,128]{2,1,0:T(8,128)(2,1)S(1)} collective-permute-done((bf16[32,16,128]{2,1,0:T(8,128)(2,1)S(1)}, bf16[32,16,128]{2,1,0:T(8,128)(2,1)S(1)}, u32[]{:S(2)}, u32[]{:S(2)}) %collective-permute-start.13) | collective-permute-done | bytes 131104 | tf_op jit(solution)/shard_map/ppermute | solution.py:242
  53.9 1.8 collective-permute-done.12.refs_2_
  56.1 1.6 backward_kernel.7.own
  59.7 2.3 %forward_kernel.7 = (f32[32,16,128]{2,1,0:T(8,128)S(1)}, f32[32,16,128]{2,1,0:T(8,128)S(1)}, bf16[32,16,128]{2,1,0:T(8,128)(2,1)S(1)}, bf16[32,16,128]{2,1,0:T(8,128)(2,1)S(1)}, bf16[32,16,128]{2,1,0:T(8,128)(2,1)S(1)}) custom-call(s32[728]{0:T(1024)S(1)} %get-tuple-element.62.plan, bf16[256,128,128]{2,1,0:T(8,128)(2,1)S(1)} %get-tuple-element.63.tile, ...), custom_call_target="tpu_custom_call" | custom-call | tf_op jit(solution)/shard_map/forward_kernel/pallas_call | solution.py:294
  62.0 2.6 %collective-permute-start.15 = (bf16[32,16,128]{2,1,0:T(8,128)(2,1)S(1)}, bf16[32,16,128]{2,1,0:T(8,128)(2,1)S(1)}, u32[]{:S(2)}, u32[]{:S(2)}) collective-permute-start(bf16[32,16,128]{2,1,0:T(8,128)(2,1)S(1)} %get-tuple-element.79), channel_id=1, source_target_pairs={{0,2},{2,0},{4,6},{6,4},{8,10},{10,8},{12,14},{14,12},{1,3},{3,1},... | collective-permute-start | bytes 393224 | tf_op jit(solution)/shard_map/ppermute | solution.py:242
  64.5 3.0 %collective-permute-start.16 = (bf16[32,16,128]{2,1,0:T(8,128)(2,1)S(1)}, bf16[32,16,128]{2,1,0:T(8,128)(2,1)S(1)}, u32[]{:S(2)}, u32[]{:S(2)}) collective-permute-start(bf16[32,16,128]{2,1,0:T(8,128)(2,1)S(1)} %get-tuple-element.80), channel_id=1, source_target_pairs={{0,4},{2,6},{4,0},{6,2},{8,12},{10,14},{12,8},{14,10},{1,5},{3,7},... | collective-permute-start | bytes 393224 | tf_op jit(solution)/shard_map/ppermute | solution.py:242
  68.6 2.4 %collective-permute-done.16.refs_1_ = bf16[32,16,128]{2,1,0:T(8,128)(2,1)S(1)} collective-permute-done((bf16[32,16,128]{2,1,0:T(8,128)(2,1)S(1)}, bf16[32,16,128]{2,1,0:T(8,128)(2,1)S(1)}, u32[]{:S(2)}, u32[]{:S(2)}) %collective-permute-start.16) | collective-permute-done | bytes 131104 | tf_op jit(solution)/shard_map/ppermute | solution.py:242
  71.0 3.2 %collective-permute-done.17.refs_2_ = bf16[32,16,128]{2,1,0:T(8,128)(2,1)S(1)} collective-permute-done((bf16[32,16,128]{2,1,0:T(8,128)(2,1)S(1)}, bf16[32,16,128]{2,1,0:T(8,128)(2,1)S(1)}, u32[]{:S(2)}, u32[]{:S(2)}) %collective-permute-start.17) | collective-permute-done | bytes 131104 | tf_op jit(solution)/shard_map/ppermute | solution.py:242
  75.4 6.1 %collective-permute-done.18.far = bf16[32,16,128]{2,1,0:T(8,128)(2,1)S(1)} collective-permute-done((bf16[32,16,128]{2,1,0:T(8,128)(2,1)S(1)}, bf16[32,16,128]{2,1,0:T(8,128)(2,1)S(1)}, u32[]{:S(2)}, u32[]{:S(2)}) %collective-permute-start.18) | collective-permute-done | bytes 131104 | tf_op jit(solution)/shard_map/ppermute | solution.py:242
  81.6 1.8 collective-permute-start.21
  86.0 2.2 collective-permute-done.21.refs_3_
  88.1 2.8 %collective-permute-done.20.refs_2_ = bf16[32,16,128]{2,1,0:T(8,128)(2,1)S(1)} collective-permute-done((bf16[32,16,128]{2,1,0:T(8,128)(2,1)S(1)}, bf16[32,16,128]{2,1,0:T(8,128)(2,1)S(1)}, u32[]{:S(2)}, u32[]{:S(2)}) %collective-permute-start.20) | collective-permute-done | bytes 131104 | tf_op jit(solution)/shard_map/ppermute | solution.py:242
  91.0 1.6 backward_kernel.8.own
  94.4 2.3 %forward_kernel.8 = (f32[32,16,128]{2,1,0:T(8,128)S(1)}, f32[32,16,128]{2,1,0:T(8,128)S(1)}, bf16[32,16,128]{2,1,0:T(8,128)(2,1)S(1)}, bf16[32,16,128]{2,1,0:T(8,128)(2,1)S(1)}, bf16[32,16,128]{2,1,0:T(8,128)(2,1)S(1)}) custom-call(s32[728]{0:T(1024)S(1)} %get-tuple-element.62.plan, bf16[256,128,128]{2,1,0:T(8,128)(2,1)S(1)} %get-tuple-element.63.tile, ...), custom_call_target="tpu_custom_call" | custom-call | tf_op jit(solution)/shard_map/forward_kernel/pallas_call | solution.py:294
  96.7 3.1 %collective-permute-start.23 = (bf16[32,16,128]{2,1,0:T(8,128)(2,1)S(1)}, bf16[32,16,128]{2,1,0:T(8,128)(2,1)S(1)}, u32[]{:S(2)}, u32[]{:S(2)}) collective-permute-start(bf16[32,16,128]{2,1,0:T(8,128)(2,1)S(1)} %get-tuple-element.88), channel_id=1, source_target_pairs={{0,2},{2,0},{4,6},{6,4},{8,10},{10,8},{12,14},{14,12},{1,3},{3,1},... | collective-permute-start | bytes 393224 | tf_op jit(solution)/shard_map/ppermute | solution.py:242
  99.8 2.7 %collective-permute-start.24 = (bf16[32,16,128]{2,1,0:T(8,128)(2,1)S(1)}, bf16[32,16,128]{2,1,0:T(8,128)(2,1)S(1)}, u32[]{:S(2)}, u32[]{:S(2)}) collective-permute-start(bf16[32,16,128]{2,1,0:T(8,128)(2,1)S(1)} %get-tuple-element.89), channel_id=1, source_target_pairs={{0,4},{2,6},{4,0},{6,2},{8,12},{10,14},{12,8},{14,10},{1,5},{3,7},... | collective-permute-start | bytes 393224 | tf_op jit(solution)/shard_map/ppermute | solution.py:242
  104.0 2.4 %collective-permute-done.24.refs_1_ = bf16[32,16,128]{2,1,0:T(8,128)(2,1)S(1)} collective-permute-done((bf16[32,16,128]{2,1,0:T(8,128)(2,1)S(1)}, bf16[32,16,128]{2,1,0:T(8,128)(2,1)S(1)}, u32[]{:S(2)}, u32[]{:S(2)}) %collective-permute-start.24) | collective-permute-done | bytes 131104 | tf_op jit(solution)/shard_map/ppermute | solution.py:242
  106.4 2.7 %collective-permute-done.25.refs_2_ = bf16[32,16,128]{2,1,0:T(8,128)(2,1)S(1)} collective-permute-done((bf16[32,16,128]{2,1,0:T(8,128)(2,1)S(1)}, bf16[32,16,128]{2,1,0:T(8,128)(2,1)S(1)}, u32[]{:S(2)}, u32[]{:S(2)}) %collective-permute-start.25) | collective-permute-done | bytes 131104 | tf_op jit(solution)/shard_map/ppermute | solution.py:242
  110.5 6.1 %collective-permute-done.26.far = bf16[32,16,128]{2,1,0:T(8,128)(2,1)S(1)} collective-permute-done((bf16[32,16,128]{2,1,0:T(8,128)(2,1)S(1)}, bf16[32,16,128]{2,1,0:T(8,128)(2,1)S(1)}, u32[]{:S(2)}, u32[]{:S(2)}) %collective-permute-start.26) | collective-permute-done | bytes 131104 | tf_op jit(solution)/shard_map/ppermute | solution.py:242
  116.6 2.8 %collective-permute-start.29 = (bf16[32,16,128]{2,1,0:T(8,128)(2,1)S(1)}, bf16[32,16,128]{2,1,0:T(8,128)(2,1)S(1)}, u32[]{:S(2)}, u32[]{:S(2)}) collective-permute-start(bf16[32,16,128]{2,1,0:T(8,128)(2,1)S(1)} %get-tuple-element.94.refs_0_), channel_id=1, source_target_pairs={{0,6},{2,4},{4,2},{6,0},{8,14},{10,12},{12,10},{14,8},{1,7},{3,5},... | collective-permute-start | bytes 393224 | tf_op jit(solution)/shard_map/ppermute | solution.py:242
  120.9 2.5 %collective-permute-done.29.refs_3_ = bf16[32,16,128]{2,1,0:T(8,128)(2,1)S(1)} collective-permute-done((bf16[32,16,128]{2,1,0:T(8,128)(2,1)S(1)}, bf16[32,16,128]{2,1,0:T(8,128)(2,1)S(1)}, u32[]{:S(2)}, u32[]{:S(2)}) %collective-permute-start.29) | collective-permute-done | bytes 131104 | tf_op jit(solution)/shard_map/ppermute | solution.py:242
  123.4 2.5 %collective-permute-done.28.refs_2_ = bf16[32,16,128]{2,1,0:T(8,128)(2,1)S(1)} collective-permute-done((bf16[32,16,128]{2,1,0:T(8,128)(2,1)S(1)}, bf16[32,16,128]{2,1,0:T(8,128)(2,1)S(1)}, u32[]{:S(2)}, u32[]{:S(2)}) %collective-permute-start.28) | collective-permute-done | bytes 131104 | tf_op jit(solution)/shard_map/ppermute | solution.py:242
  125.9 1.6 backward_kernel.9.own
  129.5 2.3 %forward_kernel.9 = (f32[32,16,128]{2,1,0:T(8,128)S(1)}, f32[32,16,128]{2,1,0:T(8,128)S(1)}, bf16[32,16,128]{2,1,0:T(8,128)(2,1)S(1)}, bf16[32,16,128]{2,1,0:T(8,128)(2,1)S(1)}, bf16[32,16,128]{2,1,0:T(8,128)(2,1)S(1)}) custom-call(s32[728]{0:T(1024)S(1)} %get-tuple-element.62.plan, bf16[256,128,128]{2,1,0:T(8,128)(2,1)S(1)} %get-tuple-element.63.tile, ...), custom_call_target="tpu_custom_call" | custom-call | tf_op jit(solution)/shard_map/forward_kernel/pallas_call | solution.py:294
  131.8 2.9 %collective-permute-start.31 = (bf16[32,16,128]{2,1,0:T(8,128)(2,1)S(1)}, bf16[32,16,128]{2,1,0:T(8,128)(2,1)S(1)}, u32[]{:S(2)}, u32[]{:S(2)}) collective-permute-start(bf16[32,16,128]{2,1,0:T(8,128)(2,1)S(1)} %get-tuple-element.97), channel_id=1, source_target_pairs={{0,2},{2,0},{4,6},{6,4},{8,10},{10,8},{12,14},{14,12},{1,3},{3,1},... | collective-permute-start | bytes 393224 | tf_op jit(solution)/shard_map/ppermute | solution.py:242
  134.7 2.7 %collective-permute-start.32 = (bf16[32,16,128]{2,1,0:T(8,128)(2,1)S(1)}, bf16[32,16,128]{2,1,0:T(8,128)(2,1)S(1)}, u32[]{:S(2)}, u32[]{:S(2)}) collective-permute-start(bf16[32,16,128]{2,1,0:T(8,128)(2,1)S(1)} %get-tuple-element.98), channel_id=1, source_target_pairs={{0,4},{2,6},{4,0},{6,2},{8,12},{10,14},{12,8},{14,10},{1,5},{3,7},... | collective-permute-start | bytes 393224 | tf_op jit(solution)/shard_map/ppermute | solution.py:242
  137.4 1.6 collective-permute-done.31.refs_0_
  139.0 2.3 %collective-permute-done.32.refs_1_ = bf16[32,16,128]{2,1,0:T(8,128)(2,1)S(1)} collective-permute-done((bf16[32,16,128]{2,1,0:T(8,128)(2,1)S(1)}, bf16[32,16,128]{2,1,0:T(8,128)(2,1)S(1)}, u32[]{:S(2)}, u32[]{:S(2)}) %collective-permute-start.32) | collective-permute-done | bytes 131104 | tf_op jit(solution)/shard_map/ppermute | solution.py:242
  141.3 2.7 %collective-permute-done.33.refs_2_ = bf16[32,16,128]{2,1,0:T(8,128)(2,1)S(1)} collective-permute-done((bf16[32,16,128]{2,1,0:T(8,128)(2,1)S(1)}, bf16[32,16,128]{2,1,0:T(8,128)(2,1)S(1)}, u32[]{:S(2)}, u32[]{:S(2)}) %collective-permute-start.33) | collective-permute-done | bytes 131104 | tf_op jit(solution)/shard_map/ppermute | solution.py:242
  145.6 5.9 %collective-permute-done.34.far = bf16[32,16,128]{2,1,0:T(8,128)(2,1)S(1)} collective-permute-done((bf16[32,16,128]{2,1,0:T(8,128)(2,1)S(1)}, bf16[32,16,128]{2,1,0:T(8,128)(2,1)S(1)}, u32[]{:S(2)}, u32[]{:S(2)}) %collective-permute-start.34) | collective-permute-done | bytes 131104 | tf_op jit(solution)/shard_map/ppermute | solution.py:242
  151.6 2.7 %collective-permute-start.37 = (bf16[32,16,128]{2,1,0:T(8,128)(2,1)S(1)}, bf16[32,16,128]{2,1,0:T(8,128)(2,1)S(1)}, u32[]{:S(2)}, u32[]{:S(2)}) collective-permute-start(bf16[32,16,128]{2,1,0:T(8,128)(2,1)S(1)} %get-tuple-element.103.refs_0_), channel_id=1, source_target_pairs={{0,6},{2,4},{4,2},{6,0},{8,14},{10,12},{12,10},{14,8},{1,7},{3,5},... | collective-permute-start | bytes 393224 | tf_op jit(solution)/shard_map/ppermute | solution.py:242
  155.8 2.5 %collective-permute-done.37.refs_3_ = bf16[32,16,128]{2,1,0:T(8,128)(2,1)S(1)} collective-permute-done((bf16[32,16,128]{2,1,0:T(8,128)(2,1)S(1)}, bf16[32,16,128]{2,1,0:T(8,128)(2,1)S(1)}, u32[]{:S(2)}, u32[]{:S(2)}) %collective-permute-start.37) | collective-permute-done | bytes 131104 | tf_op jit(solution)/shard_map/ppermute | solution.py:242
  158.3 2.5 %collective-permute-done.36.refs_2_ = bf16[32,16,128]{2,1,0:T(8,128)(2,1)S(1)} collective-permute-done((bf16[32,16,128]{2,1,0:T(8,128)(2,1)S(1)}, bf16[32,16,128]{2,1,0:T(8,128)(2,1)S(1)}, u32[]{:S(2)}, u32[]{:S(2)}) %collective-permute-start.36) | collective-permute-done | bytes 131104 | tf_op jit(solution)/shard_map/ppermute | solution.py:242
  160.8 1.6 backward_kernel.10.own
  164.4 2.5 %forward_kernel.10 = (f32[32,16,128]{2,1,0:T(8,128)S(1)}, f32[32,16,128]{2,1,0:T(8,128)S(1)}, bf16[32,16,128]{2,1,0:T(8,128)(2,1)S(1)}, bf16[32,16,128]{2,1,0:T(8,128)(2,1)S(1)}, bf16[32,16,128]{2,1,0:T(8,128)(2,1)S(1)}) custom-call(s32[728]{0:T(1024)S(1)} %get-tuple-element.62.plan, bf16[256,128,128]{2,1,0:T(8,128)(2,1)S(1)} %get-tuple-element.63.tile, ...), custom_call_target="tpu_custom_call" | custom-call | tf_op jit(solution)/shard_map/forward_kernel/pallas_call | solution.py:294
  166.9 2.9 %collective-permute-start.39 = (bf16[32,16,128]{2,1,0:T(8,128)(2,1)S(1)}, bf16[32,16,128]{2,1,0:T(8,128)(2,1)S(1)}, u32[]{:S(2)}, u32[]{:S(2)}) collective-permute-start(bf16[32,16,128]{2,1,0:T(8,128)(2,1)S(1)} %get-tuple-element.106), channel_id=1, source_target_pairs={{0,2},{2,0},{4,6},{6,4},{8,10},{10,8},{12,14},{14,12},{1,3},{3,1},... | collective-permute-start | bytes 393224 | tf_op jit(solution)/shard_map/ppermute | solution.py:242
  169.8 2.7 %collective-permute-start.40 = (bf16[32,16,128]{2,1,0:T(8,128)(2,1)S(1)}, bf16[32,16,128]{2,1,0:T(8,128)(2,1)S(1)}, u32[]{:S(2)}, u32[]{:S(2)}) collective-permute-start(bf16[32,16,128]{2,1,0:T(8,128)(2,1)S(1)} %get-tuple-element.107), channel_id=1, source_target_pairs={{0,4},{2,6},{4,0},{6,2},{8,12},{10,14},{12,8},{14,10},{1,5},{3,7},... | collective-permute-start | bytes 393224 | tf_op jit(solution)/shard_map/ppermute | solution.py:242
  172.4 1.6 collective-permute-done.39.refs_0_
  174.1 2.3 %collective-permute-done.40.refs_1_ = bf16[32,16,128]{2,1,0:T(8,128)(2,1)S(1)} collective-permute-done((bf16[32,16,128]{2,1,0:T(8,128)(2,1)S(1)}, bf16[32,16,128]{2,1,0:T(8,128)(2,1)S(1)}, u32[]{:S(2)}, u32[]{:S(2)}) %collective-permute-start.40) | collective-permute-done | bytes 131104 | tf_op jit(solution)/shard_map/ppermute | solution.py:242
  176.4 2.7 %collective-permute-done.41.refs_2_ = bf16[32,16,128]{2,1,0:T(8,128)(2,1)S(1)} collective-permute-done((bf16[32,16,128]{2,1,0:T(8,128)(2,1)S(1)}, bf16[32,16,128]{2,1,0:T(8,128)(2,1)S(1)}, u32[]{:S(2)}, u32[]{:S(2)}) %collective-permute-start.41) | collective-permute-done | bytes 131104 | tf_op jit(solution)/shard_map/ppermute | solution.py:242
  180.6 6.0 %collective-permute-done.42.far = bf16[32,16,128]{2,1,0:T(8,128)(2,1)S(1)} collective-permute-done((bf16[32,16,128]{2,1,0:T(8,128)(2,1)S(1)}, bf16[32,16,128]{2,1,0:T(8,128)(2,1)S(1)}, u32[]{:S(2)}, u32[]{:S(2)}) %collective-permute-start.42) | collective-permute-done | bytes 131104 | tf_op jit(solution)/shard_map/ppermute | solution.py:242
  186.6 2.8 %collective-permute-start.45 = (bf16[32,16,128]{2,1,0:T(8,128)(2,1)S(1)}, bf16[32,16,128]{2,1,0:T(8,128)(2,1)S(1)}, u32[]{:S(2)}, u32[]{:S(2)}) collective-permute-start(bf16[32,16,128]{2,1,0:T(8,128)(2,1)S(1)} %get-tuple-element.111.refs_0_), channel_id=1, source_target_pairs={{0,6},{2,4},{4,2},{6,0},{8,14},{10,12},{12,10},{14,8},{1,7},{3,5},... | collective-permute-start | bytes 393224 | tf_op jit(solution)/shard_map/ppermute | solution.py:242
  190.9 2.5 %collective-permute-done.45.refs_3_ = bf16[32,16,128]{2,1,0:T(8,128)(2,1)S(1)} collective-permute-done((bf16[32,16,128]{2,1,0:T(8,128)(2,1)S(1)}, bf16[32,16,128]{2,1,0:T(8,128)(2,1)S(1)}, u32[]{:S(2)}, u32[]{:S(2)}) %collective-permute-start.45) | collective-permute-done | bytes 131104 | tf_op jit(solution)/shard_map/ppermute | solution.py:242
  193.4 2.5 %collective-permute-done.44.refs_2_ = bf16[32,16,128]{2,1,0:T(8,128)(2,1)S(1)} collective-permute-done((bf16[32,16,128]{2,1,0:T(8,128)(2,1)S(1)}, bf16[32,16,128]{2,1,0:T(8,128)(2,1)S(1)}, u32[]{:S(2)}, u32[]{:S(2)}) %collective-permute-start.44) | collective-permute-done | bytes 131104 | tf_op jit(solution)/shard_map/ppermute | solution.py:242
  195.9 1.6 backward_kernel.11.own
  199.5 2.3 %forward_kernel.11 = (f32[32,16,128]{2,1,0:T(8,128)S(1)}, f32[32,16,128]{2,1,0:T(8,128)S(1)}, bf16[32,16,128]{2,1,0:T(8,128)(2,1)S(1)}, bf16[32,16,128]{2,1,0:T(8,128)(2,1)S(1)}, bf16[32,16,128]{2,1,0:T(8,128)(2,1)S(1)}) custom-call(s32[728]{0:T(1024)S(1)} %get-tuple-element.62.plan, bf16[256,128,128]{2,1,0:T(8,128)(2,1)S(1)} %get-tuple-element.63.tile, ...), custom_call_target="tpu_custom_call" | custom-call | tf_op jit(solution)/shard_map/forward_kernel/pallas_call | solution.py:294
  201.8 2.9 %collective-permute-start.47 = (bf16[32,16,128]{2,1,0:T(8,128)(2,1)S(1)}, bf16[32,16,128]{2,1,0:T(8,128)(2,1)S(1)}, u32[]{:S(2)}, u32[]{:S(2)}) collective-permute-start(bf16[32,16,128]{2,1,0:T(8,128)(2,1)S(1)} %get-tuple-element.116), channel_id=1, source_target_pairs={{0,2},{2,0},{4,6},{6,4},{8,10},{10,8},{12,14},{14,12},{1,3},{3,1},... | collective-permute-start | bytes 393224 | tf_op jit(solution)/shard_map/ppermute | solution.py:242
  204.7 2.7 %collective-permute-start.48 = (bf16[32,16,128]{2,1,0:T(8,128)(2,1)S(1)}, bf16[32,16,128]{2,1,0:T(8,128)(2,1)S(1)}, u32[]{:S(2)}, u32[]{:S(2)}) collective-permute-start(bf16[32,16,128]{2,1,0:T(8,128)(2,1)S(1)} %get-tuple-element.117), channel_id=1, source_target_pairs={{0,4},{2,6},{4,0},{6,2},{8,12},{10,14},{12,8},{14,10},{1,5},{3,7},... | collective-permute-start | bytes 393224 | tf_op jit(solution)/shard_map/ppermute | solution.py:242
  207.3 1.6 collective-permute-done.47.refs_0_
  209.0 2.3 %collective-permute-done.48.refs_1_ = bf16[32,16,128]{2,1,0:T(8,128)(2,1)S(1)} collective-permute-done((bf16[32,16,128]{2,1,0:T(8,128)(2,1)S(1)}, bf16[32,16,128]{2,1,0:T(8,128)(2,1)S(1)}, u32[]{:S(2)}, u32[]{:S(2)}) %collective-permute-start.48) | collective-permute-done | bytes 131104 | tf_op jit(solution)/shard_map/ppermute | solution.py:242
  211.3 2.7 %collective-permute-done.49.refs_2_ = bf16[32,16,128]{2,1,0:T(8,128)(2,1)S(1)} collective-permute-done((bf16[32,16,128]{2,1,0:T(8,128)(2,1)S(1)}, bf16[32,16,128]{2,1,0:T(8,128)(2,1)S(1)}, u32[]{:S(2)}, u32[]{:S(2)}) %collective-permute-start.49) | collective-permute-done | bytes 131104 | tf_op jit(solution)/shard_map/ppermute | solution.py:242
  216.1 3.3 %collective-permute-done.50.far = bf16[16,16,128]{2,1,0:T(8,128)(2,1)S(1)} collective-permute-done((bf16[16,16,128]{2,1,0:T(8,128)(2,1)S(1)}, bf16[16,16,128]{2,1,0:T(8,128)(2,1)S(1)}, u32[]{:S(2)}, u32[]{:S(2)}) %collective-permute-start.50) | collective-permute-done | bytes 65568 | tf_op jit(solution)/shard_map/ppermute | solution.py:242
  (86 shorter events, 43.1 us)
Async XLA Ops:
  1.6 6.9 %collective-permute-start = (bf16[16,16,128]{2,1,0:T(8,128)(2,1)S(1)}, bf16[16,16,128]{2,1,0:T(8,128)(2,1)S(1)}, u32[]{:S(2)}, u32[]{:S(2)}) collective-permute-start(bf16[16,16,128]{2,1,0:T(8,128)(2,1)S(1)} %bitcast.43), channel_id=1, source_target_pairs={{0,8},{2,10},{4,12},{6,14},{8,0},{10,2},{12,4},{14,6},{1,9},{3,11}... | collective-permute-start | bytes 196616 | tf_op jit(solution)/shard_map/ppermute | solution.py:242
  6.7 16.1 %collective-permute-start.6 = (f32[16,34,128]{2,1,0:T(8,128)S(1)}, f32[16,34,128]{2,1,0:T(8,128)S(1)}, u32[]{:S(2)}, u32[]{:S(2)}) collective-permute-start(f32[16,34,128]{2,1,0:T(8,128)S(1)} %pad_maximum_fusion.1), channel_id=1, source_target_pairs={{0,1},{1,0},{2,3},{3,2},{4,5},{5,4},{6,7},{7,6},{8,9},{9,8},{10,11... | collective-permute-start | bytes 835592 | tf_op jit(solution)/shard_map/ppermute | solution.py:239
  8.5 10.7 %collective-permute-start.3 = (bf16[32,16,128]{2,1,0:T(8,128)(2,1)S(1)}, bf16[32,16,128]{2,1,0:T(8,128)(2,1)S(1)}, u32[]{:S(2)}, u32[]{:S(2)}) collective-permute-start(bf16[32,16,128]{2,1,0:T(8,128)(2,1)S(1)} %pad_maximum_fusion.3.refs_0_), channel_id=1, source_target_pairs={{0,6},{2,4},{4,2},{6,0},{8,14},{10,12},{12,10},{14,8},{1,7},{3,5},... | collective-permute-start | bytes 393224 | tf_op jit(solution)/shard_map/ppermute | solution.py:242
  10.0 9.3 %collective-permute-start.2 = (bf16[32,16,128]{2,1,0:T(8,128)(2,1)S(1)}, bf16[32,16,128]{2,1,0:T(8,128)(2,1)S(1)}, u32[]{:S(2)}, u32[]{:S(2)}) collective-permute-start(bf16[32,16,128]{2,1,0:T(8,128)(2,1)S(1)} %pad_maximum_fusion.3.refs_0_), channel_id=1, source_target_pairs={{0,4},{2,6},{4,0},{6,2},{8,12},{10,14},{12,8},{14,10},{1,5},{3,7},... | collective-permute-start | bytes 393224 | tf_op jit(solution)/shard_map/ppermute | solution.py:242
  11.6 7.7 %collective-permute-start.1 = (bf16[32,16,128]{2,1,0:T(8,128)(2,1)S(1)}, bf16[32,16,128]{2,1,0:T(8,128)(2,1)S(1)}, u32[]{:S(2)}, u32[]{:S(2)}) collective-permute-start(bf16[32,16,128]{2,1,0:T(8,128)(2,1)S(1)} %pad_maximum_fusion.3.refs_0_), channel_id=1, source_target_pairs={{0,2},{2,0},{4,6},{6,4},{8,10},{10,8},{12,14},{14,12},{1,3},{3,1},... | collective-permute-start | bytes 393224 | tf_op jit(solution)/shard_map/ppermute | solution.py:242
  12.2 0.7 copy-start
  12.9 0.7 copy-start.1
  13.5 9.3 %copy-start.2 = (f32[1,2048]{1,0:T(1,128)S(1)}, f32[1,2048]{1,0:T(1,128)}, u32[]{:S(2)}) copy-start(f32[1,2048]{1,0:T(1,128)} %param.15) | copy-start | bytes 24580
  19.3 12.2 %collective-permute-start.4 = (f32[2,16,16,128]{3,2,1,0:T(8,128)S(1)}, f32[2,16,16,128]{3,2,1,0:T(8,128)S(1)}, u32[]{:S(2)}, u32[]{:S(2)}) collective-permute-start(f32[2,16,16,128]{3,2,1,0:T(8,128)S(1)} %pad_maximum_fusion.2), channel_id=1, source_target_pairs={{0,8},{2,10},{4,12},{6,14},{8,0},{10,2},{12,4},{14,6},{1,9},{3,11}... | collective-permute-start | bytes 786440 | tf_op jit(solution)/shard_map/ppermute | solution.py:242
  22.7 1.6 collective-permute-start.5
  26.6 7.5 %collective-permute-start.7 = (bf16[32,16,128]{2,1,0:T(8,128)(2,1)S(1)}, bf16[32,16,128]{2,1,0:T(8,128)(2,1)S(1)}, u32[]{:S(2)}, u32[]{:S(2)}) collective-permute-start(bf16[32,16,128]{2,1,0:T(8,128)(2,1)S(1)} %get-tuple-element.70), channel_id=1, source_target_pairs={{0,2},{2,0},{4,6},{6,4},{8,10},{10,8},{12,14},{14,12},{1,3},{3,1},... | collective-permute-start | bytes 393224 | tf_op jit(solution)/shard_map/ppermute | solution.py:242
  30.0 6.3 %collective-permute-start.8 = (bf16[32,16,128]{2,1,0:T(8,128)(2,1)S(1)}, bf16[32,16,128]{2,1,0:T(8,128)(2,1)S(1)}, u32[]{:S(2)}, u32[]{:S(2)}) collective-permute-start(bf16[32,16,128]{2,1,0:T(8,128)(2,1)S(1)} %get-tuple-element.71), channel_id=1, source_target_pairs={{0,4},{2,6},{4,0},{6,2},{8,12},{10,14},{12,8},{14,10},{1,5},{3,7},... | collective-permute-start | bytes 393224 | tf_op jit(solution)/shard_map/ppermute | solution.py:242
  30.9 7.4 %collective-permute-start.9 = (bf16[32,16,128]{2,1,0:T(8,128)(2,1)S(1)}, bf16[32,16,128]{2,1,0:T(8,128)(2,1)S(1)}, u32[]{:S(2)}, u32[]{:S(2)}) collective-permute-start(bf16[32,16,128]{2,1,0:T(8,128)(2,1)S(1)} %get-tuple-element.72), channel_id=1, source_target_pairs={{0,6},{2,4},{4,2},{6,0},{8,14},{10,12},{12,10},{14,8},{1,7},{3,5},... | collective-permute-start | bytes 393224 | tf_op jit(solution)/shard_map/ppermute | solution.py:242
  38.3 8.1 %collective-permute-start.10 = (bf16[32,16,128]{2,1,0:T(8,128)(2,1)S(1)}, bf16[32,16,128]{2,1,0:T(8,128)(2,1)S(1)}, u32[]{:S(2)}, u32[]{:S(2)}) collective-permute-start(bf16[32,16,128]{2,1,0:T(8,128)(2,1)S(1)} %get-tuple-element.74), channel_id=1, source_target_pairs={{0,8},{2,10},{4,12},{6,14},{8,0},{10,2},{12,4},{14,6},{1,9},{3,11}... | collective-permute-start | bytes 393224 | tf_op jit(solution)/shard_map/ppermute | solution.py:242
  46.4 7.5 %collective-permute-start.13 = (bf16[32,16,128]{2,1,0:T(8,128)(2,1)S(1)}, bf16[32,16,128]{2,1,0:T(8,128)(2,1)S(1)}, u32[]{:S(2)}, u32[]{:S(2)}) collective-permute-start(bf16[32,16,128]{2,1,0:T(8,128)(2,1)S(1)} %get-tuple-element.76.refs_0_), channel_id=1, source_target_pairs={{0,6},{2,4},{4,2},{6,0},{8,14},{10,12},{12,10},{14,8},{1,7},{3,5},... | collective-permute-start | bytes 393224 | tf_op jit(solution)/shard_map/ppermute | solution.py:242
  49.6 6.1 %collective-permute-start.12 = (bf16[32,16,128]{2,1,0:T(8,128)(2,1)S(1)}, bf16[32,16,128]{2,1,0:T(8,128)(2,1)S(1)}, u32[]{:S(2)}, u32[]{:S(2)}) collective-permute-start(bf16[32,16,128]{2,1,0:T(8,128)(2,1)S(1)} %get-tuple-element.76.refs_0_), channel_id=1, source_target_pairs={{0,4},{2,6},{4,0},{6,2},{8,12},{10,14},{12,8},{14,10},{1,5},{3,7},... | collective-permute-start | bytes 393224 | tf_op jit(solution)/shard_map/ppermute | solution.py:242
  49.6 6.5 %collective-permute-start.11 = (bf16[32,16,128]{2,1,0:T(8,128)(2,1)S(1)}, bf16[32,16,128]{2,1,0:T(8,128)(2,1)S(1)}, u32[]{:S(2)}, u32[]{:S(2)}) collective-permute-start(bf16[32,16,128]{2,1,0:T(8,128)(2,1)S(1)} %get-tuple-element.76.refs_0_), channel_id=1, source_target_pairs={{0,2},{2,0},{4,6},{6,4},{8,10},{10,8},{12,14},{14,12},{1,3},{3,1},... | collective-permute-start | bytes 393224 | tf_op jit(solution)/shard_map/ppermute | solution.py:242
  57.7 1.9 collective-permute-start.14
  62.0 6.6 %collective-permute-start.15 = (bf16[32,16,128]{2,1,0:T(8,128)(2,1)S(1)}, bf16[32,16,128]{2,1,0:T(8,128)(2,1)S(1)}, u32[]{:S(2)}, u32[]{:S(2)}) collective-permute-start(bf16[32,16,128]{2,1,0:T(8,128)(2,1)S(1)} %get-tuple-element.79), channel_id=1, source_target_pairs={{0,2},{2,0},{4,6},{6,4},{8,10},{10,8},{12,14},{14,12},{1,3},{3,1},... | collective-permute-start | bytes 393224 | tf_op jit(solution)/shard_map/ppermute | solution.py:242
  64.5 6.5 %collective-permute-start.16 = (bf16[32,16,128]{2,1,0:T(8,128)(2,1)S(1)}, bf16[32,16,128]{2,1,0:T(8,128)(2,1)S(1)}, u32[]{:S(2)}, u32[]{:S(2)}) collective-permute-start(bf16[32,16,128]{2,1,0:T(8,128)(2,1)S(1)} %get-tuple-element.80), channel_id=1, source_target_pairs={{0,4},{2,6},{4,0},{6,2},{8,12},{10,14},{12,8},{14,10},{1,5},{3,7},... | collective-permute-start | bytes 393224 | tf_op jit(solution)/shard_map/ppermute | solution.py:242
  67.5 6.7 %collective-permute-start.17 = (bf16[32,16,128]{2,1,0:T(8,128)(2,1)S(1)}, bf16[32,16,128]{2,1,0:T(8,128)(2,1)S(1)}, u32[]{:S(2)}, u32[]{:S(2)}) collective-permute-start(bf16[32,16,128]{2,1,0:T(8,128)(2,1)S(1)} %get-tuple-element.81), channel_id=1, source_target_pairs={{0,6},{2,4},{4,2},{6,0},{8,14},{10,12},{12,10},{14,8},{1,7},{3,5},... | collective-permute-start | bytes 393224 | tf_op jit(solution)/shard_map/ppermute | solution.py:242
  74.3 7.2 %collective-permute-start.18 = (bf16[32,16,128]{2,1,0:T(8,128)(2,1)S(1)}, bf16[32,16,128]{2,1,0:T(8,128)(2,1)S(1)}, u32[]{:S(2)}, u32[]{:S(2)}) collective-permute-start(bf16[32,16,128]{2,1,0:T(8,128)(2,1)S(1)} %get-tuple-element.83), channel_id=1, source_target_pairs={{0,8},{2,10},{4,12},{6,14},{8,0},{10,2},{12,4},{14,6},{1,9},{3,11}... | collective-permute-start | bytes 393224 | tf_op jit(solution)/shard_map/ppermute | solution.py:242
  81.6 6.6 %collective-permute-start.21 = (bf16[32,16,128]{2,1,0:T(8,128)(2,1)S(1)}, bf16[32,16,128]{2,1,0:T(8,128)(2,1)S(1)}, u32[]{:S(2)}, u32[]{:S(2)}) collective-permute-start(bf16[32,16,128]{2,1,0:T(8,128)(2,1)S(1)} %get-tuple-element.85.refs_0_), channel_id=1, source_target_pairs={{0,6},{2,4},{4,2},{6,0},{8,14},{10,12},{12,10},{14,8},{1,7},{3,5},... | collective-permute-start | bytes 393224 | tf_op jit(solution)/shard_map/ppermute | solution.py:242
  83.4 7.6 %collective-permute-start.20 = (bf16[32,16,128]{2,1,0:T(8,128)(2,1)S(1)}, bf16[32,16,128]{2,1,0:T(8,128)(2,1)S(1)}, u32[]{:S(2)}, u32[]{:S(2)}) collective-permute-start(bf16[32,16,128]{2,1,0:T(8,128)(2,1)S(1)} %get-tuple-element.85.refs_0_), channel_id=1, source_target_pairs={{0,4},{2,6},{4,0},{6,2},{8,12},{10,14},{12,8},{14,10},{1,5},{3,7},... | collective-permute-start | bytes 393224 | tf_op jit(solution)/shard_map/ppermute | solution.py:242
  84.6 6.4 %collective-permute-start.19 = (bf16[32,16,128]{2,1,0:T(8,128)(2,1)S(1)}, bf16[32,16,128]{2,1,0:T(8,128)(2,1)S(1)}, u32[]{:S(2)}, u32[]{:S(2)}) collective-permute-start(bf16[32,16,128]{2,1,0:T(8,128)(2,1)S(1)} %get-tuple-element.85.refs_0_), channel_id=1, source_target_pairs={{0,2},{2,0},{4,6},{6,4},{8,10},{10,8},{12,14},{14,12},{1,3},{3,1},... | collective-permute-start | bytes 393224 | tf_op jit(solution)/shard_map/ppermute | solution.py:242
  92.6 1.8 collective-permute-start.22
  96.7 7.3 %collective-permute-start.23 = (bf16[32,16,128]{2,1,0:T(8,128)(2,1)S(1)}, bf16[32,16,128]{2,1,0:T(8,128)(2,1)S(1)}, u32[]{:S(2)}, u32[]{:S(2)}) collective-permute-start(bf16[32,16,128]{2,1,0:T(8,128)(2,1)S(1)} %get-tuple-element.88), channel_id=1, source_target_pairs={{0,2},{2,0},{4,6},{6,4},{8,10},{10,8},{12,14},{14,12},{1,3},{3,1},... | collective-permute-start | bytes 393224 | tf_op jit(solution)/shard_map/ppermute | solution.py:242
  99.8 6.6 %collective-permute-start.24 = (bf16[32,16,128]{2,1,0:T(8,128)(2,1)S(1)}, bf16[32,16,128]{2,1,0:T(8,128)(2,1)S(1)}, u32[]{:S(2)}, u32[]{:S(2)}) collective-permute-start(bf16[32,16,128]{2,1,0:T(8,128)(2,1)S(1)} %get-tuple-element.89), channel_id=1, source_target_pairs={{0,4},{2,6},{4,0},{6,2},{8,12},{10,14},{12,8},{14,10},{1,5},{3,7},... | collective-permute-start | bytes 393224 | tf_op jit(solution)/shard_map/ppermute | solution.py:242
  102.4 6.7 %collective-permute-start.25 = (bf16[32,16,128]{2,1,0:T(8,128)(2,1)S(1)}, bf16[32,16,128]{2,1,0:T(8,128)(2,1)S(1)}, u32[]{:S(2)}, u32[]{:S(2)}) collective-permute-start(bf16[32,16,128]{2,1,0:T(8,128)(2,1)S(1)} %get-tuple-element.90), channel_id=1, source_target_pairs={{0,6},{2,4},{4,2},{6,0},{8,14},{10,12},{12,10},{14,8},{1,7},{3,5},... | collective-permute-start | bytes 393224 | tf_op jit(solution)/shard_map/ppermute | solution.py:242
  109.2 7.4 %collective-permute-start.26 = (bf16[32,16,128]{2,1,0:T(8,128)(2,1)S(1)}, bf16[32,16,128]{2,1,0:T(8,128)(2,1)S(1)}, u32[]{:S(2)}, u32[]{:S(2)}) collective-permute-start(bf16[32,16,128]{2,1,0:T(8,128)(2,1)S(1)} %get-tuple-element.92), channel_id=1, source_target_pairs={{0,8},{2,10},{4,12},{6,14},{8,0},{10,2},{12,4},{14,6},{1,9},{3,11}... | collective-permute-start | bytes 393224 | tf_op jit(solution)/shard_map/ppermute | solution.py:242
  116.6 6.8 %collective-permute-start.29 = (bf16[32,16,128]{2,1,0:T(8,128)(2,1)S(1)}, bf16[32,16,128]{2,1,0:T(8,128)(2,1)S(1)}, u32[]{:S(2)}, u32[]{:S(2)}) collective-permute-start(bf16[32,16,128]{2,1,0:T(8,128)(2,1)S(1)} %get-tuple-element.94.refs_0_), channel_id=1, source_target_pairs={{0,6},{2,4},{4,2},{6,0},{8,14},{10,12},{12,10},{14,8},{1,7},{3,5},... | collective-permute-start | bytes 393224 | tf_op jit(solution)/shard_map/ppermute | solution.py:242
  119.4 6.5 %collective-permute-start.28 = (bf16[32,16,128]{2,1,0:T(8,128)(2,1)S(1)}, bf16[32,16,128]{2,1,0:T(8,128)(2,1)S(1)}, u32[]{:S(2)}, u32[]{:S(2)}) collective-permute-start(bf16[32,16,128]{2,1,0:T(8,128)(2,1)S(1)} %get-tuple-element.94.refs_0_), channel_id=1, source_target_pairs={{0,4},{2,6},{4,0},{6,2},{8,12},{10,14},{12,8},{14,10},{1,5},{3,7},... | collective-permute-start | bytes 393224 | tf_op jit(solution)/shard_map/ppermute | solution.py:242
  119.5 6.4 %collective-permute-start.27 = (bf16[32,16,128]{2,1,0:T(8,128)(2,1)S(1)}, bf16[32,16,128]{2,1,0:T(8,128)(2,1)S(1)}, u32[]{:S(2)}, u32[]{:S(2)}) collective-permute-start(bf16[32,16,128]{2,1,0:T(8,128)(2,1)S(1)} %get-tuple-element.94.refs_0_), channel_id=1, source_target_pairs={{0,2},{2,0},{4,6},{6,4},{8,10},{10,8},{12,14},{14,12},{1,3},{3,1},... | collective-permute-start | bytes 393224 | tf_op jit(solution)/shard_map/ppermute | solution.py:242
  127.5 2.0 collective-permute-start.30
  131.8 7.2 %collective-permute-start.31 = (bf16[32,16,128]{2,1,0:T(8,128)(2,1)S(1)}, bf16[32,16,128]{2,1,0:T(8,128)(2,1)S(1)}, u32[]{:S(2)}, u32[]{:S(2)}) collective-permute-start(bf16[32,16,128]{2,1,0:T(8,128)(2,1)S(1)} %get-tuple-element.97), channel_id=1, source_target_pairs={{0,2},{2,0},{4,6},{6,4},{8,10},{10,8},{12,14},{14,12},{1,3},{3,1},... | collective-permute-start | bytes 393224 | tf_op jit(solution)/shard_map/ppermute | solution.py:242
  134.7 6.6 %collective-permute-start.32 = (bf16[32,16,128]{2,1,0:T(8,128)(2,1)S(1)}, bf16[32,16,128]{2,1,0:T(8,128)(2,1)S(1)}, u32[]{:S(2)}, u32[]{:S(2)}) collective-permute-start(bf16[32,16,128]{2,1,0:T(8,128)(2,1)S(1)} %get-tuple-element.98), channel_id=1, source_target_pairs={{0,4},{2,6},{4,0},{6,2},{8,12},{10,14},{12,8},{14,10},{1,5},{3,7},... | collective-permute-start | bytes 393224 | tf_op jit(solution)/shard_map/ppermute | solution.py:242
  137.3 6.7 %collective-permute-start.33 = (bf16[32,16,128]{2,1,0:T(8,128)(2,1)S(1)}, bf16[32,16,128]{2,1,0:T(8,128)(2,1)S(1)}, u32[]{:S(2)}, u32[]{:S(2)}) collective-permute-start(bf16[32,16,128]{2,1,0:T(8,128)(2,1)S(1)} %get-tuple-element.99), channel_id=1, source_target_pairs={{0,6},{2,4},{4,2},{6,0},{8,14},{10,12},{12,10},{14,8},{1,7},{3,5},... | collective-permute-start | bytes 393224 | tf_op jit(solution)/shard_map/ppermute | solution.py:242
  144.1 7.4 %collective-permute-start.34 = (bf16[32,16,128]{2,1,0:T(8,128)(2,1)S(1)}, bf16[32,16,128]{2,1,0:T(8,128)(2,1)S(1)}, u32[]{:S(2)}, u32[]{:S(2)}) collective-permute-start(bf16[32,16,128]{2,1,0:T(8,128)(2,1)S(1)} %get-tuple-element.101), channel_id=1, source_target_pairs={{0,8},{2,10},{4,12},{6,14},{8,0},{10,2},{12,4},{14,6},{1,9},{3,11}... | collective-permute-start | bytes 393224 | tf_op jit(solution)/shard_map/ppermute | solution.py:242
  151.6 6.8 %collective-permute-start.37 = (bf16[32,16,128]{2,1,0:T(8,128)(2,1)S(1)}, bf16[32,16,128]{2,1,0:T(8,128)(2,1)S(1)}, u32[]{:S(2)}, u32[]{:S(2)}) collective-permute-start(bf16[32,16,128]{2,1,0:T(8,128)(2,1)S(1)} %get-tuple-element.103.refs_0_), channel_id=1, source_target_pairs={{0,6},{2,4},{4,2},{6,0},{8,14},{10,12},{12,10},{14,8},{1,7},{3,5},... | collective-permute-start | bytes 393224 | tf_op jit(solution)/shard_map/ppermute | solution.py:242
  154.3 6.5 %collective-permute-start.36 = (bf16[32,16,128]{2,1,0:T(8,128)(2,1)S(1)}, bf16[32,16,128]{2,1,0:T(8,128)(2,1)S(1)}, u32[]{:S(2)}, u32[]{:S(2)}) collective-permute-start(bf16[32,16,128]{2,1,0:T(8,128)(2,1)S(1)} %get-tuple-element.103.refs_0_), channel_id=1, source_target_pairs={{0,4},{2,6},{4,0},{6,2},{8,12},{10,14},{12,8},{14,10},{1,5},{3,7},... | collective-permute-start | bytes 393224 | tf_op jit(solution)/shard_map/ppermute | solution.py:242
  154.4 6.4 %collective-permute-start.35 = (bf16[32,16,128]{2,1,0:T(8,128)(2,1)S(1)}, bf16[32,16,128]{2,1,0:T(8,128)(2,1)S(1)}, u32[]{:S(2)}, u32[]{:S(2)}) collective-permute-start(bf16[32,16,128]{2,1,0:T(8,128)(2,1)S(1)} %get-tuple-element.103.refs_0_), channel_id=1, source_target_pairs={{0,2},{2,0},{4,6},{6,4},{8,10},{10,8},{12,14},{14,12},{1,3},{3,1},... | collective-permute-start | bytes 393224 | tf_op jit(solution)/shard_map/ppermute | solution.py:242
  162.4 2.0 collective-permute-start.38
  166.9 7.2 %collective-permute-start.39 = (bf16[32,16,128]{2,1,0:T(8,128)(2,1)S(1)}, bf16[32,16,128]{2,1,0:T(8,128)(2,1)S(1)}, u32[]{:S(2)}, u32[]{:S(2)}) collective-permute-start(bf16[32,16,128]{2,1,0:T(8,128)(2,1)S(1)} %get-tuple-element.106), channel_id=1, source_target_pairs={{0,2},{2,0},{4,6},{6,4},{8,10},{10,8},{12,14},{14,12},{1,3},{3,1},... | collective-permute-start | bytes 393224 | tf_op jit(solution)/shard_map/ppermute | solution.py:242
  169.8 6.6 %collective-permute-start.40 = (bf16[32,16,128]{2,1,0:T(8,128)(2,1)S(1)}, bf16[32,16,128]{2,1,0:T(8,128)(2,1)S(1)}, u32[]{:S(2)}, u32[]{:S(2)}) collective-permute-start(bf16[32,16,128]{2,1,0:T(8,128)(2,1)S(1)} %get-tuple-element.107), channel_id=1, source_target_pairs={{0,4},{2,6},{4,0},{6,2},{8,12},{10,14},{12,8},{14,10},{1,5},{3,7},... | collective-permute-start | bytes 393224 | tf_op jit(solution)/shard_map/ppermute | solution.py:242
  172.4 6.7 %collective-permute-start.41 = (bf16[32,16,128]{2,1,0:T(8,128)(2,1)S(1)}, bf16[32,16,128]{2,1,0:T(8,128)(2,1)S(1)}, u32[]{:S(2)}, u32[]{:S(2)}) collective-permute-start(bf16[32,16,128]{2,1,0:T(8,128)(2,1)S(1)} %get-tuple-element.108), channel_id=1, source_target_pairs={{0,6},{2,4},{4,2},{6,0},{8,14},{10,12},{12,10},{14,8},{1,7},{3,5},... | collective-permute-start | bytes 393224 | tf_op jit(solution)/shard_map/ppermute | solution.py:242
  179.2 7.4 %collective-permute-start.42 = (bf16[32,16,128]{2,1,0:T(8,128)(2,1)S(1)}, bf16[32,16,128]{2,1,0:T(8,128)(2,1)S(1)}, u32[]{:S(2)}, u32[]{:S(2)}) collective-permute-start(bf16[32,16,128]{2,1,0:T(8,128)(2,1)S(1)} %get-tuple-element.110), channel_id=1, source_target_pairs={{0,8},{2,10},{4,12},{6,14},{8,0},{10,2},{12,4},{14,6},{1,9},{3,11}... | collective-permute-start | bytes 393224 | tf_op jit(solution)/shard_map/ppermute | solution.py:242
  186.6 6.8 %collective-permute-start.45 = (bf16[32,16,128]{2,1,0:T(8,128)(2,1)S(1)}, bf16[32,16,128]{2,1,0:T(8,128)(2,1)S(1)}, u32[]{:S(2)}, u32[]{:S(2)}) collective-permute-start(bf16[32,16,128]{2,1,0:T(8,128)(2,1)S(1)} %get-tuple-element.111.refs_0_), channel_id=1, source_target_pairs={{0,6},{2,4},{4,2},{6,0},{8,14},{10,12},{12,10},{14,8},{1,7},{3,5},... | collective-permute-start | bytes 393224 | tf_op jit(solution)/shard_map/ppermute | solution.py:242
  189.4 6.5 %collective-permute-start.44 = (bf16[32,16,128]{2,1,0:T(8,128)(2,1)S(1)}, bf16[32,16,128]{2,1,0:T(8,128)(2,1)S(1)}, u32[]{:S(2)}, u32[]{:S(2)}) collective-permute-start(bf16[32,16,128]{2,1,0:T(8,128)(2,1)S(1)} %get-tuple-element.111.refs_0_), channel_id=1, source_target_pairs={{0,4},{2,6},{4,0},{6,2},{8,12},{10,14},{12,8},{14,10},{1,5},{3,7},... | collective-permute-start | bytes 393224 | tf_op jit(solution)/shard_map/ppermute | solution.py:242
  189.5 6.4 %collective-permute-start.43 = (bf16[32,16,128]{2,1,0:T(8,128)(2,1)S(1)}, bf16[32,16,128]{2,1,0:T(8,128)(2,1)S(1)}, u32[]{:S(2)}, u32[]{:S(2)}) collective-permute-start(bf16[32,16,128]{2,1,0:T(8,128)(2,1)S(1)} %get-tuple-element.111.refs_0_), channel_id=1, source_target_pairs={{0,2},{2,0},{4,6},{6,4},{8,10},{10,8},{12,14},{14,12},{1,3},{3,1},... | collective-permute-start | bytes 393224 | tf_op jit(solution)/shard_map/ppermute | solution.py:242
  197.5 2.0 collective-permute-start.46
  201.8 7.2 %collective-permute-start.47 = (bf16[32,16,128]{2,1,0:T(8,128)(2,1)S(1)}, bf16[32,16,128]{2,1,0:T(8,128)(2,1)S(1)}, u32[]{:S(2)}, u32[]{:S(2)}) collective-permute-start(bf16[32,16,128]{2,1,0:T(8,128)(2,1)S(1)} %get-tuple-element.116), channel_id=1, source_target_pairs={{0,2},{2,0},{4,6},{6,4},{8,10},{10,8},{12,14},{14,12},{1,3},{3,1},... | collective-permute-start | bytes 393224 | tf_op jit(solution)/shard_map/ppermute | solution.py:242
  204.7 6.6 %collective-permute-start.48 = (bf16[32,16,128]{2,1,0:T(8,128)(2,1)S(1)}, bf16[32,16,128]{2,1,0:T(8,128)(2,1)S(1)}, u32[]{:S(2)}, u32[]{:S(2)}) collective-permute-start(bf16[32,16,128]{2,1,0:T(8,128)(2,1)S(1)} %get-tuple-element.117), channel_id=1, source_target_pairs={{0,4},{2,6},{4,0},{6,2},{8,12},{10,14},{12,8},{14,10},{1,5},{3,7},... | collective-permute-start | bytes 393224 | tf_op jit(solution)/shard_map/ppermute | solution.py:242
  207.3 6.7 %collective-permute-start.49 = (bf16[32,16,128]{2,1,0:T(8,128)(2,1)S(1)}, bf16[32,16,128]{2,1,0:T(8,128)(2,1)S(1)}, u32[]{:S(2)}, u32[]{:S(2)}) collective-permute-start(bf16[32,16,128]{2,1,0:T(8,128)(2,1)S(1)} %get-tuple-element.118), channel_id=1, source_target_pairs={{0,6},{2,4},{4,2},{6,0},{8,14},{10,12},{12,10},{14,8},{1,7},{3,5},... | collective-permute-start | bytes 393224 | tf_op jit(solution)/shard_map/ppermute | solution.py:242
  214.1 5.3 %collective-permute-start.50 = (bf16[16,16,128]{2,1,0:T(8,128)(2,1)S(1)}, bf16[16,16,128]{2,1,0:T(8,128)(2,1)S(1)}, u32[]{:S(2)}, u32[]{:S(2)}) collective-permute-start(bf16[16,16,128]{2,1,0:T(8,128)(2,1)S(1)} %get-tuple-element.120), channel_id=1, source_target_pairs={{0,8},{2,10},{4,12},{6,14},{8,0},{10,2},{12,4},{14,6},{1,9},{3,11}... | collective-permute-start | bytes 196616 | tf_op jit(solution)/shard_map/ppermute | solution.py:242

commit v4 on v0

v4 whole, which is shorter than its diff:
```python
import functools

import jax
import jax.numpy as jnp
from jax import lax
from jax.experimental import pallas as pl
from jax.experimental.pallas import tpu as pltpu
from jax.sharding import PartitionSpec as P

BS = 128
ITERS = 6
WIDE, NARROW = 48, 16
NN = (((1,), (0,)), ((), ()))
NT = (((1,), (1,)), ((), ()))

SMEM = pl.BlockSpec(memory_space=pltpu.SMEM)
VMEM = pl.BlockSpec(memory_space=pltpu.VMEM)
HBM = pl.BlockSpec(memory_space=pltpu.HBM)
PARAMS = pltpu.CompilerParams(vmem_limit_bytes=24 * 2**20)


class Plan:
    def __init__(self, ref, slots, columns):
        self.ref = ref
        self.pairs, self.room = plan_size(slots, columns)

    def first(self, near):
        return self.ref[0] if near else 0

    def count(self, near):
        return self.ref[2] if near else self.ref[1]

    def slot(self, i):
        return 8 + i

    def row(self, i):
        return 8 + 2 * self.room + i

    def col(self, pair):
        return 8 + 4 * self.room + pair


def plan_size(slots, columns):
    pairs = -(-(slots + 2 * columns) // (2 * NARROW)) * NARROW + 2 * NARROW
    return pairs, pairs + -(-slots // 2)


def setup_kernel(direct, half, count, *refs):
    given, (state, duals, y_half, order), held, sems = refs[:8], refs[8:12], refs[12:20], refs[20]
    copies = [pltpu.make_async_copy(a, b, sems.at[i]) for i, (a, b) in enumerate(zip(given, held))]
    for copy in copies:
        copy.start()
    for copy in copies:
        copy.wait()
    primal, cost, upper, kind, dual, rhs, brow, bcol = held
    cols, span, scen = state.shape[0], dual.shape[1], dual.shape[0]
    for b in range(cols):
        state[b, pl.ds(0, scen)] = primal[:, b, :]
        state[b, pl.ds(scen, scen)] = cost[:, b, :]
        state[b, pl.ds(2 * scen, 1)] = upper[pl.ds(b, 1)]
        state[b, pl.ds(2 * scen + 1, 1)] = kind[pl.ds(b, 1)].astype(jnp.float32)
    for b in range(span):
        y = dual[:, b, :]
        duals[b] = y
        duals[span + b] = rhs[:, b, :]
        y_half[b] = y.astype(y_half.dtype)
    columns = 2 * cols
    key = bcol[...] ^ (lax.axis_index("row") * cols)
    row = brow[...]
    if direct:
        row = row ^ (lax.axis_index("col") * span)
        key = key + jnp.where((row & ((half - 1) * span)) == 0, 0, columns)
    lanes = key.shape[1]
    slot = lanes * lax.broadcasted_iota(jnp.int32, key.shape, 0) + lax.broadcasted_iota(jnp.int32, key.shape, 1)
    order[pl.ds(0, key.shape[0])] = jnp.where(slot < count[0, 0], key, 2 * columns)
    order[pl.ds(key.shape[0], key.shape[0])] = row


def runs_of(count, step, run=16):
    def body(i, _):
        for k in range(run):
            step(i * run + k)
        return 0

    lax.fori_loop(0, count // run, body, 0)


def prepare_kernel(columns, rows, order, blocks, plan_ref, tile, keys, ends, sem, key_sems):
    copy = pltpu.make_async_copy(blocks, tile, sem)
    copy.start()
    key_copies = [
        pltpu.make_async_copy(order.at[i], keys.at[pl.ds(i * BS, BS)], key_sems.at[i]) for i in range(order.shape[0])
    ]
    for key_copy in key_copies:
        key_copy.start()
    slots = blocks.shape[0]
    plan = Plan(plan_ref, slots, columns)

    def clear(i, _):
        for k in range(2):
            plan_ref[plan.slot(2 * i + k)] = 0
            plan_ref[plan.row(2 * i + k)] = rows
        plan_ref[plan.col(i)] = 0
        return 0

    lax.fori_loop(0, plan.pairs, clear, 0, unroll=16)
    for c in range(2 * columns):
        ends[c] = 0
    for key_copy in key_copies:
        key_copy.wait()

    def tally(n):
        key = keys[n]
        ends[key] = ends[key] + 1

    ends[2 * columns] = 0
    runs_of(slots, tally)

    start = jnp.int32(0)
    for near in range(2):
        plan_ref[near] = start // 2
        first = start
        for c in range(near * columns, (near + 1) * columns):
            size = ends[c]
            ends[c] = start
            start = start + ((size + 1) // 2) * 2
        plan_ref[1 + near] = (start - first) // 2
        start = (start + 2 * NARROW - 1) // (2 * NARROW) * (2 * NARROW)
        if near == 0:
            plan_ref[0] = start // 2
    ends[2 * columns] = 2 * plan.pairs

    def put(n):
        key = keys[n]
        at = ends[key]
        ends[key] = at + 1
        plan_ref[plan.slot(at)] = n
        plan_ref[plan.row(at)] = keys[slots + n]
        plan_ref[plan.col(at // 2)] = lax.rem(key, columns)

    runs_of(slots, put)
    copy.wait()


def over_pairs(plan, near, step):
    begin, pairs = plan.first(near), plan.count(near)
    wide = pairs // WIDE

    def run(i, _, size, start):
        step(start + i * size, size)
        return 0

    lax.fori_loop(0, wide, functools.partial(run, size=WIDE, start=begin), 0)
    rest = wide * WIDE
    lax.fori_loop(0, (pairs - rest + NARROW - 1) // NARROW, functools.partial(run, size=NARROW, start=begin + rest), 0)


def transposed_products(plan, near, tile, vecs, acc):
    ref = plan.ref

    def step(first, n):
        terms = []
        for u in range(n):
            i = 2 * (first + u)
            left = [vecs[ref[plan.row(i + k)]] for k in range(2)]
            right = [tile[ref[plan.slot(i + k)]] for k in range(2)]
            terms.append(
                lax.dot_general(
                    jnp.concatenate(left, axis=1), jnp.concatenate(right, axis=0), NN, preferred_element_type=jnp.float32
                )
            )
        for u in range(n):
            acc[ref[plan.col(first + u)]] += terms[u]

    over_pairs(plan, near, step)


def products(plan, near, tile, vecs, acc):
    ref = plan.ref

    def step(first, n):
        terms = []
        for u in range(n):
            i = 2 * (first + u)
            right = [tile[ref[plan.slot(i + k)]] for k in range(2)]
            terms.append(
                lax.dot_general(
                    vecs[ref[plan.col(first + u)]], jnp.concatenate(right, axis=0), NT, preferred_element_type=jnp.float32
                )
            )
        for u in range(n):
            for k in range(2):
                acc[ref[plan.row(2 * (first + u) + k)]] += terms[u][:, k * BS : (k + 1) * BS]

    acc[...] = jnp.zeros(acc.shape, acc.dtype)
    over_pairs(plan, near, step)


def backward_own_kernel(plan_ref, tile, piece, grad, vecs):
    plan = Plan(plan_ref, tile.shape[0], grad.shape[0])
    span = piece.shape[0] // 2
    rows = vecs.shape[0] - 1
    vecs[pl.ds(0, span)] = piece[pl.ds(0, span)]
    vecs[pl.ds(rows // 2, span)] = piece[pl.ds(span, span)]
    vecs[rows] = jnp.zeros(vecs.shape[1:], vecs.dtype)
    grad[...] = jnp.zeros(grad.shape, grad.dtype)
    transposed_products(plan, False, tile, vecs, grad)


def backward_near_kernel(plan_ref, tile, *refs):
    pieces, (begun, grad, vecs) = refs[:-3], refs[-3:]
    plan = Plan(plan_ref, tile.shape[0], grad.shape[0])
    half = len(pieces) + 1
    span = pieces[0].shape[0] // 2
    for m in range(1, half):
        vecs[pl.ds(m * span, span)] = pieces[m - 1][pl.ds(0, span)]
        vecs[pl.ds((m + half) * span, span)] = pieces[m - 1][pl.ds(span, span)]
    vecs[2 * half * span] = jnp.zeros(vecs.shape[1:], vecs.dtype)
    grad[...] = begun[...]
    transposed_products(plan, True, tile, vecs, grad)


def primal_step(own, other, here_state, there_state, x_ref, x_out, x_bar):
    cols, scen = here_state.shape[0], own.shape[1]
    for h, state in enumerate((here_state, there_state)):
        here, there = pl.ds(h * cols, cols), pl.ds((1 - h) * cols, cols)
        x = state[:, pl.ds(0, scen)] if x_ref is None else x_ref[here]
        cost = state[:, pl.ds(scen, scen)]
        upper, kind = state[:, pl.ds(2 * scen, 1)], state[:, pl.ds(2 * scen + 1, 1)]
        value = x - 0.4 * (cost - (own[here] + other[there]))
        lifted = jnp.where(kind == 2, value, jnp.maximum(value, 0.0))
        x_next = jnp.where(kind == 1, jnp.minimum(lifted, upper), lifted)
        if x_out.shape[0] == 2 * cols:
            x_out[here] = x_next
        elif h == 0:
            for b in range(cols):
                x_out[:, b, :] = x_next[b]
        x_bar[here] = (2.0 * x_next - x).astype(x_bar.dtype)


def forward_near_kernel(first, plan_ref, tile, own, other, here_state, there_state, *refs):
    x_ref = None if first else refs[0]
    x_out, x_bar, *pieces, acc = refs if first else refs[1:]
    primal_step(own, other, here_state, there_state, x_ref, x_out, x_bar)
    if pieces:
        products(Plan(plan_ref, tile.shape[0], x_bar.shape[0]), True, tile, x_bar, acc)
        half = len(pieces) + 1
        span = pieces[0].shape[0] // 2
        for m in range(1, half):
            pieces[m - 1][pl.ds(0, span)] = acc[pl.ds(m * span, span)].astype(pieces[m - 1].dtype)
            pieces[m - 1][pl.ds(span, span)] = acc[pl.ds((m + half) * span, span)].astype(pieces[m - 1].dtype)


def forward_own_kernel(plan_ref, tile, x_bar, piece, acc):
    products(Plan(plan_ref, tile.shape[0], x_bar.shape[0]), False, tile, x_bar, acc)
    span = piece.shape[0] // 2
    piece[pl.ds(0, span)] = acc[pl.ds(0, span)]
    piece[pl.ds(span, span)] = acc[pl.ds((acc.shape[0] - 1) // 2, span)]


def near_sum_kernel(duals, own, *refs):
    pieces, (total, sent) = refs[:-2], refs[-2:]
    image = own[...]
    for piece in pieces:
        image = image + piece[...].astype(jnp.float32)
    total[...] = image
    span = image.shape[0] // 2
    at = sent.shape[0] - span
    sent[pl.ds(at, span)] = image[span:].astype(sent.dtype)
    if at:
        sent[pl.ds(0, span)] = (image[:span] - duals[pl.ds(span, span)]).astype(sent.dtype)


def dual_kernel(duals, near, far, y_own, y_far, y_out, y_half):
    span = near.shape[0] // 2
    here, there = pl.ds(0, span), pl.ds(span, span)
    own = y_own[here] + 0.9 * (duals[there] - (near[here] + far[there].astype(jnp.float32)))
    copy = y_far[there].astype(jnp.float32) - 0.9 * (far[here].astype(jnp.float32) + near[there])
    for at, y in ((here, jnp.maximum(0.0, own)), (there, jnp.maximum(0.0, copy))):
        y_out[at] = y
        y_half[at] = y.astype(y_half.dtype)


def last_dual_kernel(duals, near, far, y_own, y_out):
    span = far.shape[0]
    here, there = pl.ds(0, span), pl.ds(span, span)
    own = y_own[here] + 0.9 * (duals[there] - (near[here] + far[...].astype(jnp.float32)))
    y = jnp.maximum(0.0, own)
    for b in range(span):
        y_out[:, b, :] = y[b]


def whole_dual_kernel(y_ref, rhs, image, y_out, y_half):
    y = jnp.maximum(0.0, y_ref[...] + 0.9 * (rhs[...] - image[...]))
    y_out[...] = y
    y_half[...] = y.astype(y_half.dtype)


def in_blocks(a):
    return a.reshape(tuple(n for n in a.shape[:-1] if n > 1) + (-1, BS))


def per_device(
    cost, rhs, primal, dual, bound_kind, upper, kblocks, block_row, block_col, block_count
):
    n_col, n_row = lax.axis_size("col"), lax.axis_size("row")
    scen = primal.shape[0]
    span, cols = dual.shape[2] // BS, primal.shape[2] // BS
    row_blocks, col_blocks = span * n_col, cols * n_row
    direct = n_col in (4, 8) and span & (span - 1) == 0
    half = n_col // 2

    f32, bf16, i32 = jnp.float32, jnp.bfloat16, jnp.int32
    blocks = kblocks[0, 0]
    slots = blocks.shape[0]

    def swap(a):
        return lax.ppermute(a, "row", [(i, n_row - 1 - i) for i in range(n_row)])

    def partner(a, m):
        return lax.ppermute(a, "col", [(i, i ^ m) for i in range(n_col)])

    def near(a):
        return [partner(a, m) for m in range(1, half)]

    def shape(blocks, dtype):
        return jax.ShapeDtypeStruct((blocks, scen, BS), dtype)

    def call(kernel, outs, ins, scratch=(), scalars=0, flops=0):
        return pl.pallas_call(
            kernel,
            out_shape=outs,
            in_specs=[SMEM] * scalars + [VMEM] * ins,
            out_specs=tuple(VMEM for _ in outs),
            scratch_shapes=[pltpu.VMEM((blocks, scen, BS), dtype) for blocks, dtype in scratch],
            compiler_params=PARAMS,
            cost_estimate=pl.CostEstimate(flops=flops, bytes_accessed=0, transcendentals=0),
            name=getattr(kernel, "func", kernel).__name__,
        )

    given = [in_blocks(a) for a in (primal, cost, upper, bound_kind, dual, rhs, block_row, block_col)]
    state, duals, y_half, order = pl.pallas_call(
        functools.partial(setup_kernel, direct, half),
        out_shape=(
            jax.ShapeDtypeStruct((cols, 2 * scen + 2, BS), f32),
            shape(2 * span, f32),
            shape(span, bf16),
            jax.ShapeDtypeStruct((2 * slots // BS, BS), i32),
        ),
        in_specs=[SMEM] + [HBM] * 8,
        out_specs=(VMEM,) * 4,
        scratch_shapes=[pltpu.VMEM(a.shape, a.dtype) for a in given] + [pltpu.SemaphoreType.DMA((8,))],
        compiler_params=PARAMS,
        name="setup_kernel",
    )(block_count, *[pltpu.with_memory_space_constraint(a, pltpu.HBM) for a in given])
    other_state = swap(state)
    if direct:
        y_half, order = lax.optimization_barrier((jnp.concatenate([y_half, partner(y_half, half)]), order))
    plan, tile = pl.pallas_call(
        functools.partial(prepare_kernel, col_blocks, row_blocks),
        out_shape=(
            pltpu.SMEM((8 + 5 * plan_size(slots, col_blocks)[1],), i32),
            pltpu.VMEM(blocks.shape, blocks.dtype),
        ),
        in_specs=[VMEM, HBM],
        out_specs=(SMEM, VMEM),
        scratch_shapes=[
            pltpu.SMEM((order.size,), i32),
            pltpu.SMEM((2 * col_blocks + 1,), i32),
            pltpu.SemaphoreType.DMA,
            pltpu.SemaphoreType.DMA((order.shape[0],)),
        ],
        compiler_params=PARAMS,
        name="prepare_kernel",
    )(order, pltpu.with_memory_space_constraint(blocks, pltpu.HBM))

    flops = 2 * slots * BS * BS * scen
    backward_own = call(backward_own_kernel, (shape(col_blocks, f32),), 2, ((row_blocks + 1, bf16),), 1, flops)
    backward_near = call(
        backward_near_kernel, (shape(col_blocks, f32),), 1 + half, ((row_blocks + 1, bf16),), 1, flops
    )
    near_pieces = (shape(2 * span, bf16),) * (half - 1) if direct else ()
    forward_own = call(
        forward_own_kernel,
        (shape(2 * span if direct else row_blocks, f32),),
        2,
        ((row_blocks + 1, f32),),
        1,
        flops,
    )

    x = ()
    for step in range(ITERS):
        first, last = step == 0, step == ITERS - 1
        if direct:
            y_near = near(y_half)
            (grad,) = backward_own(plan, tile, y_half)
            (grad,) = backward_near(plan, tile, *y_near, grad)
        else:
            (grad,) = backward_own(plan, tile, lax.all_gather(y_half, "col", axis=0, tiled=True))
        x_shape = jax.ShapeDtypeStruct((scen, cols, BS), f32) if last else shape(col_blocks, f32)
        x, x_bar, *image = call(
            functools.partial(forward_near_kernel, first),
            (x_shape, shape(col_blocks, bf16)) + near_pieces,
            5 if first else 6,
            ((row_blocks + 1, f32),),
            1,
            flops,
        )(plan, tile, grad, swap(grad), state, other_state, *x)
        x = (x,)
        (own_image,) = forward_own(plan, tile, x_bar)
        if direct:
            image = [partner(image[m - 1], m) for m in range(1, half)]
            kept = 1 if last else 2
            total, sent = call(near_sum_kernel, (shape(2 * span, f32), shape(kept * span, bf16)), 1 + half)(
                duals, own_image, *image
            )
            args = (duals, total, partner(sent, half))
            if last:
                (y,) = call(last_dual_kernel, (jax.ShapeDtypeStruct((scen, span, BS), f32),), 4)(*args, y)
            else:
                y_own, y_far = (duals, y_half) if first else (y, y)
                y, y_half = call(dual_kernel, (shape(2 * span, f32), shape(2 * span, bf16)), 5)(*args, y_own, y_far)
        else:
            image = lax.psum_scatter(own_image, "col", scatter_dimension=0, tiled=True)
            y, y_half = call(whole_dual_kernel, (shape(span, f32), shape(span, bf16)), 3)(
                duals[:span] if first else y, duals[span:], image
            )

    y = y if direct else jnp.transpose(y, (1, 0, 2))
    return (x[0].reshape(scen, 1, -1), y.reshape(scen, 1, -1))


def solution(mesh):
    return jax.shard_map(
        per_device,
        mesh=mesh,
        in_specs=(
            P("grp", "col", "row"),
            P("grp", "row", "col"),
            P("grp", "col", "row"),
            P("grp", "row", "col"),
            P(("grp", "col"), "row"),
            P(("grp", "col"), "row"),
            P(("grp", "col"), "row", None, None, None),
            P(("grp", "col"), "row", None),
            P(("grp", "col"), "row", None),
            P(("grp", "col"), "row"),
        ),
        out_specs=(P("grp", "col", "row"), P("grp", "row", "col")),
        check_vma=False,
    )
```

time: 874 us -> 201 us (0.23)
  waiting for transfers between devices: 445 us -> 100 us
  blocking collectives: 185 us -> 0 us
  other arithmetic: 126 us -> 0.01 us
  starting transfers between devices: 0.5 us -> 78.6 us
  matrix products: 73 us -> 0 us
  local copies, waits for them, and re-layouts: 26.1 us -> 0 us
  Pallas kernels: 0 us -> 23.7 us
  between operations: 15.6 us -> 1.48 us
    reduce_scatter x12 -> x0, waiting for transfers between devices: 445 us -> none  [the longest x6 385 us: per_device(): lax.psum_scatter(partial_image, 'col', scatter_dimension=1, tiled=True)]
    all_gather x12 -> x0, blocking collectives: 185 us -> none  [the longest x6 173 us: per_device(): lax.all_gather(y_state.astype(jnp.bfloat16), 'col', axis=1, tiled=True)]
    scatter-add x12 -> x0, other arithmetic: 109 us -> none  [the longest x6 55.2 us: backward_tile(): summed = jax.ops.segment_sum(prod, bcol, num_segments=segments)]
    ppermute x0 -> x50, waiting for transfers between devices: none -> 100 us  [the longest x43 93.4 us: partner(): return lax.ppermute(a, 'col', [(i, i ^ m) for i in range(n_col)])]
    ppermute x0 -> x50, starting transfers between devices: none -> 78.6 us  [the longest x43 74.9 us: partner(): return lax.ppermute(a, 'col', [(i, i ^ m) for i in range(n_col)])]
    dot_general x12 -> x0, matrix products: 73 us -> none  [the longest x6 42.7 us: forward_tile(): jnp.einsum('nij,snj->nsi', kb, picked, preferred_element_type=jnp.float32)]
    pallas_call x0 -> x38, Pallas kernels: none -> 23.7 us  [the longest x6 7.09 us: per_device(): call(functools.partial(forward_near_kernel, first), (x_shape, shape(col_b...]
    convert_element_type x11 -> x0, other arithmetic: 14.8 us -> none  [the longest x6 9.2 us: per_device(): x_bar = (2.0 * x_next - x_state).astype(jnp.bfloat16)]
  transfers between devices with their start and end apart: 12 -> 50, of which waited for: 12 -> 48; matrix products, arithmetic and copies ran while one was open for 0% -> 0% of each run, Pallas kernels for 0% -> 5%
where the time goes in v4:
time: 201 us; the launch traced here: 204 us
  waiting for transfers between devices  100 us (50%)
  starting transfers between devices  78.6 us (39%)
  Pallas kernels  23.7 us (12%)
    ppermute x43, waiting for transfers between devices, partner(): return lax.ppermute(a, 'col', [(i, i ^ m) for i in range(n_col)])  93.4 us
    ppermute x43, starting transfers between devices, partner(): return lax.ppermute(a, 'col', [(i, i ^ m) for i in range(n_col)])  74.9 us
    pallas_call x6, Pallas kernels, per_device(): call(functools.partial(forward_near_kernel, first), (x_shape, shape(col_b...  7.09 us
    ppermute x7, waiting for transfers between devices, swap(): return lax.ppermute(a, 'row', [(i, n_row - 1 - i) for i in range(n_row)])  6.97 us
    pallas_call x1, Pallas kernels, per_device(): pl.pallas_call(functools.partial(prepare_kernel, col_blocks, row_blocks),...  4.74 us
  transfers between devices with their start and end apart: 50, of which 48 were waited for; matrix products, arithmetic and copies ran while one was open for 0% of the time, Pallas kernels for 5%

profile of v4, /device:TPU:10, one launch (start us, length us, event | category | flops | bytes accessed | tf_op | source)
XLA Modules:
  0.0 204.1 jit_solution(12477423694353227470)
XLA Ops:
  1.3 1.6 setup_kernel.1
  2.9 2.7 %collective-permute-start = (bf16[16,16,128]{2,1,0:T(8,128)(2,1)S(1)}, bf16[16,16,128]{2,1,0:T(8,128)(2,1)S(1)}, u32[]{:S(2)}, u32[]{:S(2)}) collective-permute-start(bf16[16,16,128]{2,1,0:T(8,128)(2,1)S(1)} %get-tuple-element.62), channel_id=1, source_target_pairs={{0,8},{2,10},{4,12},{6,14},{8,0},{10,2},{12,4},{14,6},{1,9},{3,11}... | collective-permute-start | bytes 196616 | tf_op jit(solution)/shard_map/ppermute | solution.py:321
  5.5 2.6 %collective-permute-done = bf16[16,16,128]{2,1,0:T(8,128)(2,1)S(1)} collective-permute-done((bf16[16,16,128]{2,1,0:T(8,128)(2,1)S(1)}, bf16[16,16,128]{2,1,0:T(8,128)(2,1)S(1)}, u32[]{:S(2)}, u32[]{:S(2)}) %collective-permute-start) | collective-permute-done | bytes 65568 | tf_op jit(solution)/shard_map/ppermute | solution.py:321
  8.2 2.7 %collective-permute-start.3 = (bf16[32,16,128]{2,1,0:T(8,128)(2,1)S(1)}, bf16[32,16,128]{2,1,0:T(8,128)(2,1)S(1)}, u32[]{:S(2)}, u32[]{:S(2)}) collective-permute-start(bf16[32,16,128]{2,1,0:T(8,128)(2,1)S(1)} %pad_maximum_fusion.piece.y_far), channel_id=1, source_target_pairs={{0,6},{2,4},{4,2},{6,0},{8,14},{10,12},{12,10},{14,8},{1,7},{3,5},... | collective-permute-start | bytes 393224 | tf_op jit(solution)/shard_map/ppermute | solution.py:321
  11.8 4.7 %prepare_kernel.1 = (s32[1608]{0:T(1024)S(4)}, bf16[256,128,128]{2,1,0:T(8,128)(2,1)S(1)}) custom-call(s32[4,128]{1,0:T(4,128)S(1)} %get-tuple-element.64.order, bf16[256,128,128]{2,1,0:T(8,128)(2,1)} %bitcast.11), custom_call_target="tpu_custom_call" | custom-call | tf_op jit(solution)/shard_map/prepare_kernel/pallas_call | solution.py:359
  21.1 2.4 %collective-permute-start.6 = (bf16[32,16,128]{2,1,0:T(8,128)(2,1)S(1)}, bf16[32,16,128]{2,1,0:T(8,128)(2,1)S(1)}, u32[]{:S(2)}, u32[]{:S(2)}) collective-permute-start(bf16[32,16,128]{2,1,0:T(8,128)(2,1)S(1)} %get-tuple-element.71), channel_id=1, source_target_pairs={{0,2},{2,0},{4,6},{6,4},{8,10},{10,8},{12,14},{14,12},{1,3},{3,1},... | collective-permute-start | bytes 393224 | tf_op jit(solution)/shard_map/ppermute | solution.py:321
  25.5 2.3 %collective-permute-done.6.refs_0_ = bf16[32,16,128]{2,1,0:T(8,128)(2,1)S(1)} collective-permute-done((bf16[32,16,128]{2,1,0:T(8,128)(2,1)S(1)}, bf16[32,16,128]{2,1,0:T(8,128)(2,1)S(1)}, u32[]{:S(2)}, u32[]{:S(2)}) %collective-permute-start.6) | collective-permute-done | bytes 131104 | tf_op jit(solution)/shard_map/ppermute | solution.py:321
  27.8 1.8 collective-permute-done.7.refs_1_
  29.6 2.2 %collective-permute-done.8.refs_2_ = bf16[32,16,128]{2,1,0:T(8,128)(2,1)S(1)} collective-permute-done((bf16[32,16,128]{2,1,0:T(8,128)(2,1)S(1)}, bf16[32,16,128]{2,1,0:T(8,128)(2,1)S(1)}, u32[]{:S(2)}, u32[]{:S(2)}) %collective-permute-start.8) | collective-permute-done | bytes 131104 | tf_op jit(solution)/shard_map/ppermute | solution.py:321
  31.9 4.3 %collective-permute-start.9 = (bf16[32,16,128]{2,1,0:T(8,128)(2,1)S(1)}, bf16[32,16,128]{2,1,0:T(8,128)(2,1)S(1)}, u32[]{:S(2)}, u32[]{:S(2)}) collective-permute-start(bf16[32,16,128]{2,1,0:T(8,128)(2,1)S(1)} %get-tuple-element.75), channel_id=1, source_target_pairs={{0,8},{2,10},{4,12},{6,14},{8,0},{10,2},{12,4},{14,6},{1,9},{3,11}... | collective-permute-start | bytes 393224 | tf_op jit(solution)/shard_map/ppermute | solution.py:321
  36.2 5.1 %collective-permute-done.9.far = bf16[32,16,128]{2,1,0:T(8,128)(2,1)S(1)} collective-permute-done((bf16[32,16,128]{2,1,0:T(8,128)(2,1)S(1)}, bf16[32,16,128]{2,1,0:T(8,128)(2,1)S(1)}, u32[]{:S(2)}, u32[]{:S(2)}) %collective-permute-start.9) | collective-permute-done | bytes 131104 | tf_op jit(solution)/shard_map/ppermute | solution.py:321
  41.4 2.4 %collective-permute-start.12 = (bf16[32,16,128]{2,1,0:T(8,128)(2,1)S(1)}, bf16[32,16,128]{2,1,0:T(8,128)(2,1)S(1)}, u32[]{:S(2)}, u32[]{:S(2)}) collective-permute-start(bf16[32,16,128]{2,1,0:T(8,128)(2,1)S(1)} %get-tuple-element.76.piece), channel_id=1, source_target_pairs={{0,6},{2,4},{4,2},{6,0},{8,14},{10,12},{12,10},{14,8},{1,7},{3,5},... | collective-permute-start | bytes 393224 | tf_op jit(solution)/shard_map/ppermute | solution.py:321
  45.4 3.4 %collective-permute-done.12.refs_2_ = bf16[32,16,128]{2,1,0:T(8,128)(2,1)S(1)} collective-permute-done((bf16[32,16,128]{2,1,0:T(8,128)(2,1)S(1)}, bf16[32,16,128]{2,1,0:T(8,128)(2,1)S(1)}, u32[]{:S(2)}, u32[]{:S(2)}) %collective-permute-start.12) | collective-permute-done | bytes 131104 | tf_op jit(solution)/shard_map/ppermute | solution.py:321
  53.9 2.3 %collective-permute-start.14 = (bf16[32,16,128]{2,1,0:T(8,128)(2,1)S(1)}, bf16[32,16,128]{2,1,0:T(8,128)(2,1)S(1)}, u32[]{:S(2)}, u32[]{:S(2)}) collective-permute-start(bf16[32,16,128]{2,1,0:T(8,128)(2,1)S(1)} %get-tuple-element.79), channel_id=1, source_target_pairs={{0,2},{2,0},{4,6},{6,4},{8,10},{10,8},{12,14},{14,12},{1,3},{3,1},... | collective-permute-start | bytes 393224 | tf_op jit(solution)/shard_map/ppermute | solution.py:321
  56.7 1.4 collective-permute-start.16
  58.6 1.9 collective-permute-done.14.refs_0_
  61.7 3.3 %collective-permute-done.16.refs_2_ = bf16[32,16,128]{2,1,0:T(8,128)(2,1)S(1)} collective-permute-done((bf16[32,16,128]{2,1,0:T(8,128)(2,1)S(1)}, bf16[32,16,128]{2,1,0:T(8,128)(2,1)S(1)}, u32[]{:S(2)}, u32[]{:S(2)}) %collective-permute-start.16) | collective-permute-done | bytes 131104 | tf_op jit(solution)/shard_map/ppermute | solution.py:321
  65.1 4.2 %collective-permute-start.17 = (bf16[32,16,128]{2,1,0:T(8,128)(2,1)S(1)}, bf16[32,16,128]{2,1,0:T(8,128)(2,1)S(1)}, u32[]{:S(2)}, u32[]{:S(2)}) collective-permute-start(bf16[32,16,128]{2,1,0:T(8,128)(2,1)S(1)} %get-tuple-element.83), channel_id=1, source_target_pairs={{0,8},{2,10},{4,12},{6,14},{8,0},{10,2},{12,4},{14,6},{1,9},{3,11}... | collective-permute-start | bytes 393224 | tf_op jit(solution)/shard_map/ppermute | solution.py:321
  69.3 4.9 %collective-permute-done.17.far = bf16[32,16,128]{2,1,0:T(8,128)(2,1)S(1)} collective-permute-done((bf16[32,16,128]{2,1,0:T(8,128)(2,1)S(1)}, bf16[32,16,128]{2,1,0:T(8,128)(2,1)S(1)}, u32[]{:S(2)}, u32[]{:S(2)}) %collective-permute-start.17) | collective-permute-done | bytes 131104 | tf_op jit(solution)/shard_map/ppermute | solution.py:321
  74.2 1.8 collective-permute-start.20
  76.6 1.4 collective-permute-start.18
  78.3 3.1 %collective-permute-done.20.refs_2_ = bf16[32,16,128]{2,1,0:T(8,128)(2,1)S(1)} collective-permute-done((bf16[32,16,128]{2,1,0:T(8,128)(2,1)S(1)}, bf16[32,16,128]{2,1,0:T(8,128)(2,1)S(1)}, u32[]{:S(2)}, u32[]{:S(2)}) %collective-permute-start.20) | collective-permute-done | bytes 131104 | tf_op jit(solution)/shard_map/ppermute | solution.py:321
  81.4 1.6 collective-permute-done.19.refs_1_
  86.9 2.5 %collective-permute-start.22 = (bf16[32,16,128]{2,1,0:T(8,128)(2,1)S(1)}, bf16[32,16,128]{2,1,0:T(8,128)(2,1)S(1)}, u32[]{:S(2)}, u32[]{:S(2)}) collective-permute-start(bf16[32,16,128]{2,1,0:T(8,128)(2,1)S(1)} %get-tuple-element.88), channel_id=1, source_target_pairs={{0,2},{2,0},{4,6},{6,4},{8,10},{10,8},{12,14},{14,12},{1,3},{3,1},... | collective-permute-start | bytes 393224 | tf_op jit(solution)/shard_map/ppermute | solution.py:321
  90.1 1.4 collective-permute-start.24
  92.0 1.7 collective-permute-done.22.refs_0_
  93.7 1.5 collective-permute-done.23.refs_1_
  95.2 3.1 %collective-permute-done.24.refs_2_ = bf16[32,16,128]{2,1,0:T(8,128)(2,1)S(1)} collective-permute-done((bf16[32,16,128]{2,1,0:T(8,128)(2,1)S(1)}, bf16[32,16,128]{2,1,0:T(8,128)(2,1)S(1)}, u32[]{:S(2)}, u32[]{:S(2)}) %collective-permute-start.24) | collective-permute-done | bytes 131104 | tf_op jit(solution)/shard_map/ppermute | solution.py:321
  98.4 3.8 %collective-permute-start.25 = (bf16[32,16,128]{2,1,0:T(8,128)(2,1)S(1)}, bf16[32,16,128]{2,1,0:T(8,128)(2,1)S(1)}, u32[]{:S(2)}, u32[]{:S(2)}) collective-permute-start(bf16[32,16,128]{2,1,0:T(8,128)(2,1)S(1)} %get-tuple-element.92), channel_id=1, source_target_pairs={{0,8},{2,10},{4,12},{6,14},{8,0},{10,2},{12,4},{14,6},{1,9},{3,11}... | collective-permute-start | bytes 393224 | tf_op jit(solution)/shard_map/ppermute | solution.py:321
  102.2 4.9 %collective-permute-done.25.far = bf16[32,16,128]{2,1,0:T(8,128)(2,1)S(1)} collective-permute-done((bf16[32,16,128]{2,1,0:T(8,128)(2,1)S(1)}, bf16[32,16,128]{2,1,0:T(8,128)(2,1)S(1)}, u32[]{:S(2)}, u32[]{:S(2)}) %collective-permute-start.25) | collective-permute-done | bytes 131104 | tf_op jit(solution)/shard_map/ppermute | solution.py:321
  107.2 2.2 %collective-permute-start.28 = (bf16[32,16,128]{2,1,0:T(8,128)(2,1)S(1)}, bf16[32,16,128]{2,1,0:T(8,128)(2,1)S(1)}, u32[]{:S(2)}, u32[]{:S(2)}) collective-permute-start(bf16[32,16,128]{2,1,0:T(8,128)(2,1)S(1)} %get-tuple-element.94.piece), channel_id=1, source_target_pairs={{0,6},{2,4},{4,2},{6,0},{8,14},{10,12},{12,10},{14,8},{1,7},{3,5},... | collective-permute-start | bytes 393224 | tf_op jit(solution)/shard_map/ppermute | solution.py:321
  109.5 1.4 collective-permute-start.26
  111.2 3.2 %collective-permute-done.28.refs_2_ = bf16[32,16,128]{2,1,0:T(8,128)(2,1)S(1)} collective-permute-done((bf16[32,16,128]{2,1,0:T(8,128)(2,1)S(1)}, bf16[32,16,128]{2,1,0:T(8,128)(2,1)S(1)}, u32[]{:S(2)}, u32[]{:S(2)}) %collective-permute-start.28) | collective-permute-done | bytes 131104 | tf_op jit(solution)/shard_map/ppermute | solution.py:321
  114.4 1.5 collective-permute-done.27.refs_1_
  119.6 2.5 %collective-permute-start.30 = (bf16[32,16,128]{2,1,0:T(8,128)(2,1)S(1)}, bf16[32,16,128]{2,1,0:T(8,128)(2,1)S(1)}, u32[]{:S(2)}, u32[]{:S(2)}) collective-permute-start(bf16[32,16,128]{2,1,0:T(8,128)(2,1)S(1)} %get-tuple-element.97), channel_id=1, source_target_pairs={{0,2},{2,0},{4,6},{6,4},{8,10},{10,8},{12,14},{14,12},{1,3},{3,1},... | collective-permute-start | bytes 393224 | tf_op jit(solution)/shard_map/ppermute | solution.py:321
  122.8 1.4 collective-permute-start.32
  124.7 1.7 collective-permute-done.30.refs_0_
  126.4 1.5 collective-permute-done.31.refs_1_
  127.9 3.1 %collective-permute-done.32.refs_2_ = bf16[32,16,128]{2,1,0:T(8,128)(2,1)S(1)} collective-permute-done((bf16[32,16,128]{2,1,0:T(8,128)(2,1)S(1)}, bf16[32,16,128]{2,1,0:T(8,128)(2,1)S(1)}, u32[]{:S(2)}, u32[]{:S(2)}) %collective-permute-start.32) | collective-permute-done | bytes 131104 | tf_op jit(solution)/shard_map/ppermute | solution.py:321
  131.1 3.9 %collective-permute-start.33 = (bf16[32,16,128]{2,1,0:T(8,128)(2,1)S(1)}, bf16[32,16,128]{2,1,0:T(8,128)(2,1)S(1)}, u32[]{:S(2)}, u32[]{:S(2)}) collective-permute-start(bf16[32,16,128]{2,1,0:T(8,128)(2,1)S(1)} %get-tuple-element.101), channel_id=1, source_target_pairs={{0,8},{2,10},{4,12},{6,14},{8,0},{10,2},{12,4},{14,6},{1,9},{3,11}... | collective-permute-start | bytes 393224 | tf_op jit(solution)/shard_map/ppermute | solution.py:321
  134.9 4.9 %collective-permute-done.33.far = bf16[32,16,128]{2,1,0:T(8,128)(2,1)S(1)} collective-permute-done((bf16[32,16,128]{2,1,0:T(8,128)(2,1)S(1)}, bf16[32,16,128]{2,1,0:T(8,128)(2,1)S(1)}, u32[]{:S(2)}, u32[]{:S(2)}) %collective-permute-start.33) | collective-permute-done | bytes 131104 | tf_op jit(solution)/shard_map/ppermute | solution.py:321
  139.9 2.2 %collective-permute-start.36 = (bf16[32,16,128]{2,1,0:T(8,128)(2,1)S(1)}, bf16[32,16,128]{2,1,0:T(8,128)(2,1)S(1)}, u32[]{:S(2)}, u32[]{:S(2)}) collective-permute-start(bf16[32,16,128]{2,1,0:T(8,128)(2,1)S(1)} %get-tuple-element.103.piece), channel_id=1, source_target_pairs={{0,6},{2,4},{4,2},{6,0},{8,14},{10,12},{12,10},{14,8},{1,7},{3,5},... | collective-permute-start | bytes 393224 | tf_op jit(solution)/shard_map/ppermute | solution.py:321
  142.3 1.4 collective-permute-start.34
  143.9 3.1 %collective-permute-done.36.refs_2_ = bf16[32,16,128]{2,1,0:T(8,128)(2,1)S(1)} collective-permute-done((bf16[32,16,128]{2,1,0:T(8,128)(2,1)S(1)}, bf16[32,16,128]{2,1,0:T(8,128)(2,1)S(1)}, u32[]{:S(2)}, u32[]{:S(2)}) %collective-permute-start.36) | collective-permute-done | bytes 131104 | tf_op jit(solution)/shard_map/ppermute | solution.py:321
  147.1 1.6 collective-permute-done.35.refs_1_
  152.4 2.5 %collective-permute-start.38 = (bf16[32,16,128]{2,1,0:T(8,128)(2,1)S(1)}, bf16[32,16,128]{2,1,0:T(8,128)(2,1)S(1)}, u32[]{:S(2)}, u32[]{:S(2)}) collective-permute-start(bf16[32,16,128]{2,1,0:T(8,128)(2,1)S(1)} %get-tuple-element.106), channel_id=1, source_target_pairs={{0,2},{2,0},{4,6},{6,4},{8,10},{10,8},{12,14},{14,12},{1,3},{3,1},... | collective-permute-start | bytes 393224 | tf_op jit(solution)/shard_map/ppermute | solution.py:321
  155.6 1.4 collective-permute-start.40
  157.7 1.5 collective-permute-done.38.refs_0_
  159.2 1.5 collective-permute-done.39.refs_1_
  160.7 3.1 %collective-permute-done.40.refs_2_ = bf16[32,16,128]{2,1,0:T(8,128)(2,1)S(1)} collective-permute-done((bf16[32,16,128]{2,1,0:T(8,128)(2,1)S(1)}, bf16[32,16,128]{2,1,0:T(8,128)(2,1)S(1)}, u32[]{:S(2)}, u32[]{:S(2)}) %collective-permute-start.40) | collective-permute-done | bytes 131104 | tf_op jit(solution)/shard_map/ppermute | solution.py:321
  163.9 3.8 %collective-permute-start.41 = (bf16[32,16,128]{2,1,0:T(8,128)(2,1)S(1)}, bf16[32,16,128]{2,1,0:T(8,128)(2,1)S(1)}, u32[]{:S(2)}, u32[]{:S(2)}) collective-permute-start(bf16[32,16,128]{2,1,0:T(8,128)(2,1)S(1)} %get-tuple-element.110), channel_id=1, source_target_pairs={{0,8},{2,10},{4,12},{6,14},{8,0},{10,2},{12,4},{14,6},{1,9},{3,11}... | collective-permute-start | bytes 393224 | tf_op jit(solution)/shard_map/ppermute | solution.py:321
  167.7 4.9 %collective-permute-done.41.far = bf16[32,16,128]{2,1,0:T(8,128)(2,1)S(1)} collective-permute-done((bf16[32,16,128]{2,1,0:T(8,128)(2,1)S(1)}, bf16[32,16,128]{2,1,0:T(8,128)(2,1)S(1)}, u32[]{:S(2)}, u32[]{:S(2)}) %collective-permute-start.41) | collective-permute-done | bytes 131104 | tf_op jit(solution)/shard_map/ppermute | solution.py:321
  172.7 2.2 %collective-permute-start.44 = (bf16[32,16,128]{2,1,0:T(8,128)(2,1)S(1)}, bf16[32,16,128]{2,1,0:T(8,128)(2,1)S(1)}, u32[]{:S(2)}, u32[]{:S(2)}) collective-permute-start(bf16[32,16,128]{2,1,0:T(8,128)(2,1)S(1)} %get-tuple-element.112.piece), channel_id=1, source_target_pairs={{0,6},{2,4},{4,2},{6,0},{8,14},{10,12},{12,10},{14,8},{1,7},{3,5},... | collective-permute-start | bytes 393224 | tf_op jit(solution)/shard_map/ppermute | solution.py:321
  175.0 1.4 collective-permute-start.42
  176.7 3.2 %collective-permute-done.44.refs_2_ = bf16[32,16,128]{2,1,0:T(8,128)(2,1)S(1)} collective-permute-done((bf16[32,16,128]{2,1,0:T(8,128)(2,1)S(1)}, bf16[32,16,128]{2,1,0:T(8,128)(2,1)S(1)}, u32[]{:S(2)}, u32[]{:S(2)}) %collective-permute-start.44) | collective-permute-done | bytes 131104 | tf_op jit(solution)/shard_map/ppermute | solution.py:321
  179.9 1.5 collective-permute-done.43.refs_1_
  184.0 1.7 forward_near_kernel.11
  185.8 2.4 %collective-permute-start.46 = (bf16[32,16,128]{2,1,0:T(8,128)(2,1)S(1)}, bf16[32,16,128]{2,1,0:T(8,128)(2,1)S(1)}, u32[]{:S(2)}, u32[]{:S(2)}) collective-permute-start(bf16[32,16,128]{2,1,0:T(8,128)(2,1)S(1)} %get-tuple-element.116), channel_id=1, source_target_pairs={{0,2},{2,0},{4,6},{6,4},{8,10},{10,8},{12,14},{14,12},{1,3},{3,1},... | collective-permute-start | bytes 393224 | tf_op jit(solution)/shard_map/ppermute | solution.py:321
  188.8 1.5 collective-permute-start.48
  190.8 1.7 collective-permute-done.46.refs_0_
  192.5 1.3 collective-permute-done.47.refs_1_
  193.9 3.3 %collective-permute-done.48.refs_2_ = bf16[32,16,128]{2,1,0:T(8,128)(2,1)S(1)} collective-permute-done((bf16[32,16,128]{2,1,0:T(8,128)(2,1)S(1)}, bf16[32,16,128]{2,1,0:T(8,128)(2,1)S(1)}, u32[]{:S(2)}, u32[]{:S(2)}) %collective-permute-start.48) | collective-permute-done | bytes 131104 | tf_op jit(solution)/shard_map/ppermute | solution.py:321
  197.2 3.9 %collective-permute-start.49 = (bf16[16,16,128]{2,1,0:T(8,128)(2,1)S(1)}, bf16[16,16,128]{2,1,0:T(8,128)(2,1)S(1)}, u32[]{:S(2)}, u32[]{:S(2)}) collective-permute-start(bf16[16,16,128]{2,1,0:T(8,128)(2,1)S(1)} %get-tuple-element.120), channel_id=1, source_target_pairs={{0,8},{2,10},{4,12},{6,14},{8,0},{10,2},{12,4},{14,6},{1,9},{3,11}... | collective-permute-start | bytes 196616 | tf_op jit(solution)/shard_map/ppermute | solution.py:321
  201.0 2.3 %collective-permute-done.49.far = bf16[16,16,128]{2,1,0:T(8,128)(2,1)S(1)} collective-permute-done((bf16[16,16,128]{2,1,0:T(8,128)(2,1)S(1)}, bf16[16,16,128]{2,1,0:T(8,128)(2,1)S(1)}, u32[]{:S(2)}, u32[]{:S(2)}) %collective-permute-start.49) | collective-permute-done | bytes 65568 | tf_op jit(solution)/shard_map/ppermute | solution.py:321
  (75 shorter events, 38.9 us)
Async XLA Ops:
  2.9 5.3 %collective-permute-start = (bf16[16,16,128]{2,1,0:T(8,128)(2,1)S(1)}, bf16[16,16,128]{2,1,0:T(8,128)(2,1)S(1)}, u32[]{:S(2)}, u32[]{:S(2)}) collective-permute-start(bf16[16,16,128]{2,1,0:T(8,128)(2,1)S(1)} %get-tuple-element.62), channel_id=1, source_target_pairs={{0,8},{2,10},{4,12},{6,14},{8,0},{10,2},{12,4},{14,6},{1,9},{3,11}... | collective-permute-start | bytes 196616 | tf_op jit(solution)/shard_map/ppermute | solution.py:321
  8.2 8.6 %collective-permute-start.3 = (bf16[32,16,128]{2,1,0:T(8,128)(2,1)S(1)}, bf16[32,16,128]{2,1,0:T(8,128)(2,1)S(1)}, u32[]{:S(2)}, u32[]{:S(2)}) collective-permute-start(bf16[32,16,128]{2,1,0:T(8,128)(2,1)S(1)} %pad_maximum_fusion.piece.y_far), channel_id=1, source_target_pairs={{0,6},{2,4},{4,2},{6,0},{8,14},{10,12},{12,10},{14,8},{1,7},{3,5},... | collective-permute-start | bytes 393224 | tf_op jit(solution)/shard_map/ppermute | solution.py:321
  10.9 6.1 %collective-permute-start.2 = (bf16[32,16,128]{2,1,0:T(8,128)(2,1)S(1)}, bf16[32,16,128]{2,1,0:T(8,128)(2,1)S(1)}, u32[]{:S(2)}, u32[]{:S(2)}) collective-permute-start(bf16[32,16,128]{2,1,0:T(8,128)(2,1)S(1)} %pad_maximum_fusion.piece.y_far), channel_id=1, source_target_pairs={{0,4},{2,6},{4,0},{6,2},{8,12},{10,14},{12,8},{14,10},{1,5},{3,7},... | collective-permute-start | bytes 393224 | tf_op jit(solution)/shard_map/ppermute | solution.py:321
  11.3 5.8 %collective-permute-start.1 = (bf16[32,16,128]{2,1,0:T(8,128)(2,1)S(1)}, bf16[32,16,128]{2,1,0:T(8,128)(2,1)S(1)}, u32[]{:S(2)}, u32[]{:S(2)}) collective-permute-start(bf16[32,16,128]{2,1,0:T(8,128)(2,1)S(1)} %pad_maximum_fusion.piece.y_far), channel_id=1, source_target_pairs={{0,2},{2,0},{4,6},{6,4},{8,10},{10,8},{12,14},{14,12},{1,3},{3,1},... | collective-permute-start | bytes 393224 | tf_op jit(solution)/shard_map/ppermute | solution.py:321
  11.8 7.1 %collective-permute-start.5 = (f32[16,34,128]{2,1,0:T(8,128)S(1)}, f32[16,34,128]{2,1,0:T(8,128)S(1)}, u32[]{:S(2)}, u32[]{:S(2)}) collective-permute-start(f32[16,34,128]{2,1,0:T(8,128)S(1)} %get-tuple-element.69.here_state), channel_id=1, source_target_pairs={{0,1},{1,0},{2,3},{3,2},{4,5},{5,4},{6,7},{7,6},{8,9},{9,8},{10,11... | collective-permute-start | bytes 835592 | tf_op jit(solution)/shard_map/ppermute | solution.py:318
  17.6 2.4 %collective-permute-start.4 = (f32[32,16,128]{2,1,0:T(8,128)S(1)}, f32[32,16,128]{2,1,0:T(8,128)S(1)}, u32[]{:S(2)}, u32[]{:S(2)}) collective-permute-start(f32[32,16,128]{2,1,0:T(8,128)S(1)} %backward_near_kernel.6.own), channel_id=1, source_target_pairs={{0,1},{1,0},{2,3},{3,2},{4,5},{5,4},{6,7},{7,6},{8,9},{9,8},{10,11... | collective-permute-start | bytes 786440 | tf_op jit(solution)/shard_map/ppermute | solution.py:318
  21.1 6.7 %collective-permute-start.6 = (bf16[32,16,128]{2,1,0:T(8,128)(2,1)S(1)}, bf16[32,16,128]{2,1,0:T(8,128)(2,1)S(1)}, u32[]{:S(2)}, u32[]{:S(2)}) collective-permute-start(bf16[32,16,128]{2,1,0:T(8,128)(2,1)S(1)} %get-tuple-element.71), channel_id=1, source_target_pairs={{0,2},{2,0},{4,6},{6,4},{8,10},{10,8},{12,14},{14,12},{1,3},{3,1},... | collective-permute-start | bytes 393224 | tf_op jit(solution)/shard_map/ppermute | solution.py:321
  23.5 6.2 %collective-permute-start.7 = (bf16[32,16,128]{2,1,0:T(8,128)(2,1)S(1)}, bf16[32,16,128]{2,1,0:T(8,128)(2,1)S(1)}, u32[]{:S(2)}, u32[]{:S(2)}) collective-permute-start(bf16[32,16,128]{2,1,0:T(8,128)(2,1)S(1)} %get-tuple-element.72), channel_id=1, source_target_pairs={{0,4},{2,6},{4,0},{6,2},{8,12},{10,14},{12,8},{14,10},{1,5},{3,7},... | collective-permute-start | bytes 393224 | tf_op jit(solution)/shard_map/ppermute | solution.py:321
  24.3 7.6 %collective-permute-start.8 = (bf16[32,16,128]{2,1,0:T(8,128)(2,1)S(1)}, bf16[32,16,128]{2,1,0:T(8,128)(2,1)S(1)}, u32[]{:S(2)}, u32[]{:S(2)}) collective-permute-start(bf16[32,16,128]{2,1,0:T(8,128)(2,1)S(1)} %get-tuple-element.73), channel_id=1, source_target_pairs={{0,6},{2,4},{4,2},{6,0},{8,14},{10,12},{12,10},{14,8},{1,7},{3,5},... | collective-permute-start | bytes 393224 | tf_op jit(solution)/shard_map/ppermute | solution.py:321
  31.9 9.4 %collective-permute-start.9 = (bf16[32,16,128]{2,1,0:T(8,128)(2,1)S(1)}, bf16[32,16,128]{2,1,0:T(8,128)(2,1)S(1)}, u32[]{:S(2)}, u32[]{:S(2)}) collective-permute-start(bf16[32,16,128]{2,1,0:T(8,128)(2,1)S(1)} %get-tuple-element.75), channel_id=1, source_target_pairs={{0,8},{2,10},{4,12},{6,14},{8,0},{10,2},{12,4},{14,6},{1,9},{3,11}... | collective-permute-start | bytes 393224 | tf_op jit(solution)/shard_map/ppermute | solution.py:321
  41.4 7.3 %collective-permute-start.12 = (bf16[32,16,128]{2,1,0:T(8,128)(2,1)S(1)}, bf16[32,16,128]{2,1,0:T(8,128)(2,1)S(1)}, u32[]{:S(2)}, u32[]{:S(2)}) collective-permute-start(bf16[32,16,128]{2,1,0:T(8,128)(2,1)S(1)} %get-tuple-element.76.piece), channel_id=1, source_target_pairs={{0,6},{2,4},{4,2},{6,0},{8,14},{10,12},{12,10},{14,8},{1,7},{3,5},... | collective-permute-start | bytes 393224 | tf_op jit(solution)/shard_map/ppermute | solution.py:321
  43.8 6.1 %collective-permute-start.11 = (bf16[32,16,128]{2,1,0:T(8,128)(2,1)S(1)}, bf16[32,16,128]{2,1,0:T(8,128)(2,1)S(1)}, u32[]{:S(2)}, u32[]{:S(2)}) collective-permute-start(bf16[32,16,128]{2,1,0:T(8,128)(2,1)S(1)} %get-tuple-element.76.piece), channel_id=1, source_target_pairs={{0,4},{2,6},{4,0},{6,2},{8,12},{10,14},{12,8},{14,10},{1,5},{3,7},... | collective-permute-start | bytes 393224 | tf_op jit(solution)/shard_map/ppermute | solution.py:321
  43.9 6.7 %collective-permute-start.10 = (bf16[32,16,128]{2,1,0:T(8,128)(2,1)S(1)}, bf16[32,16,128]{2,1,0:T(8,128)(2,1)S(1)}, u32[]{:S(2)}, u32[]{:S(2)}) collective-permute-start(bf16[32,16,128]{2,1,0:T(8,128)(2,1)S(1)} %get-tuple-element.76.piece), channel_id=1, source_target_pairs={{0,2},{2,0},{4,6},{6,4},{8,10},{10,8},{12,14},{14,12},{1,3},{3,1},... | collective-permute-start | bytes 393224 | tf_op jit(solution)/shard_map/ppermute | solution.py:321
  51.2 1.6 collective-permute-start.13
  53.9 6.6 %collective-permute-start.14 = (bf16[32,16,128]{2,1,0:T(8,128)(2,1)S(1)}, bf16[32,16,128]{2,1,0:T(8,128)(2,1)S(1)}, u32[]{:S(2)}, u32[]{:S(2)}) collective-permute-start(bf16[32,16,128]{2,1,0:T(8,128)(2,1)S(1)} %get-tuple-element.79), channel_id=1, source_target_pairs={{0,2},{2,0},{4,6},{6,4},{8,10},{10,8},{12,14},{14,12},{1,3},{3,1},... | collective-permute-start | bytes 393224 | tf_op jit(solution)/shard_map/ppermute | solution.py:321
  56.2 5.5 %collective-permute-start.15 = (bf16[32,16,128]{2,1,0:T(8,128)(2,1)S(1)}, bf16[32,16,128]{2,1,0:T(8,128)(2,1)S(1)}, u32[]{:S(2)}, u32[]{:S(2)}) collective-permute-start(bf16[32,16,128]{2,1,0:T(8,128)(2,1)S(1)} %get-tuple-element.80), channel_id=1, source_target_pairs={{0,4},{2,6},{4,0},{6,2},{8,12},{10,14},{12,8},{14,10},{1,5},{3,7},... | collective-permute-start | bytes 393224 | tf_op jit(solution)/shard_map/ppermute | solution.py:321
  56.7 8.3 %collective-permute-start.16 = (bf16[32,16,128]{2,1,0:T(8,128)(2,1)S(1)}, bf16[32,16,128]{2,1,0:T(8,128)(2,1)S(1)}, u32[]{:S(2)}, u32[]{:S(2)}) collective-permute-start(bf16[32,16,128]{2,1,0:T(8,128)(2,1)S(1)} %get-tuple-element.81), channel_id=1, source_target_pairs={{0,6},{2,4},{4,2},{6,0},{8,14},{10,12},{12,10},{14,8},{1,7},{3,5},... | collective-permute-start | bytes 393224 | tf_op jit(solution)/shard_map/ppermute | solution.py:321
  65.1 9.1 %collective-permute-start.17 = (bf16[32,16,128]{2,1,0:T(8,128)(2,1)S(1)}, bf16[32,16,128]{2,1,0:T(8,128)(2,1)S(1)}, u32[]{:S(2)}, u32[]{:S(2)}) collective-permute-start(bf16[32,16,128]{2,1,0:T(8,128)(2,1)S(1)} %get-tuple-element.83), channel_id=1, source_target_pairs={{0,8},{2,10},{4,12},{6,14},{8,0},{10,2},{12,4},{14,6},{1,9},{3,11}... | collective-permute-start | bytes 393224 | tf_op jit(solution)/shard_map/ppermute | solution.py:321
  74.2 7.2 %collective-permute-start.20 = (bf16[32,16,128]{2,1,0:T(8,128)(2,1)S(1)}, bf16[32,16,128]{2,1,0:T(8,128)(2,1)S(1)}, u32[]{:S(2)}, u32[]{:S(2)}) collective-permute-start(bf16[32,16,128]{2,1,0:T(8,128)(2,1)S(1)} %get-tuple-element.85.piece), channel_id=1, source_target_pairs={{0,6},{2,4},{4,2},{6,0},{8,14},{10,12},{12,10},{14,8},{1,7},{3,5},... | collective-permute-start | bytes 393224 | tf_op jit(solution)/shard_map/ppermute | solution.py:321
  76.0 7.0 %collective-permute-start.19 = (bf16[32,16,128]{2,1,0:T(8,128)(2,1)S(1)}, bf16[32,16,128]{2,1,0:T(8,128)(2,1)S(1)}, u32[]{:S(2)}, u32[]{:S(2)}) collective-permute-start(bf16[32,16,128]{2,1,0:T(8,128)(2,1)S(1)} %get-tuple-element.85.piece), channel_id=1, source_target_pairs={{0,4},{2,6},{4,0},{6,2},{8,12},{10,14},{12,8},{14,10},{1,5},{3,7},... | collective-permute-start | bytes 393224 | tf_op jit(solution)/shard_map/ppermute | solution.py:321
  76.6 6.8 %collective-permute-start.18 = (bf16[32,16,128]{2,1,0:T(8,128)(2,1)S(1)}, bf16[32,16,128]{2,1,0:T(8,128)(2,1)S(1)}, u32[]{:S(2)}, u32[]{:S(2)}) collective-permute-start(bf16[32,16,128]{2,1,0:T(8,128)(2,1)S(1)} %get-tuple-element.85.piece), channel_id=1, source_target_pairs={{0,2},{2,0},{4,6},{6,4},{8,10},{10,8},{12,14},{14,12},{1,3},{3,1},... | collective-permute-start | bytes 393224 | tf_op jit(solution)/shard_map/ppermute | solution.py:321
  84.1 1.7 collective-permute-start.21
  86.9 6.8 %collective-permute-start.22 = (bf16[32,16,128]{2,1,0:T(8,128)(2,1)S(1)}, bf16[32,16,128]{2,1,0:T(8,128)(2,1)S(1)}, u32[]{:S(2)}, u32[]{:S(2)}) collective-permute-start(bf16[32,16,128]{2,1,0:T(8,128)(2,1)S(1)} %get-tuple-element.88), channel_id=1, source_target_pairs={{0,2},{2,0},{4,6},{6,4},{8,10},{10,8},{12,14},{14,12},{1,3},{3,1},... | collective-permute-start | bytes 393224 | tf_op jit(solution)/shard_map/ppermute | solution.py:321
  89.4 5.8 %collective-permute-start.23 = (bf16[32,16,128]{2,1,0:T(8,128)(2,1)S(1)}, bf16[32,16,128]{2,1,0:T(8,128)(2,1)S(1)}, u32[]{:S(2)}, u32[]{:S(2)}) collective-permute-start(bf16[32,16,128]{2,1,0:T(8,128)(2,1)S(1)} %get-tuple-element.89), channel_id=1, source_target_pairs={{0,4},{2,6},{4,0},{6,2},{8,12},{10,14},{12,8},{14,10},{1,5},{3,7},... | collective-permute-start | bytes 393224 | tf_op jit(solution)/shard_map/ppermute | solution.py:321
  90.1 8.2 %collective-permute-start.24 = (bf16[32,16,128]{2,1,0:T(8,128)(2,1)S(1)}, bf16[32,16,128]{2,1,0:T(8,128)(2,1)S(1)}, u32[]{:S(2)}, u32[]{:S(2)}) collective-permute-start(bf16[32,16,128]{2,1,0:T(8,128)(2,1)S(1)} %get-tuple-element.90), channel_id=1, source_target_pairs={{0,6},{2,4},{4,2},{6,0},{8,14},{10,12},{12,10},{14,8},{1,7},{3,5},... | collective-permute-start | bytes 393224 | tf_op jit(solution)/shard_map/ppermute | solution.py:321
  98.4 8.7 %collective-permute-start.25 = (bf16[32,16,128]{2,1,0:T(8,128)(2,1)S(1)}, bf16[32,16,128]{2,1,0:T(8,128)(2,1)S(1)}, u32[]{:S(2)}, u32[]{:S(2)}) collective-permute-start(bf16[32,16,128]{2,1,0:T(8,128)(2,1)S(1)} %get-tuple-element.92), channel_id=1, source_target_pairs={{0,8},{2,10},{4,12},{6,14},{8,0},{10,2},{12,4},{14,6},{1,9},{3,11}... | collective-permute-start | bytes 393224 | tf_op jit(solution)/shard_map/ppermute | solution.py:321
  107.2 7.2 %collective-permute-start.28 = (bf16[32,16,128]{2,1,0:T(8,128)(2,1)S(1)}, bf16[32,16,128]{2,1,0:T(8,128)(2,1)S(1)}, u32[]{:S(2)}, u32[]{:S(2)}) collective-permute-start(bf16[32,16,128]{2,1,0:T(8,128)(2,1)S(1)} %get-tuple-element.94.piece), channel_id=1, source_target_pairs={{0,6},{2,4},{4,2},{6,0},{8,14},{10,12},{12,10},{14,8},{1,7},{3,5},... | collective-permute-start | bytes 393224 | tf_op jit(solution)/shard_map/ppermute | solution.py:321
  109.4 6.5 %collective-permute-start.27 = (bf16[32,16,128]{2,1,0:T(8,128)(2,1)S(1)}, bf16[32,16,128]{2,1,0:T(8,128)(2,1)S(1)}, u32[]{:S(2)}, u32[]{:S(2)}) collective-permute-start(bf16[32,16,128]{2,1,0:T(8,128)(2,1)S(1)} %get-tuple-element.94.piece), channel_id=1, source_target_pairs={{0,4},{2,6},{4,0},{6,2},{8,12},{10,14},{12,8},{14,10},{1,5},{3,7},... | collective-permute-start | bytes 393224 | tf_op jit(solution)/shard_map/ppermute | solution.py:321
  109.5 6.8 %collective-permute-start.26 = (bf16[32,16,128]{2,1,0:T(8,128)(2,1)S(1)}, bf16[32,16,128]{2,1,0:T(8,128)(2,1)S(1)}, u32[]{:S(2)}, u32[]{:S(2)}) collective-permute-start(bf16[32,16,128]{2,1,0:T(8,128)(2,1)S(1)} %get-tuple-element.94.piece), channel_id=1, source_target_pairs={{0,2},{2,0},{4,6},{6,4},{8,10},{10,8},{12,14},{14,12},{1,3},{3,1},... | collective-permute-start | bytes 393224 | tf_op jit(solution)/shard_map/ppermute | solution.py:321
  116.9 1.7 collective-permute-start.29
  119.6 6.8 %collective-permute-start.30 = (bf16[32,16,128]{2,1,0:T(8,128)(2,1)S(1)}, bf16[32,16,128]{2,1,0:T(8,128)(2,1)S(1)}, u32[]{:S(2)}, u32[]{:S(2)}) collective-permute-start(bf16[32,16,128]{2,1,0:T(8,128)(2,1)S(1)} %get-tuple-element.97), channel_id=1, source_target_pairs={{0,2},{2,0},{4,6},{6,4},{8,10},{10,8},{12,14},{14,12},{1,3},{3,1},... | collective-permute-start | bytes 393224 | tf_op jit(solution)/shard_map/ppermute | solution.py:321
  122.1 5.8 %collective-permute-start.31 = (bf16[32,16,128]{2,1,0:T(8,128)(2,1)S(1)}, bf16[32,16,128]{2,1,0:T(8,128)(2,1)S(1)}, u32[]{:S(2)}, u32[]{:S(2)}) collective-permute-start(bf16[32,16,128]{2,1,0:T(8,128)(2,1)S(1)} %get-tuple-element.98), channel_id=1, source_target_pairs={{0,4},{2,6},{4,0},{6,2},{8,12},{10,14},{12,8},{14,10},{1,5},{3,7},... | collective-permute-start | bytes 393224 | tf_op jit(solution)/shard_map/ppermute | solution.py:321
  122.8 8.2 %collective-permute-start.32 = (bf16[32,16,128]{2,1,0:T(8,128)(2,1)S(1)}, bf16[32,16,128]{2,1,0:T(8,128)(2,1)S(1)}, u32[]{:S(2)}, u32[]{:S(2)}) collective-permute-start(bf16[32,16,128]{2,1,0:T(8,128)(2,1)S(1)} %get-tuple-element.99), channel_id=1, source_target_pairs={{0,6},{2,4},{4,2},{6,0},{8,14},{10,12},{12,10},{14,8},{1,7},{3,5},... | collective-permute-start | bytes 393224 | tf_op jit(solution)/shard_map/ppermute | solution.py:321
  131.1 8.8 %collective-permute-start.33 = (bf16[32,16,128]{2,1,0:T(8,128)(2,1)S(1)}, bf16[32,16,128]{2,1,0:T(8,128)(2,1)S(1)}, u32[]{:S(2)}, u32[]{:S(2)}) collective-permute-start(bf16[32,16,128]{2,1,0:T(8,128)(2,1)S(1)} %get-tuple-element.101), channel_id=1, source_target_pairs={{0,8},{2,10},{4,12},{6,14},{8,0},{10,2},{12,4},{14,6},{1,9},{3,11}... | collective-permute-start | bytes 393224 | tf_op jit(solution)/shard_map/ppermute | solution.py:321
  139.9 7.2 %collective-permute-start.36 = (bf16[32,16,128]{2,1,0:T(8,128)(2,1)S(1)}, bf16[32,16,128]{2,1,0:T(8,128)(2,1)S(1)}, u32[]{:S(2)}, u32[]{:S(2)}) collective-permute-start(bf16[32,16,128]{2,1,0:T(8,128)(2,1)S(1)} %get-tuple-element.103.piece), channel_id=1, source_target_pairs={{0,6},{2,4},{4,2},{6,0},{8,14},{10,12},{12,10},{14,8},{1,7},{3,5},... | collective-permute-start | bytes 393224 | tf_op jit(solution)/shard_map/ppermute | solution.py:321
  142.1 6.6 %collective-permute-start.35 = (bf16[32,16,128]{2,1,0:T(8,128)(2,1)S(1)}, bf16[32,16,128]{2,1,0:T(8,128)(2,1)S(1)}, u32[]{:S(2)}, u32[]{:S(2)}) collective-permute-start(bf16[32,16,128]{2,1,0:T(8,128)(2,1)S(1)} %get-tuple-element.103.piece), channel_id=1, source_target_pairs={{0,4},{2,6},{4,0},{6,2},{8,12},{10,14},{12,8},{14,10},{1,5},{3,7},... | collective-permute-start | bytes 393224 | tf_op jit(solution)/shard_map/ppermute | solution.py:321
  142.3 6.8 %collective-permute-start.34 = (bf16[32,16,128]{2,1,0:T(8,128)(2,1)S(1)}, bf16[32,16,128]{2,1,0:T(8,128)(2,1)S(1)}, u32[]{:S(2)}, u32[]{:S(2)}) collective-permute-start(bf16[32,16,128]{2,1,0:T(8,128)(2,1)S(1)} %get-tuple-element.103.piece), channel_id=1, source_target_pairs={{0,2},{2,0},{4,6},{6,4},{8,10},{10,8},{12,14},{14,12},{1,3},{3,1},... | collective-permute-start | bytes 393224 | tf_op jit(solution)/shard_map/ppermute | solution.py:321
  149.6 1.7 collective-permute-start.37
  152.4 6.8 %collective-permute-start.38 = (bf16[32,16,128]{2,1,0:T(8,128)(2,1)S(1)}, bf16[32,16,128]{2,1,0:T(8,128)(2,1)S(1)}, u32[]{:S(2)}, u32[]{:S(2)}) collective-permute-start(bf16[32,16,128]{2,1,0:T(8,128)(2,1)S(1)} %get-tuple-element.106), channel_id=1, source_target_pairs={{0,2},{2,0},{4,6},{6,4},{8,10},{10,8},{12,14},{14,12},{1,3},{3,1},... | collective-permute-start | bytes 393224 | tf_op jit(solution)/shard_map/ppermute | solution.py:321
  154.9 5.8 %collective-permute-start.39 = (bf16[32,16,128]{2,1,0:T(8,128)(2,1)S(1)}, bf16[32,16,128]{2,1,0:T(8,128)(2,1)S(1)}, u32[]{:S(2)}, u32[]{:S(2)}) collective-permute-start(bf16[32,16,128]{2,1,0:T(8,128)(2,1)S(1)} %get-tuple-element.107), channel_id=1, source_target_pairs={{0,4},{2,6},{4,0},{6,2},{8,12},{10,14},{12,8},{14,10},{1,5},{3,7},... | collective-permute-start | bytes 393224 | tf_op jit(solution)/shard_map/ppermute | solution.py:321
  155.6 8.2 %collective-permute-start.40 = (bf16[32,16,128]{2,1,0:T(8,128)(2,1)S(1)}, bf16[32,16,128]{2,1,0:T(8,128)(2,1)S(1)}, u32[]{:S(2)}, u32[]{:S(2)}) collective-permute-start(bf16[32,16,128]{2,1,0:T(8,128)(2,1)S(1)} %get-tuple-element.108), channel_id=1, source_target_pairs={{0,6},{2,4},{4,2},{6,0},{8,14},{10,12},{12,10},{14,8},{1,7},{3,5},... | collective-permute-start | bytes 393224 | tf_op jit(solution)/shard_map/ppermute | solution.py:321
  163.9 8.7 %collective-permute-start.41 = (bf16[32,16,128]{2,1,0:T(8,128)(2,1)S(1)}, bf16[32,16,128]{2,1,0:T(8,128)(2,1)S(1)}, u32[]{:S(2)}, u32[]{:S(2)}) collective-permute-start(bf16[32,16,128]{2,1,0:T(8,128)(2,1)S(1)} %get-tuple-element.110), channel_id=1, source_target_pairs={{0,8},{2,10},{4,12},{6,14},{8,0},{10,2},{12,4},{14,6},{1,9},{3,11}... | collective-permute-start | bytes 393224 | tf_op jit(solution)/shard_map/ppermute | solution.py:321
  172.7 7.2 %collective-permute-start.44 = (bf16[32,16,128]{2,1,0:T(8,128)(2,1)S(1)}, bf16[32,16,128]{2,1,0:T(8,128)(2,1)S(1)}, u32[]{:S(2)}, u32[]{:S(2)}) collective-permute-start(bf16[32,16,128]{2,1,0:T(8,128)(2,1)S(1)} %get-tuple-element.112.piece), channel_id=1, source_target_pairs={{0,6},{2,4},{4,2},{6,0},{8,14},{10,12},{12,10},{14,8},{1,7},{3,5},... | collective-permute-start | bytes 393224 | tf_op jit(solution)/shard_map/ppermute | solution.py:321
  174.9 6.5 %collective-permute-start.43 = (bf16[32,16,128]{2,1,0:T(8,128)(2,1)S(1)}, bf16[32,16,128]{2,1,0:T(8,128)(2,1)S(1)}, u32[]{:S(2)}, u32[]{:S(2)}) collective-permute-start(bf16[32,16,128]{2,1,0:T(8,128)(2,1)S(1)} %get-tuple-element.112.piece), channel_id=1, source_target_pairs={{0,4},{2,6},{4,0},{6,2},{8,12},{10,14},{12,8},{14,10},{1,5},{3,7},... | collective-permute-start | bytes 393224 | tf_op jit(solution)/shard_map/ppermute | solution.py:321
  175.0 6.8 %collective-permute-start.42 = (bf16[32,16,128]{2,1,0:T(8,128)(2,1)S(1)}, bf16[32,16,128]{2,1,0:T(8,128)(2,1)S(1)}, u32[]{:S(2)}, u32[]{:S(2)}) collective-permute-start(bf16[32,16,128]{2,1,0:T(8,128)(2,1)S(1)} %get-tuple-element.112.piece), channel_id=1, source_target_pairs={{0,2},{2,0},{4,6},{6,4},{8,10},{10,8},{12,14},{14,12},{1,3},{3,1},... | collective-permute-start | bytes 393224 | tf_op jit(solution)/shard_map/ppermute | solution.py:321
  182.4 1.7 collective-permute-start.45
  185.8 6.7 %collective-permute-start.46 = (bf16[32,16,128]{2,1,0:T(8,128)(2,1)S(1)}, bf16[32,16,128]{2,1,0:T(8,128)(2,1)S(1)}, u32[]{:S(2)}, u32[]{:S(2)}) collective-permute-start(bf16[32,16,128]{2,1,0:T(8,128)(2,1)S(1)} %get-tuple-element.116), channel_id=1, source_target_pairs={{0,2},{2,0},{4,6},{6,4},{8,10},{10,8},{12,14},{14,12},{1,3},{3,1},... | collective-permute-start | bytes 393224 | tf_op jit(solution)/shard_map/ppermute | solution.py:321
  188.2 5.6 %collective-permute-start.47 = (bf16[32,16,128]{2,1,0:T(8,128)(2,1)S(1)}, bf16[32,16,128]{2,1,0:T(8,128)(2,1)S(1)}, u32[]{:S(2)}, u32[]{:S(2)}) collective-permute-start(bf16[32,16,128]{2,1,0:T(8,128)(2,1)S(1)} %get-tuple-element.117), channel_id=1, source_target_pairs={{0,4},{2,6},{4,0},{6,2},{8,12},{10,14},{12,8},{14,10},{1,5},{3,7},... | collective-permute-start | bytes 393224 | tf_op jit(solution)/shard_map/ppermute | solution.py:321
  188.8 8.3 %collective-permute-start.48 = (bf16[32,16,128]{2,1,0:T(8,128)(2,1)S(1)}, bf16[32,16,128]{2,1,0:T(8,128)(2,1)S(1)}, u32[]{:S(2)}, u32[]{:S(2)}) collective-permute-start(bf16[32,16,128]{2,1,0:T(8,128)(2,1)S(1)} %get-tuple-element.118), channel_id=1, source_target_pairs={{0,6},{2,4},{4,2},{6,0},{8,14},{10,12},{12,10},{14,8},{1,7},{3,5},... | collective-permute-start | bytes 393224 | tf_op jit(solution)/shard_map/ppermute | solution.py:321
  197.2 6.2 %collective-permute-start.49 = (bf16[16,16,128]{2,1,0:T(8,128)(2,1)S(1)}, bf16[16,16,128]{2,1,0:T(8,128)(2,1)S(1)}, u32[]{:S(2)}, u32[]{:S(2)}) collective-permute-start(bf16[16,16,128]{2,1,0:T(8,128)(2,1)S(1)} %get-tuple-element.120), channel_id=1, source_target_pairs={{0,8},{2,10},{4,12},{6,14},{8,0},{10,2},{12,4},{14,6},{1,9},{3,11}... | collective-permute-start | bytes 196616 | tf_op jit(solution)/shard_map/ppermute | solution.py:321

commit v5 on v4

--- a/solution.py
+++ b/solution.py
@@ -9,7 +9,7 @@
 
 BS = 128
 ITERS = 6
-WIDE, NARROW = 48, 16
+WIDE, NARROW = (48, 112), 16
 NN = (((1,), (0,)), ((), ()))
 NT = (((1,), (1,)), ((), ()))
 
@@ -27,8 +27,8 @@
     def first(self, near):
         return self.ref[0] if near else 0
 
-    def count(self, near):
-        return self.ref[2] if near else self.ref[1]
+    def runs(self, near):
+        return self.ref[1 + 2 * near], self.ref[2 + 2 * near]
 
     def slot(self, i):
         return 8 + i
@@ -41,7 +41,7 @@
 
 
 def plan_size(slots, columns):
-    pairs = -(-(slots + 2 * columns) // (2 * NARROW)) * NARROW + 2 * NARROW
+    pairs = -(-(slots + 2 * columns) // (2 * NARROW)) * NARROW + sum(WIDE)
     return pairs, pairs + -(-slots // 2)
 
 
@@ -118,14 +118,17 @@
 
     start = jnp.int32(0)
     for near in range(2):
-        plan_ref[near] = start // 2
         first = start
         for c in range(near * columns, (near + 1) * columns):
             size = ends[c]
             ends[c] = start
             start = start + ((size + 1) // 2) * 2
-        plan_ref[1 + near] = (start - first) // 2
-        start = (start + 2 * NARROW - 1) // (2 * NARROW) * (2 * NARROW)
+        pairs = (start - first) // 2
+        wide = (pairs + WIDE[near] - 1 - 3 * NARROW) // WIDE[near]
+        narrow = (jnp.maximum(pairs - wide * WIDE[near], 0) + NARROW - 1) // NARROW
+        plan_ref[1 + 2 * near] = wide
+        plan_ref[2 + 2 * near] = narrow
+        start = first + 2 * (wide * WIDE[near] + narrow * NARROW)
         if near == 0:
             plan_ref[0] = start // 2
     ends[2 * columns] = 2 * plan.pairs
@@ -143,16 +146,15 @@
 
 
 def over_pairs(plan, near, step):
-    begin, pairs = plan.first(near), plan.count(near)
-    wide = pairs // WIDE
+    begin, (wide, narrow) = plan.first(near), plan.runs(near)
 
     def run(i, _, size, start):
         step(start + i * size, size)
         return 0
 
-    lax.fori_loop(0, wide, functools.partial(run, size=WIDE, start=begin), 0)
-    rest = wide * WIDE
-    lax.fori_loop(0, (pairs - rest + NARROW - 1) // NARROW, functools.partial(run, size=NARROW, start=begin + rest), 0)
+    lax.fori_loop(0, wide, functools.partial(run, size=WIDE[near], start=begin), 0)
+    begin = begin + wide * WIDE[near]
+    lax.fori_loop(0, narrow, functools.partial(run, size=NARROW, start=begin), 0)
 
 
 def transposed_products(plan, near, tile, vecs, acc):
@@ -175,8 +177,9 @@
     over_pairs(plan, near, step)
 
 
-def products(plan, near, tile, vecs, acc):
+def products(plan, near, tile, flipped, vecs, acc):
     ref = plan.ref
+    axis, dims = (1, NN) if flipped else (0, NT)
 
     def step(first, n):
         terms = []
@@ -185,7 +188,10 @@
             right = [tile[ref[plan.slot(i + k)]] for k in range(2)]
             terms.append(
                 lax.dot_general(
-                    vecs[ref[plan.col(first + u)]], jnp.concatenate(right, axis=0), NT, preferred_element_type=jnp.float32
+                    vecs[ref[plan.col(first + u)]],
+                    jnp.concatenate(right, axis=axis),
+                    dims,
+                    preferred_element_type=jnp.float32,
                 )
             )
         for u in range(n):
@@ -243,7 +249,7 @@
     x_out, x_bar, *pieces, acc = refs if first else refs[1:]
     primal_step(own, other, here_state, there_state, x_ref, x_out, x_bar)
     if pieces:
-        products(Plan(plan_ref, tile.shape[0], x_bar.shape[0]), True, tile, x_bar, acc)
+        products(Plan(plan_ref, tile.shape[0], x_bar.shape[0]), True, tile, not first, x_bar, acc)
         half = len(pieces) + 1
         span = pieces[0].shape[0] // 2
         for m in range(1, half):
@@ -251,11 +257,21 @@
             pieces[m - 1][pl.ds(span, span)] = acc[pl.ds((m + half) * span, span)].astype(pieces[m - 1].dtype)
 
 
-def forward_own_kernel(plan_ref, tile, x_bar, piece, acc):
-    products(Plan(plan_ref, tile.shape[0], x_bar.shape[0]), False, tile, x_bar, acc)
+def forward_own_kernel(flipped, plan_ref, tile, x_bar, piece, acc):
+    products(Plan(plan_ref, tile.shape[0], x_bar.shape[0]), False, tile, flipped, x_bar, acc)
     span = piece.shape[0] // 2
     piece[pl.ds(0, span)] = acc[pl.ds(0, span)]
     piece[pl.ds(span, span)] = acc[pl.ds((acc.shape[0] - 1) // 2, span)]
+
+
+def flip_kernel(after, tile, flipped, done):
+    def run(i, _):
+        for k in range(8):
+            flipped[i * 8 + k] = tile[i * 8 + k].T
+        return 0
+
+    lax.fori_loop(0, tile.shape[0] // 8, run, 0)
+    done[...] = jnp.zeros(done.shape, done.dtype)
 
 
 def near_sum_kernel(duals, own, *refs):
@@ -271,7 +287,8 @@
         sent[pl.ds(0, span)] = (image[:span] - duals[pl.ds(span, span)]).astype(sent.dtype)
 
 
-def dual_kernel(duals, near, far, y_own, y_far, y_out, y_half):
+def dual_kernel(duals, near, far, y_own, y_far, *refs):
+    y_out, y_half = refs[-2:]
     span = near.shape[0] // 2
     here, there = pl.ds(0, span), pl.ds(span, span)
     own = y_own[here] + 0.9 * (duals[there] - (near[here] + far[there].astype(jnp.float32)))
@@ -380,15 +397,6 @@
         backward_near_kernel, (shape(col_blocks, f32),), 1 + half, ((row_blocks + 1, bf16),), 1, flops
     )
     near_pieces = (shape(2 * span, bf16),) * (half - 1) if direct else ()
-    forward_own = call(
-        forward_own_kernel,
-        (shape(2 * span if direct else row_blocks, f32),),
-        2,
-        ((row_blocks + 1, f32),),
-        1,
-        flops,
-    )
-
     x = ()
     for step in range(ITERS):
         first, last = step == 0, step == ITERS - 1
@@ -406,9 +414,19 @@
             ((row_blocks + 1, f32),),
             1,
             flops,
-        )(plan, tile, grad, swap(grad), state, other_state, *x)
+        )(plan, tile if first else flipped, grad, swap(grad), state, other_state, *x)
         x = (x,)
-        (own_image,) = forward_own(plan, tile, x_bar)
+        (own_image,) = call(
+            functools.partial(forward_own_kernel, not first),
+            (shape(2 * span if direct else row_blocks, f32),),
+            2,
+            ((row_blocks + 1, f32),),
+            1,
+            flops,
+        )(plan, tile if first else flipped, x_bar)
+        token = ()
+        if first:
+            after = own_image
         if direct:
             image = [partner(image[m - 1], m) for m in range(1, half)]
             kept = 1 if last else 2
@@ -416,11 +434,25 @@
                 duals, own_image, *image
             )
             args = (duals, total, partner(sent, half))
+            after = total
+        if first:
+            flipped, *token = pl.pallas_call(
+                flip_kernel,
+                out_shape=(pltpu.VMEM(blocks.shape, blocks.dtype), jax.ShapeDtypeStruct((8, BS), f32)),
+                in_specs=[VMEM] * 2,
+                out_specs=(VMEM,) * 2,
+                compiler_params=PARAMS,
+                cost_estimate=pl.CostEstimate(flops=16 * flops, bytes_accessed=0, transcendentals=0),
+                name="flip_kernel",
+            )(after, tile)
+        if direct:
             if last:
                 (y,) = call(last_dual_kernel, (jax.ShapeDtypeStruct((scen, span, BS), f32),), 4)(*args, y)
             else:
                 y_own, y_far = (duals, y_half) if first else (y, y)
-                y, y_half = call(dual_kernel, (shape(2 * span, f32), shape(2 * span, bf16)), 5)(*args, y_own, y_far)
+                y, y_half = call(dual_kernel, (shape(2 * span, f32), shape(2 * span, bf16)), 5 + len(token))(
+                    *args, y_own, y_far, *token
+                )
         else:
             image = lax.psum_scatter(own_image, "col", scatter_dimension=0, tiled=True)
             y, y_half = call(whole_dual_kernel, (shape(span, f32), shape(span, bf16)), 3)(

time: 201 us -> 201 us (level); the launches traced: 204 us -> 199 us
  Pallas kernels: 23.7 us -> 41.3 us
  starting transfers between devices: 78.6 us -> 66.9 us
  waiting for transfers between devices: 100 us -> 89.5 us
    ppermute x43, waiting for transfers between devices: 93.4 us -> 80.4 us  [partner(): return lax.ppermute(a, 'col', [(i, i ^ m) for i in range(n_col)])]
    ppermute x43, starting transfers between devices: 74.9 us -> 66.4 us  [partner(): return lax.ppermute(a, 'col', [(i, i ^ m) for i in range(n_col)])]
    pallas_call x11 -> x12, Pallas kernels: 3.63 us -> 10.6 us  [the longest x6 6.38 us: per_device(): call(functools.partial(forward_own_kernel, not first), (shape(2 * span if...]
    pallas_call x6, Pallas kernels: 7.09 us -> 11 us  [per_device(): call(functools.partial(forward_near_kernel, first), (x_shape, shape(col_b...]
    pallas_call x6, Pallas kernels: 3.65 us -> 7.35 us  [per_device(): grad, = backward_near(plan, tile, *y_near, grad)]
    ppermute x7, starting transfers between devices: 3.72 us -> 0.43 us  [swap(): return lax.ppermute(a, 'row', [(i, n_row - 1 - i) for i in range(n_row)])]
    pallas_call x6, Pallas kernels: 1.82 us -> 4.93 us  [per_device(): grad, = backward_own(plan, tile, y_half)]
    ppermute x7, waiting for transfers between devices: 6.97 us -> 9.12 us  [swap(): return lax.ppermute(a, 'row', [(i, n_row - 1 - i) for i in range(n_row)])]
  transfers between devices with their start and end apart: 50 -> 50, of which waited for: 48 -> 46; matrix products, arithmetic and copies ran while one was open for 0% -> 0% of each run, Pallas kernels for 5% -> 11%
where the time goes in v5:
time: 201 us; the launch traced here: 199 us
  waiting for transfers between devices  89.5 us (45%)
  starting transfers between devices  66.9 us (33%)
  Pallas kernels  41.3 us (21%)
    ppermute x43, waiting for transfers between devices, partner(): return lax.ppermute(a, 'col', [(i, i ^ m) for i in range(n_col)])  80.4 us
    ppermute x43, starting transfers between devices, partner(): return lax.ppermute(a, 'col', [(i, i ^ m) for i in range(n_col)])  66.4 us
    pallas_call x6, Pallas kernels, per_device(): call(functools.partial(forward_near_kernel, first), (x_shape, shape(col_b...  11 us
    ppermute x7, waiting for transfers between devices, swap(): return lax.ppermute(a, 'row', [(i, n_row - 1 - i) for i in range(n_row)])  9.12 us
    pallas_call x6, Pallas kernels, per_device(): grad, = backward_near(plan, tile, *y_near, grad)  7.35 us
    pallas_call x6, Pallas kernels, per_device(): call(functools.partial(forward_own_kernel, not first), (shape(2 * span if...  6.38 us
    pallas_call x6, Pallas kernels, per_device(): grad, = backward_own(plan, tile, y_half)  4.93 us
    pallas_call x1, Pallas kernels, per_device(): pl.pallas_call(functools.partial(prepare_kernel, col_blocks, row_blocks),...  4.77 us
  transfers between devices with their start and end apart: 50, of which 46 were waited for; matrix products, arithmetic and copies ran while one was open for 0% of the time, Pallas kernels for 11%

profile of v5, /device:TPU:10, one launch (start us, length us, event | category | flops | bytes accessed | tf_op | source)
XLA Modules:
  0.0 199.4 jit_solution(10268321740174863358)
XLA Ops:
  1.3 1.6 setup_kernel.1
  2.9 2.7 %collective-permute-start = (bf16[16,16,128]{2,1,0:T(8,128)(2,1)S(1)}, bf16[16,16,128]{2,1,0:T(8,128)(2,1)S(1)}, u32[]{:S(2)}, u32[]{:S(2)}) collective-permute-start(bf16[16,16,128]{2,1,0:T(8,128)(2,1)S(1)} %get-tuple-element.64), channel_id=1, source_target_pairs={{0,8},{2,10},{4,12},{6,14},{8,0},{10,2},{12,4},{14,6},{1,9},{3,11}... | collective-permute-start | bytes 196616 | tf_op jit(solution)/shard_map/ppermute | solution.py:338
  5.5 2.6 %collective-permute-done = bf16[16,16,128]{2,1,0:T(8,128)(2,1)S(1)} collective-permute-done((bf16[16,16,128]{2,1,0:T(8,128)(2,1)S(1)}, bf16[16,16,128]{2,1,0:T(8,128)(2,1)S(1)}, u32[]{:S(2)}, u32[]{:S(2)}) %collective-permute-start) | collective-permute-done | bytes 65568 | tf_op jit(solution)/shard_map/ppermute | solution.py:338
  8.2 2.7 %collective-permute-start.3 = (bf16[32,16,128]{2,1,0:T(8,128)(2,1)S(1)}, bf16[32,16,128]{2,1,0:T(8,128)(2,1)S(1)}, u32[]{:S(2)}, u32[]{:S(2)}) collective-permute-start(bf16[32,16,128]{2,1,0:T(8,128)(2,1)S(1)} %pad_maximum_fusion.piece.y_far), channel_id=1, source_target_pairs={{0,6},{2,4},{4,2},{6,0},{8,14},{10,12},{12,10},{14,8},{1,7},{3,5},... | collective-permute-start | bytes 393224 | tf_op jit(solution)/shard_map/ppermute | solution.py:338
  11.8 4.8 %prepare_kernel.1 = (s32[2248]{0:T(1024)S(4)}, bf16[256,128,128]{2,1,0:T(8,128)(2,1)S(1)}) custom-call(s32[4,128]{1,0:T(4,128)S(1)} %get-tuple-element.66.order, bf16[256,128,128]{2,1,0:T(8,128)(2,1)} %bitcast.11), custom_call_target="tpu_custom_call" | custom-call | tf_op jit(solution)/shard_map/prepare_kernel/pallas_call | solution.py:376
  18.7 1.5 collective-permute-done.4.other
  20.2 2.3 %forward_near_kernel.6 = (f32[32,16,128]{2,1,0:T(8,128)S(1)}, bf16[32,16,128]{2,1,0:T(8,128)(2,1)S(1)}, bf16[32,16,128]{2,1,0:T(8,128)(2,1)S(1)}, bf16[32,16,128...) custom-call(s32[2248]{0:T(1024)S(4)} %get-tuple-element.67.plan_ref, bf16[256,128,128]{2,1,0:T(8,128)(2,1)S(1)} %get-tuple-element.69.tile, ...), custom_call_target="tpu_custom_call" | custom-call | flops 134217728 | tf_op jit(solution)/shard_map/forward_near_kernel/pallas_call | solution.py:410
  22.8 2.9 %collective-permute-start.7 = (bf16[32,16,128]{2,1,0:T(8,128)(2,1)S(1)}, bf16[32,16,128]{2,1,0:T(8,128)(2,1)S(1)}, u32[]{:S(2)}, u32[]{:S(2)}) collective-permute-start(bf16[32,16,128]{2,1,0:T(8,128)(2,1)S(1)} %get-tuple-element.74), channel_id=1, source_target_pairs={{0,4},{2,6},{4,0},{6,2},{8,12},{10,14},{12,8},{14,10},{1,5},{3,7},... | collective-permute-start | bytes 393224 | tf_op jit(solution)/shard_map/ppermute | solution.py:338
  26.1 1.3 forward_own_kernel.6.own
  27.6 2.4 %collective-permute-done.7.refs_1_ = bf16[32,16,128]{2,1,0:T(8,128)(2,1)S(1)} collective-permute-done((bf16[32,16,128]{2,1,0:T(8,128)(2,1)S(1)}, bf16[32,16,128]{2,1,0:T(8,128)(2,1)S(1)}, u32[]{:S(2)}, u32[]{:S(2)}) %collective-permute-start.7) | collective-permute-done | bytes 131104 | tf_op jit(solution)/shard_map/ppermute | solution.py:338
  30.0 2.2 %collective-permute-done.8.refs_2_ = bf16[32,16,128]{2,1,0:T(8,128)(2,1)S(1)} collective-permute-done((bf16[32,16,128]{2,1,0:T(8,128)(2,1)S(1)}, bf16[32,16,128]{2,1,0:T(8,128)(2,1)S(1)}, u32[]{:S(2)}, u32[]{:S(2)}) %collective-permute-start.8) | collective-permute-done | bytes 131104 | tf_op jit(solution)/shard_map/ppermute | solution.py:338
  32.2 3.6 %collective-permute-start.9 = (bf16[32,16,128]{2,1,0:T(8,128)(2,1)S(1)}, bf16[32,16,128]{2,1,0:T(8,128)(2,1)S(1)}, u32[]{:S(2)}, u32[]{:S(2)}) collective-permute-start(bf16[32,16,128]{2,1,0:T(8,128)(2,1)S(1)} %get-tuple-element.78), channel_id=1, source_target_pairs={{0,8},{2,10},{4,12},{6,14},{8,0},{10,2},{12,4},{14,6},{1,9},{3,11}... | collective-permute-start | bytes 393224 | tf_op jit(solution)/shard_map/ppermute | solution.py:338
  35.8 3.9 %flip_kernel.1 = (bf16[256,128,128]{2,1,0:T(8,128)(2,1)S(1)}, f32[8,128]{1,0:T(8,128)S(1)}) custom-call(f32[32,16,128]{2,1,0:T(8,128)S(1)} %get-tuple-element.76.after.near, bf16[256,128,128]{2,1,0:T(8,128)(2,1)S(1)} %get-tuple-element.69.tile), custom_call_target="tpu_custom_call" | custom-call | flops 2147483648 | tf_op jit(solution)/shard_map/flip_kernel/pallas_call | solution.py:439
  40.7 3.1 %collective-permute-start.12 = (bf16[32,16,128]{2,1,0:T(8,128)(2,1)S(1)}, bf16[32,16,128]{2,1,0:T(8,128)(2,1)S(1)}, u32[]{:S(2)}, u32[]{:S(2)}) collective-permute-start(bf16[32,16,128]{2,1,0:T(8,128)(2,1)S(1)} %get-tuple-element.80.piece), channel_id=1, source_target_pairs={{0,6},{2,4},{4,2},{6,0},{8,14},{10,12},{12,10},{14,8},{1,7},{3,5},... | collective-permute-start | bytes 393224 | tf_op jit(solution)/shard_map/ppermute | solution.py:338
  45.2 2.8 %collective-permute-done.12.refs_2_ = bf16[32,16,128]{2,1,0:T(8,128)(2,1)S(1)} collective-permute-done((bf16[32,16,128]{2,1,0:T(8,128)(2,1)S(1)}, bf16[32,16,128]{2,1,0:T(8,128)(2,1)S(1)}, u32[]{:S(2)}, u32[]{:S(2)}) %collective-permute-start.12) | collective-permute-done | bytes 131104 | tf_op jit(solution)/shard_map/ppermute | solution.py:338
  48.0 1.4 collective-permute-done.11.refs_1_
  51.5 1.5 collective-permute-done.13.other
  53.0 1.7 forward_near_kernel.7
  54.8 3.3 %collective-permute-start.15 = (bf16[32,16,128]{2,1,0:T(8,128)(2,1)S(1)}, bf16[32,16,128]{2,1,0:T(8,128)(2,1)S(1)}, u32[]{:S(2)}, u32[]{:S(2)}) collective-permute-start(bf16[32,16,128]{2,1,0:T(8,128)(2,1)S(1)} %get-tuple-element.84), channel_id=1, source_target_pairs={{0,4},{2,6},{4,0},{6,2},{8,12},{10,14},{12,8},{14,10},{1,5},{3,7},... | collective-permute-start | bytes 393224 | tf_op jit(solution)/shard_map/ppermute | solution.py:338
  59.8 2.6 %collective-permute-done.15.refs_1_ = bf16[32,16,128]{2,1,0:T(8,128)(2,1)S(1)} collective-permute-done((bf16[32,16,128]{2,1,0:T(8,128)(2,1)S(1)}, bf16[32,16,128]{2,1,0:T(8,128)(2,1)S(1)}, u32[]{:S(2)}, u32[]{:S(2)}) %collective-permute-start.15) | collective-permute-done | bytes 131104 | tf_op jit(solution)/shard_map/ppermute | solution.py:338
  62.4 1.9 collective-permute-done.16.refs_2_
  64.4 3.0 %collective-permute-start.17 = (bf16[32,16,128]{2,1,0:T(8,128)(2,1)S(1)}, bf16[32,16,128]{2,1,0:T(8,128)(2,1)S(1)}, u32[]{:S(2)}, u32[]{:S(2)}) collective-permute-start(bf16[32,16,128]{2,1,0:T(8,128)(2,1)S(1)} %get-tuple-element.87), channel_id=1, source_target_pairs={{0,8},{2,10},{4,12},{6,14},{8,0},{10,2},{12,4},{14,6},{1,9},{3,11}... | collective-permute-start | bytes 393224 | tf_op jit(solution)/shard_map/ppermute | solution.py:338
  67.3 5.3 %collective-permute-done.17.far = bf16[32,16,128]{2,1,0:T(8,128)(2,1)S(1)} collective-permute-done((bf16[32,16,128]{2,1,0:T(8,128)(2,1)S(1)}, bf16[32,16,128]{2,1,0:T(8,128)(2,1)S(1)}, u32[]{:S(2)}, u32[]{:S(2)}) %collective-permute-start.17) | collective-permute-done | bytes 131104 | tf_op jit(solution)/shard_map/ppermute | solution.py:338
  72.7 2.9 %collective-permute-start.20 = (bf16[32,16,128]{2,1,0:T(8,128)(2,1)S(1)}, bf16[32,16,128]{2,1,0:T(8,128)(2,1)S(1)}, u32[]{:S(2)}, u32[]{:S(2)}) collective-permute-start(bf16[32,16,128]{2,1,0:T(8,128)(2,1)S(1)} %get-tuple-element.89.piece), channel_id=1, source_target_pairs={{0,6},{2,4},{4,2},{6,0},{8,14},{10,12},{12,10},{14,8},{1,7},{3,5},... | collective-permute-start | bytes 393224 | tf_op jit(solution)/shard_map/ppermute | solution.py:338
  77.1 2.9 %collective-permute-done.20.refs_2_ = bf16[32,16,128]{2,1,0:T(8,128)(2,1)S(1)} collective-permute-done((bf16[32,16,128]{2,1,0:T(8,128)(2,1)S(1)}, bf16[32,16,128]{2,1,0:T(8,128)(2,1)S(1)}, u32[]{:S(2)}, u32[]{:S(2)}) %collective-permute-start.20) | collective-permute-done | bytes 131104 | tf_op jit(solution)/shard_map/ppermute | solution.py:338
  80.0 1.3 collective-permute-done.19.refs_1_
  83.3 1.5 collective-permute-done.21.other
  84.8 1.6 forward_near_kernel.8
  86.5 3.3 %collective-permute-start.23 = (bf16[32,16,128]{2,1,0:T(8,128)(2,1)S(1)}, bf16[32,16,128]{2,1,0:T(8,128)(2,1)S(1)}, u32[]{:S(2)}, u32[]{:S(2)}) collective-permute-start(bf16[32,16,128]{2,1,0:T(8,128)(2,1)S(1)} %get-tuple-element.93), channel_id=1, source_target_pairs={{0,4},{2,6},{4,0},{6,2},{8,12},{10,14},{12,8},{14,10},{1,5},{3,7},... | collective-permute-start | bytes 393224 | tf_op jit(solution)/shard_map/ppermute | solution.py:338
  91.5 2.6 %collective-permute-done.23.refs_1_ = bf16[32,16,128]{2,1,0:T(8,128)(2,1)S(1)} collective-permute-done((bf16[32,16,128]{2,1,0:T(8,128)(2,1)S(1)}, bf16[32,16,128]{2,1,0:T(8,128)(2,1)S(1)}, u32[]{:S(2)}, u32[]{:S(2)}) %collective-permute-start.23) | collective-permute-done | bytes 131104 | tf_op jit(solution)/shard_map/ppermute | solution.py:338
  94.1 1.9 collective-permute-done.24.refs_2_
  96.1 3.3 %collective-permute-start.25 = (bf16[32,16,128]{2,1,0:T(8,128)(2,1)S(1)}, bf16[32,16,128]{2,1,0:T(8,128)(2,1)S(1)}, u32[]{:S(2)}, u32[]{:S(2)}) collective-permute-start(bf16[32,16,128]{2,1,0:T(8,128)(2,1)S(1)} %get-tuple-element.96), channel_id=1, source_target_pairs={{0,8},{2,10},{4,12},{6,14},{8,0},{10,2},{12,4},{14,6},{1,9},{3,11}... | collective-permute-start | bytes 393224 | tf_op jit(solution)/shard_map/ppermute | solution.py:338
  99.4 5.3 %collective-permute-done.25.far = bf16[32,16,128]{2,1,0:T(8,128)(2,1)S(1)} collective-permute-done((bf16[32,16,128]{2,1,0:T(8,128)(2,1)S(1)}, bf16[32,16,128]{2,1,0:T(8,128)(2,1)S(1)}, u32[]{:S(2)}, u32[]{:S(2)}) %collective-permute-start.25) | collective-permute-done | bytes 131104 | tf_op jit(solution)/shard_map/ppermute | solution.py:338
  104.8 2.5 %collective-permute-start.28 = (bf16[32,16,128]{2,1,0:T(8,128)(2,1)S(1)}, bf16[32,16,128]{2,1,0:T(8,128)(2,1)S(1)}, u32[]{:S(2)}, u32[]{:S(2)}) collective-permute-start(bf16[32,16,128]{2,1,0:T(8,128)(2,1)S(1)} %get-tuple-element.98.piece), channel_id=1, source_target_pairs={{0,6},{2,4},{4,2},{6,0},{8,14},{10,12},{12,10},{14,8},{1,7},{3,5},... | collective-permute-start | bytes 393224 | tf_op jit(solution)/shard_map/ppermute | solution.py:338
  109.1 2.9 %collective-permute-done.28.refs_2_ = bf16[32,16,128]{2,1,0:T(8,128)(2,1)S(1)} collective-permute-done((bf16[32,16,128]{2,1,0:T(8,128)(2,1)S(1)}, bf16[32,16,128]{2,1,0:T(8,128)(2,1)S(1)}, u32[]{:S(2)}, u32[]{:S(2)}) %collective-permute-start.28) | collective-permute-done | bytes 131104 | tf_op jit(solution)/shard_map/ppermute | solution.py:338
  115.3 1.5 collective-permute-done.29.other
  116.8 1.6 forward_near_kernel.9
  118.4 3.0 %collective-permute-start.31 = (bf16[32,16,128]{2,1,0:T(8,128)(2,1)S(1)}, bf16[32,16,128]{2,1,0:T(8,128)(2,1)S(1)}, u32[]{:S(2)}, u32[]{:S(2)}) collective-permute-start(bf16[32,16,128]{2,1,0:T(8,128)(2,1)S(1)} %get-tuple-element.102), channel_id=1, source_target_pairs={{0,4},{2,6},{4,0},{6,2},{8,12},{10,14},{12,8},{14,10},{1,5},{3,7},... | collective-permute-start | bytes 393224 | tf_op jit(solution)/shard_map/ppermute | solution.py:338
  123.4 2.4 %collective-permute-done.31.refs_1_ = bf16[32,16,128]{2,1,0:T(8,128)(2,1)S(1)} collective-permute-done((bf16[32,16,128]{2,1,0:T(8,128)(2,1)S(1)}, bf16[32,16,128]{2,1,0:T(8,128)(2,1)S(1)}, u32[]{:S(2)}, u32[]{:S(2)}) %collective-permute-start.31) | collective-permute-done | bytes 131104 | tf_op jit(solution)/shard_map/ppermute | solution.py:338
  125.8 1.9 collective-permute-done.32.refs_2_
  127.7 3.7 %collective-permute-start.33 = (bf16[32,16,128]{2,1,0:T(8,128)(2,1)S(1)}, bf16[32,16,128]{2,1,0:T(8,128)(2,1)S(1)}, u32[]{:S(2)}, u32[]{:S(2)}) collective-permute-start(bf16[32,16,128]{2,1,0:T(8,128)(2,1)S(1)} %get-tuple-element.105), channel_id=1, source_target_pairs={{0,8},{2,10},{4,12},{6,14},{8,0},{10,2},{12,4},{14,6},{1,9},{3,11}... | collective-permute-start | bytes 393224 | tf_op jit(solution)/shard_map/ppermute | solution.py:338
  131.5 5.3 %collective-permute-done.33.far = bf16[32,16,128]{2,1,0:T(8,128)(2,1)S(1)} collective-permute-done((bf16[32,16,128]{2,1,0:T(8,128)(2,1)S(1)}, bf16[32,16,128]{2,1,0:T(8,128)(2,1)S(1)}, u32[]{:S(2)}, u32[]{:S(2)}) %collective-permute-start.33) | collective-permute-done | bytes 131104 | tf_op jit(solution)/shard_map/ppermute | solution.py:338
  136.8 2.2 %collective-permute-start.36 = (bf16[32,16,128]{2,1,0:T(8,128)(2,1)S(1)}, bf16[32,16,128]{2,1,0:T(8,128)(2,1)S(1)}, u32[]{:S(2)}, u32[]{:S(2)}) collective-permute-start(bf16[32,16,128]{2,1,0:T(8,128)(2,1)S(1)} %get-tuple-element.107.piece), channel_id=1, source_target_pairs={{0,6},{2,4},{4,2},{6,0},{8,14},{10,12},{12,10},{14,8},{1,7},{3,5},... | collective-permute-start | bytes 393224 | tf_op jit(solution)/shard_map/ppermute | solution.py:338
  139.0 1.4 collective-permute-start.34
  141.2 2.9 %collective-permute-done.36.refs_2_ = bf16[32,16,128]{2,1,0:T(8,128)(2,1)S(1)} collective-permute-done((bf16[32,16,128]{2,1,0:T(8,128)(2,1)S(1)}, bf16[32,16,128]{2,1,0:T(8,128)(2,1)S(1)}, u32[]{:S(2)}, u32[]{:S(2)}) %collective-permute-start.36) | collective-permute-done | bytes 131104 | tf_op jit(solution)/shard_map/ppermute | solution.py:338
  144.7 1.4 collective-permute-done.34.refs_0_
  147.3 1.5 collective-permute-done.37.other
  148.9 1.6 forward_near_kernel.10
  150.5 2.6 %collective-permute-start.39 = (bf16[32,16,128]{2,1,0:T(8,128)(2,1)S(1)}, bf16[32,16,128]{2,1,0:T(8,128)(2,1)S(1)}, u32[]{:S(2)}, u32[]{:S(2)}) collective-permute-start(bf16[32,16,128]{2,1,0:T(8,128)(2,1)S(1)} %get-tuple-element.111), channel_id=1, source_target_pairs={{0,4},{2,6},{4,0},{6,2},{8,12},{10,14},{12,8},{14,10},{1,5},{3,7},... | collective-permute-start | bytes 393224 | tf_op jit(solution)/shard_map/ppermute | solution.py:338
  155.5 2.0 collective-permute-done.39.refs_1_
  157.5 2.3 %collective-permute-done.40.refs_2_ = bf16[32,16,128]{2,1,0:T(8,128)(2,1)S(1)} collective-permute-done((bf16[32,16,128]{2,1,0:T(8,128)(2,1)S(1)}, bf16[32,16,128]{2,1,0:T(8,128)(2,1)S(1)}, u32[]{:S(2)}, u32[]{:S(2)}) %collective-permute-start.40) | collective-permute-done | bytes 131104 | tf_op jit(solution)/shard_map/ppermute | solution.py:338
  159.8 3.7 %collective-permute-start.41 = (bf16[32,16,128]{2,1,0:T(8,128)(2,1)S(1)}, bf16[32,16,128]{2,1,0:T(8,128)(2,1)S(1)}, u32[]{:S(2)}, u32[]{:S(2)}) collective-permute-start(bf16[32,16,128]{2,1,0:T(8,128)(2,1)S(1)} %get-tuple-element.114), channel_id=1, source_target_pairs={{0,8},{2,10},{4,12},{6,14},{8,0},{10,2},{12,4},{14,6},{1,9},{3,11}... | collective-permute-start | bytes 393224 | tf_op jit(solution)/shard_map/ppermute | solution.py:338
  163.5 5.3 %collective-permute-done.41.far = bf16[32,16,128]{2,1,0:T(8,128)(2,1)S(1)} collective-permute-done((bf16[32,16,128]{2,1,0:T(8,128)(2,1)S(1)}, bf16[32,16,128]{2,1,0:T(8,128)(2,1)S(1)}, u32[]{:S(2)}, u32[]{:S(2)}) %collective-permute-start.41) | collective-permute-done | bytes 131104 | tf_op jit(solution)/shard_map/ppermute | solution.py:338
  168.9 1.8 collective-permute-start.44
  170.7 1.8 collective-permute-start.42
  173.3 2.9 %collective-permute-done.44.refs_2_ = bf16[32,16,128]{2,1,0:T(8,128)(2,1)S(1)} collective-permute-done((bf16[32,16,128]{2,1,0:T(8,128)(2,1)S(1)}, bf16[32,16,128]{2,1,0:T(8,128)(2,1)S(1)}, u32[]{:S(2)}, u32[]{:S(2)}) %collective-permute-start.44) | collective-permute-done | bytes 131104 | tf_op jit(solution)/shard_map/ppermute | solution.py:338
  176.3 1.7 collective-permute-done.42.refs_0_
  179.4 1.5 collective-permute-done.45.other
  180.9 2.2 %forward_near_kernel.11 = (f32[16,16,128]{2,1,0:T(8,128)}, bf16[32,16,128]{2,1,0:T(8,128)(2,1)S(1)}, bf16[32,16,128]{2,1,0:T(8,128)(2,1)S(1)}, bf16[32,16,128]{2,1,0:T(8,128)(2,1)S(1)}, bf16[32,16,128]{2,1,0:T(8,128)(2,1)S(1)}) custom-call(s32[2248]{0:T(1024)S(4)} %get-tuple-element.67.plan_ref, bf16[256,128,128]{2,1,0:T(8,128)(2,1)S(1)} %get-tuple-element.77.tile, ...), custom_call_target="tpu_custom_call" | custom-call | flops 134217728 | tf_op jit(solution)/shard_map/forward_near_kernel/pallas_call | solution.py:410
  183.2 2.3 %collective-permute-start.47 = (bf16[32,16,128]{2,1,0:T(8,128)(2,1)S(1)}, bf16[32,16,128]{2,1,0:T(8,128)(2,1)S(1)}, u32[]{:S(2)}, u32[]{:S(2)}) collective-permute-start(bf16[32,16,128]{2,1,0:T(8,128)(2,1)S(1)} %get-tuple-element.121), channel_id=1, source_target_pairs={{0,4},{2,6},{4,0},{6,2},{8,12},{10,14},{12,8},{14,10},{1,5},{3,7},... | collective-permute-start | bytes 393224 | tf_op jit(solution)/shard_map/ppermute | solution.py:338
  188.1 1.6 collective-permute-done.47.refs_1_
  189.8 2.7 %collective-permute-done.48.refs_2_ = bf16[32,16,128]{2,1,0:T(8,128)(2,1)S(1)} collective-permute-done((bf16[32,16,128]{2,1,0:T(8,128)(2,1)S(1)}, bf16[32,16,128]{2,1,0:T(8,128)(2,1)S(1)}, u32[]{:S(2)}, u32[]{:S(2)}) %collective-permute-start.48) | collective-permute-done | bytes 131104 | tf_op jit(solution)/shard_map/ppermute | solution.py:338
  192.5 3.7 %collective-permute-start.49 = (bf16[16,16,128]{2,1,0:T(8,128)(2,1)S(1)}, bf16[16,16,128]{2,1,0:T(8,128)(2,1)S(1)}, u32[]{:S(2)}, u32[]{:S(2)}) collective-permute-start(bf16[16,16,128]{2,1,0:T(8,128)(2,1)S(1)} %get-tuple-element.124), channel_id=1, source_target_pairs={{0,8},{2,10},{4,12},{6,14},{8,0},{10,2},{12,4},{14,6},{1,9},{3,11}... | collective-permute-start | bytes 196616 | tf_op jit(solution)/shard_map/ppermute | solution.py:338
  196.2 2.5 %collective-permute-done.49.far = bf16[16,16,128]{2,1,0:T(8,128)(2,1)S(1)} collective-permute-done((bf16[16,16,128]{2,1,0:T(8,128)(2,1)S(1)}, bf16[16,16,128]{2,1,0:T(8,128)(2,1)S(1)}, u32[]{:S(2)}, u32[]{:S(2)}) %collective-permute-start.49) | collective-permute-done | bytes 65568 | tf_op jit(solution)/shard_map/ppermute | solution.py:338
  (76 shorter events, 33.6 us)
Async XLA Ops:
  2.9 5.3 %collective-permute-start = (bf16[16,16,128]{2,1,0:T(8,128)(2,1)S(1)}, bf16[16,16,128]{2,1,0:T(8,128)(2,1)S(1)}, u32[]{:S(2)}, u32[]{:S(2)}) collective-permute-start(bf16[16,16,128]{2,1,0:T(8,128)(2,1)S(1)} %get-tuple-element.64), channel_id=1, source_target_pairs={{0,8},{2,10},{4,12},{6,14},{8,0},{10,2},{12,4},{14,6},{1,9},{3,11}... | collective-permute-start | bytes 196616 | tf_op jit(solution)/shard_map/ppermute | solution.py:338
  8.2 9.2 %collective-permute-start.3 = (bf16[32,16,128]{2,1,0:T(8,128)(2,1)S(1)}, bf16[32,16,128]{2,1,0:T(8,128)(2,1)S(1)}, u32[]{:S(2)}, u32[]{:S(2)}) collective-permute-start(bf16[32,16,128]{2,1,0:T(8,128)(2,1)S(1)} %pad_maximum_fusion.piece.y_far), channel_id=1, source_target_pairs={{0,6},{2,4},{4,2},{6,0},{8,14},{10,12},{12,10},{14,8},{1,7},{3,5},... | collective-permute-start | bytes 393224 | tf_op jit(solution)/shard_map/ppermute | solution.py:338
  10.9 6.5 %collective-permute-start.2 = (bf16[32,16,128]{2,1,0:T(8,128)(2,1)S(1)}, bf16[32,16,128]{2,1,0:T(8,128)(2,1)S(1)}, u32[]{:S(2)}, u32[]{:S(2)}) collective-permute-start(bf16[32,16,128]{2,1,0:T(8,128)(2,1)S(1)} %pad_maximum_fusion.piece.y_far), channel_id=1, source_target_pairs={{0,4},{2,6},{4,0},{6,2},{8,12},{10,14},{12,8},{14,10},{1,5},{3,7},... | collective-permute-start | bytes 393224 | tf_op jit(solution)/shard_map/ppermute | solution.py:338
  11.3 6.1 %collective-permute-start.1 = (bf16[32,16,128]{2,1,0:T(8,128)(2,1)S(1)}, bf16[32,16,128]{2,1,0:T(8,128)(2,1)S(1)}, u32[]{:S(2)}, u32[]{:S(2)}) collective-permute-start(bf16[32,16,128]{2,1,0:T(8,128)(2,1)S(1)} %pad_maximum_fusion.piece.y_far), channel_id=1, source_target_pairs={{0,2},{2,0},{4,6},{6,4},{8,10},{10,8},{12,14},{14,12},{1,3},{3,1},... | collective-permute-start | bytes 393224 | tf_op jit(solution)/shard_map/ppermute | solution.py:338
  11.8 7.0 %collective-permute-start.5 = (f32[16,34,128]{2,1,0:T(8,128)S(1)}, f32[16,34,128]{2,1,0:T(8,128)S(1)}, u32[]{:S(2)}, u32[]{:S(2)}) collective-permute-start(f32[16,34,128]{2,1,0:T(8,128)S(1)} %get-tuple-element.71.here_state), channel_id=1, source_target_pairs={{0,1},{1,0},{2,3},{3,2},{4,5},{5,4},{6,7},{7,6},{8,9},{9,8},{10,11... | collective-permute-start | bytes 835592 | tf_op jit(solution)/shard_map/ppermute | solution.py:335
  18.6 1.6 collective-permute-start.4
  22.5 5.0 %collective-permute-start.6 = (bf16[32,16,128]{2,1,0:T(8,128)(2,1)S(1)}, bf16[32,16,128]{2,1,0:T(8,128)(2,1)S(1)}, u32[]{:S(2)}, u32[]{:S(2)}) collective-permute-start(bf16[32,16,128]{2,1,0:T(8,128)(2,1)S(1)} %get-tuple-element.73), channel_id=1, source_target_pairs={{0,2},{2,0},{4,6},{6,4},{8,10},{10,8},{12,14},{14,12},{1,3},{3,1},... | collective-permute-start | bytes 393224 | tf_op jit(solution)/shard_map/ppermute | solution.py:338
  22.8 7.2 %collective-permute-start.7 = (bf16[32,16,128]{2,1,0:T(8,128)(2,1)S(1)}, bf16[32,16,128]{2,1,0:T(8,128)(2,1)S(1)}, u32[]{:S(2)}, u32[]{:S(2)}) collective-permute-start(bf16[32,16,128]{2,1,0:T(8,128)(2,1)S(1)} %get-tuple-element.74), channel_id=1, source_target_pairs={{0,4},{2,6},{4,0},{6,2},{8,12},{10,14},{12,8},{14,10},{1,5},{3,7},... | collective-permute-start | bytes 393224 | tf_op jit(solution)/shard_map/ppermute | solution.py:338
  25.7 6.4 %collective-permute-start.8 = (bf16[32,16,128]{2,1,0:T(8,128)(2,1)S(1)}, bf16[32,16,128]{2,1,0:T(8,128)(2,1)S(1)}, u32[]{:S(2)}, u32[]{:S(2)}) collective-permute-start(bf16[32,16,128]{2,1,0:T(8,128)(2,1)S(1)} %get-tuple-element.75), channel_id=1, source_target_pairs={{0,6},{2,4},{4,2},{6,0},{8,14},{10,12},{12,10},{14,8},{1,7},{3,5},... | collective-permute-start | bytes 393224 | tf_op jit(solution)/shard_map/ppermute | solution.py:338
  32.2 8.4 %collective-permute-start.9 = (bf16[32,16,128]{2,1,0:T(8,128)(2,1)S(1)}, bf16[32,16,128]{2,1,0:T(8,128)(2,1)S(1)}, u32[]{:S(2)}, u32[]{:S(2)}) collective-permute-start(bf16[32,16,128]{2,1,0:T(8,128)(2,1)S(1)} %get-tuple-element.78), channel_id=1, source_target_pairs={{0,8},{2,10},{4,12},{6,14},{8,0},{10,2},{12,4},{14,6},{1,9},{3,11}... | collective-permute-start | bytes 393224 | tf_op jit(solution)/shard_map/ppermute | solution.py:338
  40.7 7.4 %collective-permute-start.12 = (bf16[32,16,128]{2,1,0:T(8,128)(2,1)S(1)}, bf16[32,16,128]{2,1,0:T(8,128)(2,1)S(1)}, u32[]{:S(2)}, u32[]{:S(2)}) collective-permute-start(bf16[32,16,128]{2,1,0:T(8,128)(2,1)S(1)} %get-tuple-element.80.piece), channel_id=1, source_target_pairs={{0,6},{2,4},{4,2},{6,0},{8,14},{10,12},{12,10},{14,8},{1,7},{3,5},... | collective-permute-start | bytes 393224 | tf_op jit(solution)/shard_map/ppermute | solution.py:338
  43.7 5.7 %collective-permute-start.11 = (bf16[32,16,128]{2,1,0:T(8,128)(2,1)S(1)}, bf16[32,16,128]{2,1,0:T(8,128)(2,1)S(1)}, u32[]{:S(2)}, u32[]{:S(2)}) collective-permute-start(bf16[32,16,128]{2,1,0:T(8,128)(2,1)S(1)} %get-tuple-element.80.piece), channel_id=1, source_target_pairs={{0,4},{2,6},{4,0},{6,2},{8,12},{10,14},{12,8},{14,10},{1,5},{3,7},... | collective-permute-start | bytes 393224 | tf_op jit(solution)/shard_map/ppermute | solution.py:338
  43.7 6.4 %collective-permute-start.10 = (bf16[32,16,128]{2,1,0:T(8,128)(2,1)S(1)}, bf16[32,16,128]{2,1,0:T(8,128)(2,1)S(1)}, u32[]{:S(2)}, u32[]{:S(2)}) collective-permute-start(bf16[32,16,128]{2,1,0:T(8,128)(2,1)S(1)} %get-tuple-element.80.piece), channel_id=1, source_target_pairs={{0,2},{2,0},{4,6},{6,4},{8,10},{10,8},{12,14},{14,12},{1,3},{3,1},... | collective-permute-start | bytes 393224 | tf_op jit(solution)/shard_map/ppermute | solution.py:338
  51.4 1.6 collective-permute-start.13
  54.7 5.0 %collective-permute-start.14 = (bf16[32,16,128]{2,1,0:T(8,128)(2,1)S(1)}, bf16[32,16,128]{2,1,0:T(8,128)(2,1)S(1)}, u32[]{:S(2)}, u32[]{:S(2)}) collective-permute-start(bf16[32,16,128]{2,1,0:T(8,128)(2,1)S(1)} %get-tuple-element.83), channel_id=1, source_target_pairs={{0,2},{2,0},{4,6},{6,4},{8,10},{10,8},{12,14},{14,12},{1,3},{3,1},... | collective-permute-start | bytes 393224 | tf_op jit(solution)/shard_map/ppermute | solution.py:338
  54.8 7.6 %collective-permute-start.15 = (bf16[32,16,128]{2,1,0:T(8,128)(2,1)S(1)}, bf16[32,16,128]{2,1,0:T(8,128)(2,1)S(1)}, u32[]{:S(2)}, u32[]{:S(2)}) collective-permute-start(bf16[32,16,128]{2,1,0:T(8,128)(2,1)S(1)} %get-tuple-element.84), channel_id=1, source_target_pairs={{0,4},{2,6},{4,0},{6,2},{8,12},{10,14},{12,8},{14,10},{1,5},{3,7},... | collective-permute-start | bytes 393224 | tf_op jit(solution)/shard_map/ppermute | solution.py:338
  58.1 6.2 %collective-permute-start.16 = (bf16[32,16,128]{2,1,0:T(8,128)(2,1)S(1)}, bf16[32,16,128]{2,1,0:T(8,128)(2,1)S(1)}, u32[]{:S(2)}, u32[]{:S(2)}) collective-permute-start(bf16[32,16,128]{2,1,0:T(8,128)(2,1)S(1)} %get-tuple-element.85), channel_id=1, source_target_pairs={{0,6},{2,4},{4,2},{6,0},{8,14},{10,12},{12,10},{14,8},{1,7},{3,5},... | collective-permute-start | bytes 393224 | tf_op jit(solution)/shard_map/ppermute | solution.py:338
  64.4 8.3 %collective-permute-start.17 = (bf16[32,16,128]{2,1,0:T(8,128)(2,1)S(1)}, bf16[32,16,128]{2,1,0:T(8,128)(2,1)S(1)}, u32[]{:S(2)}, u32[]{:S(2)}) collective-permute-start(bf16[32,16,128]{2,1,0:T(8,128)(2,1)S(1)} %get-tuple-element.87), channel_id=1, source_target_pairs={{0,8},{2,10},{4,12},{6,14},{8,0},{10,2},{12,4},{14,6},{1,9},{3,11}... | collective-permute-start | bytes 393224 | tf_op jit(solution)/shard_map/ppermute | solution.py:338
  72.7 7.3 %collective-permute-start.20 = (bf16[32,16,128]{2,1,0:T(8,128)(2,1)S(1)}, bf16[32,16,128]{2,1,0:T(8,128)(2,1)S(1)}, u32[]{:S(2)}, u32[]{:S(2)}) collective-permute-start(bf16[32,16,128]{2,1,0:T(8,128)(2,1)S(1)} %get-tuple-element.89.piece), channel_id=1, source_target_pairs={{0,6},{2,4},{4,2},{6,0},{8,14},{10,12},{12,10},{14,8},{1,7},{3,5},... | collective-permute-start | bytes 393224 | tf_op jit(solution)/shard_map/ppermute | solution.py:338
  75.6 5.7 %collective-permute-start.19 = (bf16[32,16,128]{2,1,0:T(8,128)(2,1)S(1)}, bf16[32,16,128]{2,1,0:T(8,128)(2,1)S(1)}, u32[]{:S(2)}, u32[]{:S(2)}) collective-permute-start(bf16[32,16,128]{2,1,0:T(8,128)(2,1)S(1)} %get-tuple-element.89.piece), channel_id=1, source_target_pairs={{0,4},{2,6},{4,0},{6,2},{8,12},{10,14},{12,8},{14,10},{1,5},{3,7},... | collective-permute-start | bytes 393224 | tf_op jit(solution)/shard_map/ppermute | solution.py:338
  75.6 6.4 %collective-permute-start.18 = (bf16[32,16,128]{2,1,0:T(8,128)(2,1)S(1)}, bf16[32,16,128]{2,1,0:T(8,128)(2,1)S(1)}, u32[]{:S(2)}, u32[]{:S(2)}) collective-permute-start(bf16[32,16,128]{2,1,0:T(8,128)(2,1)S(1)} %get-tuple-element.89.piece), channel_id=1, source_target_pairs={{0,2},{2,0},{4,6},{6,4},{8,10},{10,8},{12,14},{14,12},{1,3},{3,1},... | collective-permute-start | bytes 393224 | tf_op jit(solution)/shard_map/ppermute | solution.py:338
  83.2 1.6 collective-permute-start.21
  86.4 5.0 %collective-permute-start.22 = (bf16[32,16,128]{2,1,0:T(8,128)(2,1)S(1)}, bf16[32,16,128]{2,1,0:T(8,128)(2,1)S(1)}, u32[]{:S(2)}, u32[]{:S(2)}) collective-permute-start(bf16[32,16,128]{2,1,0:T(8,128)(2,1)S(1)} %get-tuple-element.92), channel_id=1, source_target_pairs={{0,2},{2,0},{4,6},{6,4},{8,10},{10,8},{12,14},{14,12},{1,3},{3,1},... | collective-permute-start | bytes 393224 | tf_op jit(solution)/shard_map/ppermute | solution.py:338
  86.5 7.6 %collective-permute-start.23 = (bf16[32,16,128]{2,1,0:T(8,128)(2,1)S(1)}, bf16[32,16,128]{2,1,0:T(8,128)(2,1)S(1)}, u32[]{:S(2)}, u32[]{:S(2)}) collective-permute-start(bf16[32,16,128]{2,1,0:T(8,128)(2,1)S(1)} %get-tuple-element.93), channel_id=1, source_target_pairs={{0,4},{2,6},{4,0},{6,2},{8,12},{10,14},{12,8},{14,10},{1,5},{3,7},... | collective-permute-start | bytes 393224 | tf_op jit(solution)/shard_map/ppermute | solution.py:338
  89.8 6.2 %collective-permute-start.24 = (bf16[32,16,128]{2,1,0:T(8,128)(2,1)S(1)}, bf16[32,16,128]{2,1,0:T(8,128)(2,1)S(1)}, u32[]{:S(2)}, u32[]{:S(2)}) collective-permute-start(bf16[32,16,128]{2,1,0:T(8,128)(2,1)S(1)} %get-tuple-element.94), channel_id=1, source_target_pairs={{0,6},{2,4},{4,2},{6,0},{8,14},{10,12},{12,10},{14,8},{1,7},{3,5},... | collective-permute-start | bytes 393224 | tf_op jit(solution)/shard_map/ppermute | solution.py:338
  96.1 8.6 %collective-permute-start.25 = (bf16[32,16,128]{2,1,0:T(8,128)(2,1)S(1)}, bf16[32,16,128]{2,1,0:T(8,128)(2,1)S(1)}, u32[]{:S(2)}, u32[]{:S(2)}) collective-permute-start(bf16[32,16,128]{2,1,0:T(8,128)(2,1)S(1)} %get-tuple-element.96), channel_id=1, source_target_pairs={{0,8},{2,10},{4,12},{6,14},{8,0},{10,2},{12,4},{14,6},{1,9},{3,11}... | collective-permute-start | bytes 393224 | tf_op jit(solution)/shard_map/ppermute | solution.py:338
  104.8 7.3 %collective-permute-start.28 = (bf16[32,16,128]{2,1,0:T(8,128)(2,1)S(1)}, bf16[32,16,128]{2,1,0:T(8,128)(2,1)S(1)}, u32[]{:S(2)}, u32[]{:S(2)}) collective-permute-start(bf16[32,16,128]{2,1,0:T(8,128)(2,1)S(1)} %get-tuple-element.98.piece), channel_id=1, source_target_pairs={{0,6},{2,4},{4,2},{6,0},{8,14},{10,12},{12,10},{14,8},{1,7},{3,5},... | collective-permute-start | bytes 393224 | tf_op jit(solution)/shard_map/ppermute | solution.py:338
  107.3 5.7 %collective-permute-start.27 = (bf16[32,16,128]{2,1,0:T(8,128)(2,1)S(1)}, bf16[32,16,128]{2,1,0:T(8,128)(2,1)S(1)}, u32[]{:S(2)}, u32[]{:S(2)}) collective-permute-start(bf16[32,16,128]{2,1,0:T(8,128)(2,1)S(1)} %get-tuple-element.98.piece), channel_id=1, source_target_pairs={{0,4},{2,6},{4,0},{6,2},{8,12},{10,14},{12,8},{14,10},{1,5},{3,7},... | collective-permute-start | bytes 393224 | tf_op jit(solution)/shard_map/ppermute | solution.py:338
  107.3 6.7 %collective-permute-start.26 = (bf16[32,16,128]{2,1,0:T(8,128)(2,1)S(1)}, bf16[32,16,128]{2,1,0:T(8,128)(2,1)S(1)}, u32[]{:S(2)}, u32[]{:S(2)}) collective-permute-start(bf16[32,16,128]{2,1,0:T(8,128)(2,1)S(1)} %get-tuple-element.98.piece), channel_id=1, source_target_pairs={{0,2},{2,0},{4,6},{6,4},{8,10},{10,8},{12,14},{14,12},{1,3},{3,1},... | collective-permute-start | bytes 393224 | tf_op jit(solution)/shard_map/ppermute | solution.py:338
  115.2 1.6 collective-permute-start.29
  118.4 5.0 %collective-permute-start.30 = (bf16[32,16,128]{2,1,0:T(8,128)(2,1)S(1)}, bf16[32,16,128]{2,1,0:T(8,128)(2,1)S(1)}, u32[]{:S(2)}, u32[]{:S(2)}) collective-permute-start(bf16[32,16,128]{2,1,0:T(8,128)(2,1)S(1)} %get-tuple-element.101), channel_id=1, source_target_pairs={{0,2},{2,0},{4,6},{6,4},{8,10},{10,8},{12,14},{14,12},{1,3},{3,1},... | collective-permute-start | bytes 393224 | tf_op jit(solution)/shard_map/ppermute | solution.py:338
  118.4 7.3 %collective-permute-start.31 = (bf16[32,16,128]{2,1,0:T(8,128)(2,1)S(1)}, bf16[32,16,128]{2,1,0:T(8,128)(2,1)S(1)}, u32[]{:S(2)}, u32[]{:S(2)}) collective-permute-start(bf16[32,16,128]{2,1,0:T(8,128)(2,1)S(1)} %get-tuple-element.102), channel_id=1, source_target_pairs={{0,4},{2,6},{4,0},{6,2},{8,12},{10,14},{12,8},{14,10},{1,5},{3,7},... | collective-permute-start | bytes 393224 | tf_op jit(solution)/shard_map/ppermute | solution.py:338
  121.5 6.2 %collective-permute-start.32 = (bf16[32,16,128]{2,1,0:T(8,128)(2,1)S(1)}, bf16[32,16,128]{2,1,0:T(8,128)(2,1)S(1)}, u32[]{:S(2)}, u32[]{:S(2)}) collective-permute-start(bf16[32,16,128]{2,1,0:T(8,128)(2,1)S(1)} %get-tuple-element.103), channel_id=1, source_target_pairs={{0,6},{2,4},{4,2},{6,0},{8,14},{10,12},{12,10},{14,8},{1,7},{3,5},... | collective-permute-start | bytes 393224 | tf_op jit(solution)/shard_map/ppermute | solution.py:338
  127.7 9.0 %collective-permute-start.33 = (bf16[32,16,128]{2,1,0:T(8,128)(2,1)S(1)}, bf16[32,16,128]{2,1,0:T(8,128)(2,1)S(1)}, u32[]{:S(2)}, u32[]{:S(2)}) collective-permute-start(bf16[32,16,128]{2,1,0:T(8,128)(2,1)S(1)} %get-tuple-element.105), channel_id=1, source_target_pairs={{0,8},{2,10},{4,12},{6,14},{8,0},{10,2},{12,4},{14,6},{1,9},{3,11}... | collective-permute-start | bytes 393224 | tf_op jit(solution)/shard_map/ppermute | solution.py:338
  136.8 7.3 %collective-permute-start.36 = (bf16[32,16,128]{2,1,0:T(8,128)(2,1)S(1)}, bf16[32,16,128]{2,1,0:T(8,128)(2,1)S(1)}, u32[]{:S(2)}, u32[]{:S(2)}) collective-permute-start(bf16[32,16,128]{2,1,0:T(8,128)(2,1)S(1)} %get-tuple-element.107.piece), channel_id=1, source_target_pairs={{0,6},{2,4},{4,2},{6,0},{8,14},{10,12},{12,10},{14,8},{1,7},{3,5},... | collective-permute-start | bytes 393224 | tf_op jit(solution)/shard_map/ppermute | solution.py:338
  139.0 5.7 %collective-permute-start.35 = (bf16[32,16,128]{2,1,0:T(8,128)(2,1)S(1)}, bf16[32,16,128]{2,1,0:T(8,128)(2,1)S(1)}, u32[]{:S(2)}, u32[]{:S(2)}) collective-permute-start(bf16[32,16,128]{2,1,0:T(8,128)(2,1)S(1)} %get-tuple-element.107.piece), channel_id=1, source_target_pairs={{0,4},{2,6},{4,0},{6,2},{8,12},{10,14},{12,8},{14,10},{1,5},{3,7},... | collective-permute-start | bytes 393224 | tf_op jit(solution)/shard_map/ppermute | solution.py:338
  139.0 7.0 %collective-permute-start.34 = (bf16[32,16,128]{2,1,0:T(8,128)(2,1)S(1)}, bf16[32,16,128]{2,1,0:T(8,128)(2,1)S(1)}, u32[]{:S(2)}, u32[]{:S(2)}) collective-permute-start(bf16[32,16,128]{2,1,0:T(8,128)(2,1)S(1)} %get-tuple-element.107.piece), channel_id=1, source_target_pairs={{0,2},{2,0},{4,6},{6,4},{8,10},{10,8},{12,14},{14,12},{1,3},{3,1},... | collective-permute-start | bytes 393224 | tf_op jit(solution)/shard_map/ppermute | solution.py:338
  147.3 1.6 collective-permute-start.37
  150.4 5.0 %collective-permute-start.38 = (bf16[32,16,128]{2,1,0:T(8,128)(2,1)S(1)}, bf16[32,16,128]{2,1,0:T(8,128)(2,1)S(1)}, u32[]{:S(2)}, u32[]{:S(2)}) collective-permute-start(bf16[32,16,128]{2,1,0:T(8,128)(2,1)S(1)} %get-tuple-element.110), channel_id=1, source_target_pairs={{0,2},{2,0},{4,6},{6,4},{8,10},{10,8},{12,14},{14,12},{1,3},{3,1},... | collective-permute-start | bytes 393224 | tf_op jit(solution)/shard_map/ppermute | solution.py:338
  150.5 6.9 %collective-permute-start.39 = (bf16[32,16,128]{2,1,0:T(8,128)(2,1)S(1)}, bf16[32,16,128]{2,1,0:T(8,128)(2,1)S(1)}, u32[]{:S(2)}, u32[]{:S(2)}) collective-permute-start(bf16[32,16,128]{2,1,0:T(8,128)(2,1)S(1)} %get-tuple-element.111), channel_id=1, source_target_pairs={{0,4},{2,6},{4,0},{6,2},{8,12},{10,14},{12,8},{14,10},{1,5},{3,7},... | collective-permute-start | bytes 393224 | tf_op jit(solution)/shard_map/ppermute | solution.py:338
  153.1 6.6 %collective-permute-start.40 = (bf16[32,16,128]{2,1,0:T(8,128)(2,1)S(1)}, bf16[32,16,128]{2,1,0:T(8,128)(2,1)S(1)}, u32[]{:S(2)}, u32[]{:S(2)}) collective-permute-start(bf16[32,16,128]{2,1,0:T(8,128)(2,1)S(1)} %get-tuple-element.112), channel_id=1, source_target_pairs={{0,6},{2,4},{4,2},{6,0},{8,14},{10,12},{12,10},{14,8},{1,7},{3,5},... | collective-permute-start | bytes 393224 | tf_op jit(solution)/shard_map/ppermute | solution.py:338
  159.8 9.0 %collective-permute-start.41 = (bf16[32,16,128]{2,1,0:T(8,128)(2,1)S(1)}, bf16[32,16,128]{2,1,0:T(8,128)(2,1)S(1)}, u32[]{:S(2)}, u32[]{:S(2)}) collective-permute-start(bf16[32,16,128]{2,1,0:T(8,128)(2,1)S(1)} %get-tuple-element.114), channel_id=1, source_target_pairs={{0,8},{2,10},{4,12},{6,14},{8,0},{10,2},{12,4},{14,6},{1,9},{3,11}... | collective-permute-start | bytes 393224 | tf_op jit(solution)/shard_map/ppermute | solution.py:338
  168.9 7.3 %collective-permute-start.44 = (bf16[32,16,128]{2,1,0:T(8,128)(2,1)S(1)}, bf16[32,16,128]{2,1,0:T(8,128)(2,1)S(1)}, u32[]{:S(2)}, u32[]{:S(2)}) collective-permute-start(bf16[32,16,128]{2,1,0:T(8,128)(2,1)S(1)} %get-tuple-element.116.piece), channel_id=1, source_target_pairs={{0,6},{2,4},{4,2},{6,0},{8,14},{10,12},{12,10},{14,8},{1,7},{3,5},... | collective-permute-start | bytes 393224 | tf_op jit(solution)/shard_map/ppermute | solution.py:338
  170.7 5.7 %collective-permute-start.43 = (bf16[32,16,128]{2,1,0:T(8,128)(2,1)S(1)}, bf16[32,16,128]{2,1,0:T(8,128)(2,1)S(1)}, u32[]{:S(2)}, u32[]{:S(2)}) collective-permute-start(bf16[32,16,128]{2,1,0:T(8,128)(2,1)S(1)} %get-tuple-element.116.piece), channel_id=1, source_target_pairs={{0,4},{2,6},{4,0},{6,2},{8,12},{10,14},{12,8},{14,10},{1,5},{3,7},... | collective-permute-start | bytes 393224 | tf_op jit(solution)/shard_map/ppermute | solution.py:338
  170.7 7.4 %collective-permute-start.42 = (bf16[32,16,128]{2,1,0:T(8,128)(2,1)S(1)}, bf16[32,16,128]{2,1,0:T(8,128)(2,1)S(1)}, u32[]{:S(2)}, u32[]{:S(2)}) collective-permute-start(bf16[32,16,128]{2,1,0:T(8,128)(2,1)S(1)} %get-tuple-element.116.piece), channel_id=1, source_target_pairs={{0,2},{2,0},{4,6},{6,4},{8,10},{10,8},{12,14},{14,12},{1,3},{3,1},... | collective-permute-start | bytes 393224 | tf_op jit(solution)/shard_map/ppermute | solution.py:338
  179.3 1.6 collective-permute-start.45
  183.2 5.0 %collective-permute-start.46 = (bf16[32,16,128]{2,1,0:T(8,128)(2,1)S(1)}, bf16[32,16,128]{2,1,0:T(8,128)(2,1)S(1)}, u32[]{:S(2)}, u32[]{:S(2)}) collective-permute-start(bf16[32,16,128]{2,1,0:T(8,128)(2,1)S(1)} %get-tuple-element.120), channel_id=1, source_target_pairs={{0,2},{2,0},{4,6},{6,4},{8,10},{10,8},{12,14},{14,12},{1,3},{3,1},... | collective-permute-start | bytes 393224 | tf_op jit(solution)/shard_map/ppermute | solution.py:338
  183.2 6.6 %collective-permute-start.47 = (bf16[32,16,128]{2,1,0:T(8,128)(2,1)S(1)}, bf16[32,16,128]{2,1,0:T(8,128)(2,1)S(1)}, u32[]{:S(2)}, u32[]{:S(2)}) collective-permute-start(bf16[32,16,128]{2,1,0:T(8,128)(2,1)S(1)} %get-tuple-element.121), channel_id=1, source_target_pairs={{0,4},{2,6},{4,0},{6,2},{8,12},{10,14},{12,8},{14,10},{1,5},{3,7},... | collective-permute-start | bytes 393224 | tf_op jit(solution)/shard_map/ppermute | solution.py:338
  185.4 7.0 %collective-permute-start.48 = (bf16[32,16,128]{2,1,0:T(8,128)(2,1)S(1)}, bf16[32,16,128]{2,1,0:T(8,128)(2,1)S(1)}, u32[]{:S(2)}, u32[]{:S(2)}) collective-permute-start(bf16[32,16,128]{2,1,0:T(8,128)(2,1)S(1)} %get-tuple-element.122), channel_id=1, source_target_pairs={{0,6},{2,4},{4,2},{6,0},{8,14},{10,12},{12,10},{14,8},{1,7},{3,5},... | collective-permute-start | bytes 393224 | tf_op jit(solution)/shard_map/ppermute | solution.py:338
  192.5 6.2 %collective-permute-start.49 = (bf16[16,16,128]{2,1,0:T(8,128)(2,1)S(1)}, bf16[16,16,128]{2,1,0:T(8,128)(2,1)S(1)}, u32[]{:S(2)}, u32[]{:S(2)}) collective-permute-start(bf16[16,16,128]{2,1,0:T(8,128)(2,1)S(1)} %get-tuple-element.124), channel_id=1, source_target_pairs={{0,8},{2,10},{4,12},{6,14},{8,0},{10,2},{12,4},{14,6},{1,9},{3,11}... | collective-permute-start | bytes 196616 | tf_op jit(solution)/shard_map/ppermute | solution.py:338
